TPU v7x, 32 devices: a whole 2x2x4 slice. The times are simulated.
32 devices in a mesh: item: 4 (over y, x), seq: 8 (over z, core).
Axes of the slice: x: 2, y: 2, z: 4, core: 2. Of those that a mesh axis runs over, the one named last changes fastest.
Arguments:
- inputs: float32 [4, 2048, 768], P('item', 'seq'), may hold values from -6 to 6
- lengths: int32 [4], P('item'), may hold values from 512 to 2048, as said below
- pad_mask: int32 [4, 2048], P('item', 'seq'), may hold values 0 or 1
- hash_proj: float32 [64, 256], replicated, may hold values from -6 to 6
- w_query: bfloat16 [768, 768], replicated, may hold values from -0.21875 to 0.21875
- b_query: float32 [768], replicated, may hold values from -1.75 to 1.75
- w_key: bfloat16 [768, 768], replicated, may hold values from -0.21875 to 0.21875
- b_key: float32 [768], replicated, may hold values from -1.75 to 1.75
- w_value: bfloat16 [768, 768], replicated, may hold values from -0.21875 to 0.21875
- b_value: float32 [768], replicated, may hold values from -1.75 to 1.75
- conv_taps: float32 [12, 9], replicated, may hold values from -0.875 to 0.875
- w_out: bfloat16 [768, 768], replicated, may hold values from -0.625 to 0.625
- b_out: float32 [768], replicated, may hold values from -1.75 to 1.75
- gain_one: float32 [768], replicated, may hold values from 0.5 to 1.5
- bias_one: float32 [768], replicated, may hold values from -1.75 to 1.75
- w_up: bfloat16 [768, 3072], replicated, may hold values from -0.21875 to 0.21875
- b_up: float32 [3072], replicated, may hold values from -1.75 to 1.75
- w_down: bfloat16 [3072, 768], replicated, may hold values from -0.109375 to 0.109375
- b_down: float32 [768], replicated, may hold values from -1.75 to 1.75
- gain_two: float32 [768], replicated, may hold values from 0.5 to 1.5
- bias_two: float32 [768], replicated, may hold values from -1.75 to 1.75
- out_grad: float32 [4, 2048, 768], P('item', 'seq'), may hold values from -6 to 6
Outputs:
- output: float32 [4, 2048, 768], P('item', 'seq')
- d_inputs: float32 [4, 2048, 768], P('item', 'seq')
- counts: float32 [4, 12, 32, 256], P('item', None, 'seq')
- d_w_query: float32 [768, 768], replicated
- d_b_query: float32 [768], replicated
- d_w_key: float32 [768, 768], replicated
- d_b_key: float32 [768], replicated
- d_w_value: float32 [768, 768], replicated
- d_b_value: float32 [768], replicated
- d_conv_taps: float32 [12, 9], replicated
- d_w_out: float32 [768, 768], replicated
- d_b_out: float32 [768], replicated
- d_gain_one: float32 [768], replicated
- d_bias_one: float32 [768], replicated
- d_w_up: float32 [768, 3072], replicated
- d_b_up: float32 [3072], replicated
- d_w_down: float32 [3072, 768], replicated
- d_b_down: float32 [768], replicated
- d_gain_two: float32 [768], replicated
- d_bias_two: float32 [768], replicated
Inputs may be any that keep to these rules, and one draw needn't show every extreme that they name: `lengths`: one item, drawn from the seed, has length 2048; every other item has at least 512 tokens.
All inputs are finite; a program needn't handle non-finite values. No bound on the sum of `pad_mask` on one device may be relied on, other than what follows from the above.
Results may differ from a plain program's by a relative error of at most 0.0003.
Values sent between devices are 32-bit elements; how exact they have to be, the bound alone decides.
No kernel may reach another device: no remote copies, remote signals or barrier semaphores. Data moves between devices by JAX's collectives and lax.ppermute only.
A program may use at most 256 MiB of HBM per device.

v0:
```python
import jax
import jax.numpy as jnp
from jax import lax
from jax.sharding import PartitionSpec as P

MODEL_WIDTH = 768
HEAD_COUNT = 12
HEAD_SIZE = 64
HASH_COUNT = 32
HASH_BITS = 8
CONV = 9


highest = lax.Precision.HIGHEST
softness_scale = 2.0


def extended(block, sides, width):
    for axis, dim in sides:
        count = lax.axis_size(axis)
        forward = [(i, i + 1) for i in range(count - 1)]
        backward = [(target, source) for source, target in forward]
        low = lax.ppermute(
            lax.slice_in_dim(block, block.shape[dim] - width, None, axis=dim), axis, forward
        )
        high = lax.ppermute(lax.slice_in_dim(block, 0, width, axis=dim), axis, backward)
        block = jnp.concatenate([low, block, high], axis=dim)
    return block


def unit_rows(matrix):
    return matrix * lax.rsqrt(jnp.mean(matrix * matrix, axis=-1, keepdims=True) + 1e-06) * 0.125


def hash_signs(matrix, hash_proj):
    sequence_length = matrix.shape[0]
    normed = unit_rows(matrix.reshape(sequence_length, HEAD_COUNT, HEAD_SIZE))
    rotation_angles = jnp.einsum("thd,dk->htk", normed, hash_proj, precision=highest)
    return (
        jnp.tanh(softness_scale * rotation_angles)
        .reshape(HEAD_COUNT, sequence_length, HASH_COUNT, HASH_BITS)
        .transpose(0, 2, 3, 1)
    )


def member(signs):
    groups = signs.shape[0]
    sequence_length = signs.shape[2]
    weights = jnp.ones((groups, 1, sequence_length), jnp.float32)
    for column in range(signs.shape[1]):
        upper = 0.5 * (1.0 + signs[:, column])
        lower = 0.5 * (1.0 - signs[:, column])
        weights = jnp.stack([weights * upper[:, None], weights * lower[:, None]], axis=2)
        weights = weights.reshape(groups, -1, sequence_length)
    return weights


def fill(key_signs, valid_mask, value_rows):
    weights = member(key_signs) * valid_mask
    tables = jnp.einsum("gbt,td->gbd", weights, value_rows, precision=highest)
    return (tables, jnp.sum(weights, axis=2))


def read(query_signs, tables, counts):
    weights = member(query_signs)
    numer = jnp.einsum("gbt,gbd->td", weights, tables, precision=highest)
    denom = jnp.einsum("gbt,gb->t", weights, counts, precision=highest)
    return (numer, denom)


def read_back(query_signs, tables, counts, num_grad, den_grad):
    weights, pull = jax.vjp(member, query_signs)
    table_grad = jnp.einsum("gbt,td->gbd", weights, num_grad, precision=highest)
    count_grad = jnp.einsum("gbt,t->gb", weights, den_grad, precision=highest)
    weight_grad = (
        jnp.einsum("td,gbd->gbt", num_grad, tables, precision=highest)
        + counts[:, :, None] * den_grad[None, None, :]
    )
    return (pull(weight_grad)[0], table_grad, count_grad)


def fill_back(key_signs, valid_mask, value_rows, table_grad, count_grad):
    weights, pull = jax.vjp(member, key_signs)
    value_grad = jnp.einsum("gbt,gbd->td", weights * valid_mask, table_grad, precision=highest)
    weight_grad = (
        jnp.einsum("td,gbd->gbt", value_rows, table_grad, precision=highest)
        + count_grad[:, :, None]
    ) * valid_mask
    return (pull(weight_grad)[0], value_grad)


def layer_norm(matrix):
    centered = matrix - jnp.mean(matrix, axis=-1, keepdims=True)
    return centered * lax.rsqrt(jnp.mean(centered * centered, axis=-1, keepdims=True) + 1e-05)


def project(hidden_in, w_query, b_query, w_key, b_key, w_value, b_value):
    query = jnp.dot(hidden_in, w_query, precision=highest) + b_query
    keys = jnp.dot(hidden_in, w_key, precision=highest) + b_key
    value_rows = jnp.dot(hidden_in, w_value, precision=highest) + b_value
    return (query, keys, value_rows)


def post(
    attn,
    hidden_in,
    w_out,
    b_out,
    gain_one,
    bias_one,
    w_up,
    b_up,
    w_down,
    b_down,
    gain_two,
    bias_two,
):
    first = (
        layer_norm(hidden_in + jnp.dot(attn, w_out, precision=highest) + b_out) * gain_one
        + bias_one
    )
    inner = jax.nn.gelu(jnp.dot(first, w_up, precision=highest) + b_up, approximate=False)
    second = first + jnp.dot(inner, w_down, precision=highest) + b_down
    return layer_norm(second) * gain_two + bias_two


def per_device(
    inputs,
    lengths,
    pad_mask,
    hash_proj,
    w_query,
    b_query,
    w_key,
    b_key,
    w_value,
    b_value,
    conv_taps,
    w_out,
    b_out,
    gain_one,
    bias_one,
    w_up,
    b_up,
    w_down,
    b_down,
    gain_two,
    bias_two,
    out_grad,
):
    local_length = inputs.shape[1]
    window_half = CONV // 2
    hidden_in = inputs[0]
    params = tuple(
        (
            param.astype(jnp.float32)
            for param in (
                w_query,
                b_query,
                w_key,
                b_key,
                w_value,
                b_value,
                conv_taps,
                w_out,
                b_out,
                gain_one,
                bias_one,
                w_up,
                b_up,
                w_down,
                b_down,
                gain_two,
                bias_two,
            )
        )
    )
    position = lax.axis_index("seq") * local_length + lax.iota(jnp.int32, local_length)
    valid_mask = ((position < lengths[0]) & (pad_mask[0] == 1)).astype(jnp.float32)
    (query, keys, value_rows), proj_pull = jax.vjp(project, hidden_in, *params[:6])

    def signs_of(matrix):
        return hash_signs(matrix, hash_proj)

    q_signs, q_pull = jax.vjp(signs_of, query)
    k_signs, k_pull = jax.vjp(signs_of, keys)
    masked_values = value_rows * valid_mask[:, None]
    per_head_values = masked_values.reshape(local_length, HEAD_COUNT, HEAD_SIZE).transpose(1, 0, 2)

    def fill_head(packed):
        return fill(packed[0], valid_mask, packed[1])

    def read_head(packed):
        return read(packed[0], packed[1], packed[2])

    def back_head(packed):
        return read_back(packed[0], packed[1], packed[2], packed[3], packed[4])

    def key_head(packed):
        return fill_back(packed[0], valid_mask, packed[1], packed[2], packed[3])

    part_tab, part_cnt = lax.map(fill_head, (k_signs, per_head_values))
    own_tab, own_cnt = (
        lax.psum_scatter(part_tab, "seq", scatter_dimension=1, tiled=True),
        lax.psum_scatter(part_cnt, "seq", scatter_dimension=1, tiled=True),
    )
    whole_tab, whole_cnt = (
        lax.all_gather(own_tab, "seq", axis=1, tiled=True),
        lax.all_gather(own_cnt, "seq", axis=1, tiled=True),
    )
    num_heads, den_heads = lax.map(read_head, (q_signs, whole_tab, whole_cnt))
    numer = num_heads.transpose(1, 0, 2).reshape(local_length, MODEL_WIDTH)
    denom = den_heads.T
    denom = denom + HASH_COUNT
    mixed = numer.reshape(local_length, HEAD_COUNT, HEAD_SIZE) / denom[:, :, None]
    padded_rows = extended(masked_values, (("seq", 0),), window_half)
    bucket_spread = jnp.repeat(params[6], HEAD_SIZE, axis=0)
    conv = jnp.zeros((local_length, MODEL_WIDTH), jnp.float32)
    for shift_amount in range(CONV):
        conv = (
            conv
            + padded_rows[shift_amount : shift_amount + local_length]
            * bucket_spread[:, shift_amount]
        )
    attn = mixed.reshape(local_length, MODEL_WIDTH) + conv
    output, post_pull = jax.vjp(post, attn, hidden_in, *params[7:])
    post_grads = post_pull(out_grad[0])
    d_attn = post_grads[0]
    padded_gradient = extended(d_attn, (("seq", 0),), window_half)
    masked_value_gradient = jnp.zeros((local_length, MODEL_WIDTH), jnp.float32)
    tap_rows = []
    for shift_amount in range(CONV):
        start_index = 2 * window_half - shift_amount
        masked_value_gradient = (
            masked_value_gradient
            + padded_gradient[start_index : start_index + local_length]
            * bucket_spread[:, shift_amount]
        )
        tap_rows.append(
            jnp.sum(d_attn * padded_rows[shift_amount : shift_amount + local_length], axis=0)
        )
    d_taps = jnp.stack(tap_rows, axis=1).reshape(HEAD_COUNT, HEAD_SIZE, CONV).sum(axis=1)
    d_heads = d_attn.reshape(local_length, HEAD_COUNT, HEAD_SIZE)
    num_grad = d_heads / denom[:, :, None]
    den_grad = -jnp.sum(d_heads * mixed, axis=2) / denom
    sign_grad, tab_part, cnt_part = lax.map(
        back_head, (q_signs, whole_tab, whole_cnt, num_grad.transpose(1, 0, 2), den_grad.T)
    )
    own_tab_grad, own_cnt_grad = (
        lax.psum_scatter(tab_part, "seq", scatter_dimension=1, tiled=True),
        lax.psum_scatter(cnt_part, "seq", scatter_dimension=1, tiled=True),
    )
    tab_grad, cnt_grad = (
        lax.all_gather(own_tab_grad, "seq", axis=1, tiled=True),
        lax.all_gather(own_cnt_grad, "seq", axis=1, tiled=True),
    )
    key_sign_grad, value_portion = lax.map(key_head, (k_signs, per_head_values, tab_grad, cnt_grad))
    masked_value_gradient = masked_value_gradient + value_portion.transpose(1, 0, 2).reshape(
        local_length, MODEL_WIDTH
    )
    value_gradient = masked_value_gradient * valid_mask[:, None]
    d_query = q_pull(sign_grad)[0]
    d_keys = k_pull(key_sign_grad)[0]
    proj_grads = proj_pull((d_query, d_keys, value_gradient))
    grad_list = (
        proj_grads[1],
        proj_grads[2],
        proj_grads[3],
        proj_grads[4],
        proj_grads[5],
        proj_grads[6],
        d_taps,
        post_grads[2],
        post_grads[3],
        post_grads[4],
        post_grads[5],
        post_grads[6],
        post_grads[7],
        post_grads[8],
        post_grads[9],
        post_grads[10],
        post_grads[11],
    )
    flat_grads = jnp.concatenate([grad_piece.reshape(-1) for grad_piece in grad_list])
    device_total = lax.axis_size("item") * lax.axis_size("seq")
    flat_length = flat_grads.shape[0]
    padded_length = -(-flat_length // device_total) * device_total
    flat_grads = jnp.pad(flat_grads, (0, padded_length - flat_length))
    grad_share = lax.psum_scatter(flat_grads, ("item", "seq"), scatter_dimension=0, tiled=True)
    summed_flat = lax.all_gather(grad_share, ("item", "seq"), axis=0, tiled=True)
    summed = []
    offset = 0
    for grad_piece in grad_list:
        piece_size = grad_piece.size
        summed.append(summed_flat[offset : offset + piece_size].reshape(grad_piece.shape))
        offset = offset + piece_size
    d_input = post_grads[1] + proj_grads[0]
    return (output[None], d_input[None], own_cnt[None], *summed)


def solution(mesh):
    in_specs = (
        P("item", "seq", None),
        P("item"),
        P("item", "seq"),
        P(),
        P(),
        P(),
        P(),
        P(),
        P(),
        P(),
        P(),
        P(),
        P(),
        P(),
        P(),
        P(),
        P(),
        P(),
        P(),
        P(),
        P(),
        P("item", "seq", None),
    )
    out_specs = (
        P("item", "seq", None),
        P("item", "seq", None),
        P("item", None, "seq", None),
        P(),
        P(),
        P(),
        P(),
        P(),
        P(),
        P(),
        P(),
        P(),
        P(),
        P(),
        P(),
        P(),
        P(),
        P(),
        P(),
        P(),
    )
    return jax.shard_map(
        per_device, mesh=mesh, in_specs=in_specs, out_specs=out_specs, check_vma=False
    )
```

profile of v0, /device:TPU:25, one launch (start us, length us, event | category | flops | bytes accessed | tf_op | source)
XLA Modules:
  0.0 5842.5 jit_solution(29921998181566566)
XLA Ops:
  21.6 11.5 broadcast.1256.clone3
  33.9 285.7 %while.50 = (s32[]{:T(128)}, f32[12,32,256,64]{2,3,1,0:T(8,128)}, f32[12,32,256]{2,1,0:T(8,128)}, f32[12,32,8,256]{3,1,2,0:T(8,128)}, f32[256]{0:T(256)S(1)}, /*index=5*/f32[12,256,64]{1,2,0:T(8,128)}, s32[]{:T(128)}) while((s32[]{:T(128)}, f32[12,32,256,64]{2,3,1,0:T(8,128)}, f32[12,32,256]{2,1,0:T(8,128)}, f32[12,32,8,256]{3,1,2,0:T(8,128)}, ...), condition=%wide.region_4.5_spmd, body=%wide.region_2.4_spmd.sunk | while | flops 1623400448 | bytes 112231520 | solution.py:202
  321.5 497.4 %all-reduce.52.cloned.1.call-done = (f32[12,32,256,64]{2,3,1,0:T(8,128)}, f32[12,32,256]{2,1,0:T(8,128)}) async-done(((f32[12,32,256,64]{2,3,1,0:T(8,128)}, f32[12,32,256]{2,1,0:T(8,128)}), (f32[12,32,256,64]{2,3,1,0:T(8,128)}, f32[12,32,256]{2,1,0:T(8,128)})) %all-reduce.52.cloned.1.call-update) | async-done | bytes 25559056
  842.0 22.1 all_gather.16
  865.1 180.0 %all-gather.3.cloned.1.call-done = f32[12,32,256,64]{2,3,1,0:T(8,128)} async-done(((f32[12,4,256,64]{2,3,1,0:T(8,128)}), f32[12,32,256,64]{2,3,1,0:T(8,128)}) %all-gather.3.cloned.1.call-update) | async-done | bytes 25165840 | tf_op jit(solution)/shard_map/all_gather | solution.py:208
  1045.1 494.9 %while.51 = (s32[]{:T(128)}, f32[12,256,64]{1,2,0:T(8,128)S(1)}, f32[12,256]{1,0:T(8,128)S(1)}, f32[12,32,8,256]{3,1,2,0:T(8,128)}, f32[12,32,256,64]{2,3,1,0:T(...) while((s32[]{:T(128)}, f32[12,256,64]{1,2,0:T(8,128)S(1)}, f32[12,256]{1,0:T(8,128)S(1)}, ...), condition=%wide.region_8.9_spmd, body=%wide.region_7.8_spmd.sunk | while | flops 1644380160 | bytes 162435216 | solution.py:211
  1585.2 11.5 broadcast.1256.clone2
  1597.5 1206.6 %while.52 = (s32[]{:T(128)}, f32[12,32,8,256]{3,1,2,0:T(8,128)}, f32[12,32,256,64]{2,3,1,0:T(8,128)}, f32[12,32,256]{2,1,0:T(8,128)}, f32[12,32,8,256]{3,1,2,0:T...) while((s32[]{:T(128)}, f32[12,32,8,256]{3,1,2,0:T(8,128)}, ...), condition=%wide.region_33.34_spmd, body=%wide.region_18.33_spmd.sunk | while | flops 3274833920 | bytes 296557696 | solution.py:246
  1629.0 11.6 fusion.329
  1677.4 13.0 bitcast_dynamic-update-slice_fusion.7
  1729.5 11.6 fusion.329
  1777.9 13.1 bitcast_dynamic-update-slice_fusion.7
  1830.1 11.6 fusion.329
  1878.5 13.0 bitcast_dynamic-update-slice_fusion.7
  1930.6 11.6 fusion.329
  1978.9 13.0 bitcast_dynamic-update-slice_fusion.7
  2031.0 11.6 fusion.329
  2079.4 13.0 bitcast_dynamic-update-slice_fusion.7
  2131.5 11.6 fusion.329
  2179.9 13.1 bitcast_dynamic-update-slice_fusion.7
  2232.0 11.6 fusion.329
  2280.4 13.0 bitcast_dynamic-update-slice_fusion.7
  2332.5 11.6 fusion.329
  2380.9 13.1 bitcast_dynamic-update-slice_fusion.7
  2433.0 11.6 fusion.329
  2481.4 13.0 bitcast_dynamic-update-slice_fusion.7
  2533.5 11.6 fusion.329
  2581.9 13.1 bitcast_dynamic-update-slice_fusion.7
  2634.1 11.6 fusion.329
  2682.4 13.0 bitcast_dynamic-update-slice_fusion.7
  2734.6 11.6 fusion.329
  2782.9 13.0 bitcast_dynamic-update-slice_fusion.7
  2804.2 499.0 %all-reduce.50.cloned.1.call-done = (f32[12,32,256,64]{2,3,1,0:T(8,128)}, f32[12,32,256]{2,1,0:T(8,128)}) async-done(((f32[12,32,256,64]{2,3,1,0:T(8,128)}, f32[12,32,256]{2,1,0:T(8,128)}), (f32[12,32,256,64]{2,3,1,0:T(8,128)}, f32[12,32,256]{2,1,0:T(8,128)})) %all-reduce.50.cloned.1.call-update) | async-done | bytes 25559056
  3372.5 23.2 all_gather.18
  3395.7 133.7 %all-gather.5.cloned.1.call-done = f32[12,32,256,64]{2,3,1,0:T(8,128)} async-done(((f32[12,4,256,64]{2,3,1,0:T(8,128)}), f32[12,32,256,64]{2,3,1,0:T(8,128)}) %all-gather.5.cloned.1.call-update) | async-done | bytes 25165840 | tf_op jit(solution)/shard_map/all_gather | solution.py:254
  3532.4 1067.4 %while.53 = (s32[]{:T(128)}, f32[12,32,8,256]{3,1,2,0:T(8,128)}, f32[12,256,64]{1,2,0:T(8,128)}, f32[12,32,8,256]{3,1,2,0:T(8,128)}, f32[12,32,256,64]{2,3,1,0:T...) while((s32[]{:T(128)}, f32[12,32,8,256]{3,1,2,0:T(8,128)}, ...), condition=%wide.region_51.52_spmd, body=%wide.region_36.51_spmd.sunk | while | flops 3251765248 | bytes 254579824 | solution.py:257
  3541.4 11.5 add_multiply_fusion.2
  3563.4 11.6 fusion.349
  3630.3 11.5 add_multiply_fusion.2
  3652.3 11.6 fusion.349
  3719.2 11.5 add_multiply_fusion.2
  3741.2 11.6 fusion.349
  3808.1 11.5 add_multiply_fusion.2
  3830.2 11.6 fusion.349
  3897.0 11.5 add_multiply_fusion.2
  3919.1 11.6 fusion.349
  3986.0 11.5 add_multiply_fusion.2
  4008.0 11.6 fusion.349
  4074.9 11.5 add_multiply_fusion.2
  4096.9 11.6 fusion.349
  4163.8 11.5 add_multiply_fusion.2
  4185.8 11.6 fusion.349
  4252.7 11.5 add_multiply_fusion.2
  4274.7 11.6 fusion.349
  4341.6 11.5 add_multiply_fusion.2
  4363.6 11.6 fusion.349
  4430.5 11.5 add_multiply_fusion.2
  4452.5 11.6 fusion.349
  4541.4 11.6 fusion.349
  4638.4 236.4 %concatenate.34 = f32[7087980]{0:T(1024)} concatenate(f32[589824]{0:T(1024)} %reshape.1638, f32[768]{0:T(1024)S(1)} %reduce_sum.605, f32[589824]{0:T(1024)} %reshape.1639, f32[768]{0:T(1024)S(1)} %reduce_sum.607, f32[589824]{0:T(1024)} %reshape.1640, f32[768]{0:T(1024)S(1)} %get-tuple-element.377, f32[108]{0:T(128)S(1)} %copy-done.172, f32[589824]{0:T(1024)S(1)} %copy-done.33, ...), dimensions={0} | concatenate | bytes 56703840 | tf_op jit(solution)/shard_map/concatenate | solution.py:284
  4874.8 21.7 pad.100
  4896.6 432.1 %all-reduce.48.cloned.1.call-done = f32[7088000]{0:T(1024)} async-done(((f32[7088000]{0:T(1024)}), f32[7088000]{0:T(1024)}) %all-reduce.48.cloned.1.call-update) | async-done | bytes 28352016
  5349.2 424.4 %all-reduce.46.cloned.1.call-done = f32[7088000]{0:T(1024)} async-done(((f32[7088000]{0:T(1024)}), f32[7088000]{0:T(1024)}) %all-reduce.46.cloned.1.call-update) | async-done | bytes 28352016
  5794.2 16.1 fusion.225
  (3863 shorter events, 2733.4 us)
Async XLA Ops:
  7.2 1539.8 %copy-start = (bf16[768,768]{1,0:T(8,128)(2,1)S(1)}, bf16[768,768]{1,0:T(8,128)(2,1)}, u32[]{:S(2)}) copy-start(bf16[768,768]{1,0:T(8,128)(2,1)} %param.41) | copy-start | bytes 3538948
  7.2 811.6 %all-reduce.52.cloned.1.call-start = ((), (), s32[]{:S(2)}) async-start(), calls=%async_computation.5 | async-start | bytes 51118080
  20.4 12.7 copy-start.94
  320.2 724.9 %all-gather.3.cloned.1.call-start = ((), (), s32[]{:S(2)}) async-start(), calls=%async_computation | async-start | bytes 28311552 | tf_op jit(solution)/shard_map/all_gather | solution.py:208
  822.8 2480.4 %all-reduce.50.cloned.1.call-start = ((), (), s32[]{:S(2)}) async-start(), calls=%async_computation.4 | async-start | bytes 51118080
  824.3 720.4 %collective-permute-start = (f32[4,768]{1,0:T(4,128)}, f32[4,768]{1,0:T(4,128)}, u32[]{:S(2)}, u32[]{:S(2)}) collective-permute-start(f32[4,768]{1,0:T(4,128)} %get-tuple-element.592), channel_id=1, source_target_pairs={{0,1},{1,2},{2,3},{3,4},{4,5},{5,6},{6,7},{8,9},{9,10},{10,11},{11... | collective-permute-start | bytes 36872 | tf_op jit(solution)/shard_map/ppermute | solution.py:23
  825.6 719.1 %collective-permute-start.1 = (f32[4,768]{1,0:T(4,128)}, f32[4,768]{1,0:T(4,128)}, u32[]{:S(2)}, u32[]{:S(2)}) collective-permute-start(f32[4,768]{1,0:T(4,128)} %get-tuple-element.591), channel_id=1, source_target_pairs={{1,0},{2,1},{3,2},{4,3},{5,4},{6,5},{7,6},{9,8},{10,9},{11,10},{12... | collective-permute-start | bytes 36872 | tf_op jit(solution)/shard_map/ppermute | solution.py:26
  1547.0 12.6 copy-start.102
  1547.0 12.6 slice-start
  1549.2 28.1 copy-start.14
  1549.2 28.1 copy-start.128
  1549.5 27.9 copy-start.130
  1629.0 11.6 copy-start.5
  1629.0 11.6 copy-start.52
  1629.0 11.7 copy-start.53
  1677.4 13.0 copy-start.3
  1729.5 11.6 copy-start.5
  1729.5 11.6 copy-start.52
  1729.5 11.7 copy-start.53
  1777.9 13.1 copy-start.3
  1830.1 11.6 copy-start.5
  1830.1 11.6 copy-start.52
  1830.1 11.7 copy-start.53
  1878.5 13.0 copy-start.3
  1930.6 11.6 copy-start.5
  1930.6 11.6 copy-start.52
  1930.6 11.7 copy-start.53
  1978.9 13.0 copy-start.3
  2031.0 11.6 copy-start.5
  2031.0 11.6 copy-start.52
  2031.0 11.7 copy-start.53
  2079.4 13.0 copy-start.3
  2131.5 11.6 copy-start.5
  2131.5 11.6 copy-start.52
  2131.5 11.7 copy-start.53
  2179.9 13.1 copy-start.3
  2232.0 11.6 copy-start.5
  2232.0 11.6 copy-start.52
  2232.0 11.7 copy-start.53
  2280.4 13.0 copy-start.3
  2332.5 11.6 copy-start.5
  2332.5 11.6 copy-start.52
  2332.5 11.7 copy-start.53
  2380.9 13.1 copy-start.3
  2433.0 11.6 copy-start.5
  2433.0 11.6 copy-start.52
  2433.0 11.7 copy-start.53
  2481.4 13.0 copy-start.3
  2533.5 11.6 copy-start.52
  2533.5 11.7 copy-start.53
  2581.9 13.1 copy-start.3
  2634.0 11.6 copy-start.52
  2634.1 11.7 copy-start.53
  2682.4 13.0 copy-start.3
  2734.6 11.6 copy-start.52
  2734.6 11.7 copy-start.53
  2782.9 13.0 copy-start.3
  2804.1 725.3 %all-gather.5.cloned.1.call-start = ((), (), s32[]{:S(2)}) async-start(), calls=%async_computation.1 | async-start | bytes 28311552 | tf_op jit(solution)/shard_map/all_gather | solution.py:254
  3307.2 2021.5 %all-reduce.48.cloned.1.call-start = ((), (), s32[]{:S(2)}) async-start(), calls=%async_computation.3 | async-start | bytes 56705024
  3310.2 1317.9 %collective-permute-start.3 = (f32[4,768]{1,0:T(4,128)}, f32[4,768]{1,0:T(4,128)}, u32[]{:S(2)}, u32[]{:S(2)}) collective-permute-start(f32[4,768]{1,0:T(4,128)} %get-tuple-element.588), channel_id=1, source_target_pairs={{0,1},{1,2},{2,3},{3,4},{4,5},{5,6},{6,7},{8,9},{9,10},{10,11},{11... | collective-permute-start | bytes 36872 | tf_op jit(solution)/shard_map/ppermute | solution.py:23
  3311.5 1316.6 %collective-permute-start.2 = (f32[4,768]{1,0:T(4,128)}, f32[4,768]{1,0:T(4,128)}, u32[]{:S(2)}, u32[]{:S(2)}) collective-permute-start(f32[4,768]{1,0:T(4,128)} %get-tuple-element.587), channel_id=1, source_target_pairs={{1,0},{2,1},{3,2},{4,3},{5,4},{6,5},{7,6},{9,8},{10,9},{11,10},{12... | collective-permute-start | bytes 36872 | tf_op jit(solution)/shard_map/ppermute | solution.py:26
  3370.9 161.5 %copy-start.119 = (f32[256]{0:T(256)S(1)}, f32[256]{0:T(256)}, u32[]{:S(2)}) copy-start(f32[256]{0:T(256)} %copy-done.118) | copy-start | bytes 3076
  4896.5 877.1 %all-reduce.46.cloned.1.call-start = ((), (), s32[]{:S(2)}) async-start(), calls=%async_computation.2 | async-start | bytes 56705024
  5821.2 14.3 copy-start.1
  (872 other events, 1787.6 us)
Sparse Core Ops, SparseCore 0:
  319.7 499.0 all-reduce.51
  822.9 222.1 all-gather.2
  2804.3 498.8 all-reduce.49
  3307.3 222.0 all-gather.4
  4896.6 431.9 all-reduce.47
  5341.3 432.2 all-reduce.45
where the time goes:
time: 5890 us; the launch traced here: 5840 us
  waiting for transfers between devices  2170 us (37%)
  local copies, waits for them, and re-layouts  2020 us (34%)
  matrix products  993 us (17%)
  other arithmetic  564 us (10%)
    unnamed x10, waiting for transfers between devices  1850 us
    another operation x300, local copies, waits for them, and re-layouts, member(): jnp.stack([weights * upper[:, None], weights * lower[:, None]], axis=2)  709 us
    reshape x60, local copies, waits for them, and re-layouts, member(): weights = weights.reshape(groups, -1, sequence_length)  644 us
    mul x360, other arithmetic, member(): weights * upper[:, None]  296 us
    concatenate x1, local copies, waits for them, and re-layouts, per_device(): jnp.concatenate([grad_piece.reshape(-1) for grad_piece in grad_list])  236 us
    all_gather x1, waiting for transfers between devices, per_device(): lax.all_gather(own_tab, 'seq', axis=1, tiled=True)  180 us
    dot_general x12, matrix products, read_back(): table_grad = jnp.einsum('gbt,td->gbd', weights, num_grad, precision=highest)  156 us
    dot_general x12, matrix products, fill_back(): jnp.einsum('td,gbd->gbt', value_rows, table_grad, precision=highest)  137 us
  transfers between devices with their start and end apart: 10, of which 6 were waited for; matrix products, arithmetic and copies ran while one was open for 28% of the time, Pallas kernels for 0%

commit v1 on v0

v1 whole, which is shorter than its diff:
```python
import functools
import math

import jax
import jax.numpy as jnp
from jax import lax
from jax.experimental import pallas as pl
from jax.experimental.pallas import tpu as pltpu
from jax.sharding import PartitionSpec as P

MODEL_WIDTH = 768
HEAD_COUNT = 12
HEAD_SIZE = 64
HASH_COUNT = 32
HASH_BITS = 8
BUCKETS = 256
CONV = 9
HALF = CONV // 2
ROWS = 80
CHUNK = 256
VMEM_BYTES = 56 * 1024 * 1024

BF = jnp.bfloat16
F32 = jnp.float32


def split(x):
    hi = x.astype(BF)
    return hi, (x - hi.astype(F32)).astype(BF)


def parts_of(x):
    hi = lax.reduce_precision(x, 8, 7)
    return hi.astype(BF), (x - hi).astype(BF)


def dot(a, b):
    return jnp.dot(a, b, preferred_element_type=F32)


def dot3(a, b):
    ah, al = split(a)
    bh, bl = split(b)
    return dot(ah, bh) + dot(ah, bl) + dot(al, bh)


def contract(a, b, i, j):
    return lax.dot_general(a, b, (((i,), (j,)), ((), ())), preferred_element_type=F32)


def by_weight(x, w, i, j):
    hi, lo = parts_of(x)
    return contract(hi, w, i, j) + contract(lo, w, i, j)


def outer_sum(a, b):
    ah, al = parts_of(a)
    bh, bl = parts_of(b)
    return contract(
        jnp.concatenate([ah, al, ah], axis=0), jnp.concatenate([bh, bh, bl], axis=0), 0, 0
    )


def factors(s8):
    w = s8.shape[1]
    r = lax.broadcasted_iota(jnp.int32, (8, w), 0)
    rows = [jnp.broadcast_to(s8[j : j + 1], (8, w)) for j in range(8)]
    low = [jnp.where((r & m) != 0, rows[j], 1.0) for j, m in ((5, 4), (6, 2), (7, 1))]
    return r, rows, low


def monomials(rows, low):
    out = [low[0] * low[1] * low[2]]
    for j in (4, 3, 2, 1, 0):
        out = out + [rows[j] * x for x in out]
    return out


def row_sums(r, parts):
    step = 1
    while len(parts) > 1:
        bit = (r & step) != 0
        parts = [
            jnp.where(bit, b, a) + pltpu.roll(jnp.where(bit, a, b), step, 0)
            for a, b in zip(parts[0::2], parts[1::2])
        ]
        step *= 2
    return parts[0]


def sign_grad(r, rows, low, phi, d):
    c = [d[8 * v : 8 * v + 8] for v in range(32)]
    parts = []
    for j in range(5):
        half = len(c) // 2
        acc = phi[0] * c[half]
        for n in range(1, half):
            acc = acc + phi[n] * c[half + n]
        parts.append(acc)
        c = [c[n] + rows[j] * c[half + n] for n in range(half)]
    m = c[0]
    zero = jnp.zeros_like(m)
    parts.append(jnp.where((r & 4) != 0, m * low[1] * low[2], zero))
    parts.append(jnp.where((r & 2) != 0, m * low[0] * low[2], zero))
    parts.append(jnp.where((r & 1) != 0, m * low[0] * low[1], zero))
    return row_sums(r, parts)


def norm_scale(u):
    return lax.rsqrt(jnp.mean(u * u, axis=0, keepdims=True) + 1e-06)


def signs_of(u, proj):
    return jnp.tanh(2.0 * dot3(proj, u * (norm_scale(u) * 0.125)))


def columns(rows64, row):
    t = jnp.concatenate([rows64, row, jnp.zeros((63, row.shape[1]), F32)], axis=0).T
    return jnp.concatenate(split(t), axis=1)


def stacked(rows64, row):
    width = row.shape[1]
    hi, lo = split(jnp.concatenate([rows64, row, jnp.zeros((15, width), F32)], axis=0))
    return jnp.concatenate([hi, hi, lo, jnp.zeros((16, width), BF)], axis=0)


def beside(tab):
    hi = tab.astype(BF).astype(F32)
    lo = pltpu.roll(tab - hi, ROWS, 1)
    again = pltpu.roll(hi, 2 * ROWS - 128, 1)
    lane = lax.broadcasted_iota(jnp.int32, tab.shape, 1)
    return jnp.concatenate(
        [jnp.where(lane < ROWS, hi, lo), jnp.where(lane < 2 * ROWS - 128, lo, again)], axis=1
    ).astype(BF)


def halves(tab):
    return jnp.concatenate(split(tab.T[:ROWS]), axis=0)


def shifted(x, offset):
    if offset == 0:
        return x
    width = x.shape[1]
    t = lax.broadcasted_iota(jnp.int32, x.shape, 1) + offset
    return jnp.where((t >= 0) & (t < width), pltpu.roll(x, (-offset) % width, 1), 0.0)


def reorder(x, outer, inner, block):
    return jnp.concatenate(
        [
            x[:, (o * inner + i) * block : (o * inner + i + 1) * block]
            for i in range(inner)
            for o in range(outer)
        ],
        axis=1,
    )


def fwd_kernel(
    hashes, groups, inner, q_ref, k_ref, v_ref, valid_ref, proj_ref, taps_ref,
    num_ref, tab_ref, conv_ref, sq, sk, cols,
):
    head = pl.program_id(0)
    width = q_ref.shape[2]
    block = width // (groups * inner)
    sq[...] = signs_of(q_ref[0], proj_ref[...])
    sk[...] = signs_of(k_ref[0], proj_ref[...])
    v = v_ref[0]
    cols[...] = columns(v, valid_ref[...])
    num_ref[0] = jnp.zeros(num_ref.shape[1:], F32)
    natural = reorder(v, inner, groups, block)
    conv = jnp.zeros(natural.shape, F32)
    for j in range(CONV):
        conv = conv + shifted(natural, j - HALF) * taps_ref[head, j]
    conv_ref[0] = reorder(conv, groups, inner, block)

    @pl.loop(0, hashes)
    def _(g):
        base = pl.multiple_of(g * 8, 8)
        acc = None
        for c in range(0, width, CHUNK):
            _, rows, low = factors(sk[pl.ds(base, 8), c : c + CHUNK])
            hi, lo = split(jnp.concatenate(monomials(rows, low), axis=0))
            value = cols[c : c + CHUNK, :]
            p = dot(hi, value) + dot(lo, value)
            acc = p if acc is None else acc + p
        tab = (acc[:, :128] + acc[:, 128:]) * (1.0 / BUCKETS)
        tab_ref[0, g] = tab
        ext = halves(tab)
        for c in range(0, width, CHUNK):
            _, rows, low = factors(sq[pl.ds(base, 8), c : c + CHUNK])
            hi, lo = split(jnp.concatenate(monomials(rows, low), axis=0))
            p = dot(ext, hi)
            num_ref[0, :, c : c + CHUNK] += p[:ROWS] + p[ROWS:] + dot(ext[:ROWS], lo)


def bwd_kernel(
    hashes, groups, inner, q_ref, k_ref, v_ref, valid_ref, proj_ref, num_ref, da_ref, tab_ref, taps_ref,
    dq_ref, dk_ref, dv_ref, dt_ref, sq, sk, gq, gk, cols, xq, xk, dv,
):
    head = pl.program_id(0)
    width = q_ref.shape[2]
    block = width // (groups * inner)
    sq[...] = signs_of(q_ref[0], proj_ref[...])
    sk[...] = signs_of(k_ref[0], proj_ref[...])
    da = da_ref[0]
    v = v_ref[0]
    inv = 1.0 / (num_ref[0, 64:65, :] + HASH_COUNT)
    dn = da * inv
    dd = -jnp.sum(dn * num_ref[0, :64, :], axis=0, keepdims=True) * inv
    cols[...] = columns(dn, dd)
    xq[...] = stacked(dn, dd)
    xk[...] = stacked(v, valid_ref[...])
    dv[...] = jnp.zeros(dv.shape, F32)

    @pl.loop(0, hashes)
    def _(g):
        base = pl.multiple_of(g * 8, 8)
        tabs = beside(tab_ref[0, g])
        acc = None
        for c in range(0, width, CHUNK):
            s8 = sq[pl.ds(base, 8), c : c + CHUNK]
            r, rows, low = factors(s8)
            phi = monomials(rows, low)
            hi, lo = split(jnp.concatenate(phi, axis=0))
            value = cols[c : c + CHUNK, :]
            p = dot(hi, value) + dot(lo, value)
            acc = p if acc is None else acc + p
            d = dot(tabs, xq[:, c : c + CHUNK])
            gq[pl.ds(base, 8), c : c + CHUNK] = sign_grad(r, rows, low, phi, d) * (2.0 - 2.0 * s8 * s8)
        tab = (acc[:, :128] + acc[:, 128:]) * (1.0 / BUCKETS)
        ext = halves(tab)
        tabs = beside(tab)
        for c in range(0, width, CHUNK):
            s8 = sk[pl.ds(base, 8), c : c + CHUNK]
            r, rows, low = factors(s8)
            phi = monomials(rows, low)
            hi, lo = split(jnp.concatenate(phi, axis=0))
            p = dot(ext, hi)
            dv[:, c : c + CHUNK] += p[:ROWS] + p[ROWS:] + dot(ext[:ROWS], lo)
            d = dot(tabs, xk[:, c : c + CHUNK])
            gk[pl.ds(base, 8), c : c + CHUNK] = sign_grad(r, rows, low, phi, d) * (2.0 - 2.0 * s8 * s8)

    back = proj_ref[...].T
    for u_ref, g_ref, o_ref in ((q_ref, gq, dq_ref), (k_ref, gk, dk_ref)):
        u = u_ref[0]
        scale = norm_scale(u)
        g = dot3(back, g_ref[...])
        inside = g - u * (scale * scale * jnp.mean(g * u, axis=0, keepdims=True))
        o_ref[0] = (scale * 0.125) * inside
    natural = reorder(v, inner, groups, block)
    grad = reorder(da, inner, groups, block)
    conv = jnp.zeros(natural.shape, F32)
    for j in range(CONV):
        conv = conv + shifted(grad, HALF - j) * taps_ref[head, j]
        moved = grad * shifted(natural, j - HALF)
        dt_ref[0, j : j + 1, :] = jnp.sum(moved, axis=0, keepdims=True)
    dv_ref[0] = (dv[:64, :] + reorder(conv, groups, inner, block)) * valid_ref[...]


def one(*shape, at=0):
    return pl.BlockSpec((1,) + shape, lambda h: (h + at,) + (0,) * len(shape))


def same(*shape):
    return pl.BlockSpec(shape, lambda h: (0,) * len(shape))


SMEM = pl.BlockSpec(memory_space=pltpu.SMEM)


def attend(qkv, valid, proj, taps, groups, inner):
    heads, width = qkv.shape[0] // 3, qkv.shape[2]
    hashes = proj.shape[0] // 8
    return pl.pallas_call(
        functools.partial(fwd_kernel, hashes, groups, inner),
        grid=(heads,),
        in_specs=[
            one(64, width), one(64, width, at=heads), one(64, width, at=2 * heads),
            same(1, width), same(*proj.shape), SMEM,
        ],
        out_specs=[one(ROWS, width), one(hashes, BUCKETS, 128), one(64, width)],
        out_shape=[
            jax.ShapeDtypeStruct((heads, ROWS, width), F32),
            jax.ShapeDtypeStruct((heads, hashes, BUCKETS, 128), F32),
            jax.ShapeDtypeStruct((heads, 64, width), F32),
        ],
        scratch_shapes=[pltpu.VMEM((hashes * 8, width), F32)] * 2 + [pltpu.VMEM((width, 256), BF)],
        compiler_params=pltpu.CompilerParams(vmem_limit_bytes=VMEM_BYTES),
        name="attend",
    )(qkv, qkv, qkv, valid, proj, taps)


def attend_back(qkv, valid, proj, num, d_attn, tab, taps, groups, inner):
    heads, width = qkv.shape[0] // 3, qkv.shape[2]
    hashes = proj.shape[0] // 8
    return pl.pallas_call(
        functools.partial(bwd_kernel, hashes, groups, inner),
        grid=(heads,),
        in_specs=[
            one(64, width), one(64, width, at=heads), one(64, width, at=2 * heads),
            same(1, width), same(*proj.shape), one(ROWS, width), one(64, width),
            one(hashes, BUCKETS, 128), SMEM,
        ],
        out_specs=[one(64, width)] * 3 + [one(16, width)],
        out_shape=[jax.ShapeDtypeStruct((heads, 64, width), F32)] * 3
        + [jax.ShapeDtypeStruct((heads, 16, width), F32)],
        scratch_shapes=[pltpu.VMEM((hashes * 8, width), F32)] * 4
        + [pltpu.VMEM((width, 256), BF)]
        + [pltpu.VMEM((256, width), BF)] * 2
        + [pltpu.VMEM((ROWS, width), F32)],
        compiler_params=pltpu.CompilerParams(vmem_limit_bytes=VMEM_BYTES),
        name="attend_back",
    )(qkv, qkv, qkv, valid, proj, num, d_attn, tab, taps)


class Line:
    def __init__(self, groups, inner):
        self.groups, self.inner = groups, inner
        index = lax.axis_index("seq")
        self.z, self.c = index // inner, index % inner

    def send(self, x, target):
        pairs = []
        for z in range(self.groups):
            for c in range(self.inner):
                to = target(z, c)
                if to is not None:
                    pairs.append((z * self.inner + c, to[0] * self.inner + to[1]))
        return lax.ppermute(x, "seq", pairs)

    def ordered(self, parts, place):
        count = len(parts)
        whole = jnp.stack(parts)
        return jnp.stack(
            [
                lax.dynamic_index_in_dim(whole, (place - s) % count, 0, keepdims=False)
                for s in range(count)
            ]
        )

    def gather_z(self, x):
        groups = self.groups
        right, left = [x], [x]
        for step in range(1, groups):
            right.append(
                self.send(right[-1], lambda z, c: (z + 1, c) if step - 1 <= z < groups - 1 else None)
            )
            left.append(
                self.send(left[-1], lambda z, c: (z - 1, c) if 0 < z <= groups - step else None)
            )
        parts = [x] + [right[s] + left[groups - s] for s in range(1, groups)]
        return self.ordered(parts, self.z)

    def gather_c(self, x):
        parts = [x] + [
            self.send(x, lambda z, c: (z, (c + s) % self.inner)) for s in range(1, self.inner)
        ]
        return self.ordered(parts, self.c)

    def sum_c(self, x):
        step = 1
        while step < self.inner:
            x = x + self.send(x, lambda z, c: (z, c ^ step))
            step *= 2
        return x

    def share_c(self, x):
        total = lax.dynamic_index_in_dim(x, self.c, 0, keepdims=False)
        for s in range(1, self.inner):
            block = lax.dynamic_index_in_dim(x, (self.c + s) % self.inner, 0, keepdims=False)
            total = total + self.send(block, lambda z, c: (z, (c + s) % self.inner))
        return total

    def swap_z(self, x):
        parts = [lax.dynamic_index_in_dim(x, self.z, 0, keepdims=False)]
        for s in range(1, self.groups):
            block = lax.dynamic_index_in_dim(x, (self.z + s) % self.groups, 0, keepdims=False)
            parts.append(self.send(block, lambda z, c: ((z + s) % self.groups, c)))
        return self.ordered(parts, self.z)


def normalize(x):
    centered = x - jnp.mean(x, axis=-1, keepdims=True)
    scale = lax.rsqrt(jnp.mean(centered * centered, axis=-1, keepdims=True) + 1e-05)
    return centered * scale, scale


def normalize_back(grad, normed, scale):
    mean = jnp.mean(grad, axis=-1, keepdims=True)
    along = jnp.mean(grad * normed, axis=-1, keepdims=True)
    return scale * (grad - mean - normed * along)


def dense(x, attn_t, out_grad, w_out, b_out, gain_one, bias_one, w_up, b_up, w_down, b_down, gain_two, bias_two):
    n1, scale1 = normalize(x + by_weight(attn_t, w_out, 0, 0) + b_out)
    first = n1 * gain_one + bias_one
    hidden = by_weight(first, w_up, 1, 0) + b_up
    cdf = 0.5 + 0.5 * lax.erf(hidden * math.sqrt(0.5))
    inner = hidden * cdf
    n2, scale2 = normalize(first + by_weight(inner, w_down, 1, 0) + b_down)
    output = n2 * gain_two + bias_two
    d_second = normalize_back(out_grad * gain_two, n2, scale2)
    slope = cdf + hidden * (jnp.exp(-0.5 * hidden * hidden) * (1.0 / math.sqrt(2.0 * math.pi)))
    d_hidden = by_weight(d_second, w_down, 1, 1) * slope
    d_first = d_second + by_weight(d_hidden, w_up, 1, 1)
    d_pre = normalize_back(d_first * gain_one, n1, scale1)
    d_hi, d_lo = parts_of(d_pre)
    d_attn_t = contract(w_out, d_hi, 1, 1) + contract(w_out, d_lo, 1, 1)
    grads = dict(
        w_out=outer_sum(attn_t.T, d_pre),
        b_out=jnp.sum(d_pre, axis=0),
        gain_one=jnp.sum(d_first * n1, axis=0),
        bias_one=jnp.sum(d_first, axis=0),
        w_up=outer_sum(first, d_hidden),
        b_up=jnp.sum(d_hidden, axis=0),
        w_down=outer_sum(inner, d_second),
        b_down=jnp.sum(d_second, axis=0),
        gain_two=jnp.sum(out_grad * n2, axis=0),
        bias_two=jnp.sum(out_grad, axis=0),
    )
    return output, d_attn_t, d_pre, grads


def hadamard():
    index = lax.iota(jnp.int32, BUCKETS)
    both = lax.population_count(index[:, None] & index[None, :])
    return jnp.where((both & 1) == 0, 1.0, -1.0).astype(BF)


def per_device(
    inputs, lengths, pad_mask, hash_proj, w_query, b_query, w_key, b_key, w_value, b_value, conv_taps,
    w_out, b_out, gain_one, bias_one, w_up, b_up, w_down, b_down, gain_two, bias_two, out_grad,
):
    count = lax.axis_size("seq")
    groups = math.gcd(HEAD_COUNT, count)
    inner = count // groups
    line = Line(groups, inner)
    heads = HEAD_COUNT // groups
    feats = heads * HEAD_SIZE
    own_hashes = HASH_COUNT // count
    hashes = own_hashes * groups
    tokens = inputs.shape[1]
    width = count * tokens
    x = inputs[0]

    x_line = line.gather_z(x)
    x_all = line.gather_c(x_line).reshape(width, MODEL_WIDTH)
    mask_all = line.gather_c(line.gather_z(pad_mask)).reshape(inner, groups, tokens)
    position = (
        (lax.iota(jnp.int32, groups)[None, :, None] * inner + lax.iota(jnp.int32, inner)[:, None, None])
        * tokens
        + lax.iota(jnp.int32, tokens)[None, None, :]
    )
    valid = ((position < lengths[0]) & (mask_all == 1)).astype(F32).reshape(1, width)

    def head_columns(w):
        return lax.dynamic_slice_in_dim(w, line.z * feats, feats, axis=w.ndim - 1)

    w_qkv = jnp.concatenate([head_columns(w) for w in (w_query, w_key, w_value)], axis=1)
    b_qkv = jnp.concatenate([head_columns(b) for b in (b_query, b_key, b_value)])
    x_hi, x_lo = parts_of(x_all)
    qkv = contract(w_qkv, x_hi, 0, 1) + contract(w_qkv, x_lo, 0, 1) + b_qkv[:, None]
    keep = jnp.concatenate(
        [jnp.ones((2 * feats, 1), F32), jnp.zeros((feats, 1), F32)], axis=0
    )
    qkv = qkv * jnp.where(keep > 0, 1.0, valid)
    qkv = qkv.reshape(3 * heads, HEAD_SIZE, width)
    proj = lax.dynamic_index_in_dim(
        hash_proj.reshape(HEAD_SIZE, groups, inner, own_hashes * HASH_BITS), line.c, 2, keepdims=False
    )
    proj = proj.reshape(HEAD_SIZE, hashes * HASH_BITS).T
    taps = lax.dynamic_slice_in_dim(conv_taps, line.z * heads, heads, axis=0)

    num_part, tab, conv = attend(qkv, valid, proj, taps, groups, inner)
    num = line.sum_c(num_part)
    mixed = num[:, :HEAD_SIZE] / (num[:, HEAD_SIZE : HEAD_SIZE + 1] + HASH_COUNT)
    attn = (mixed + conv).reshape(feats, inner, groups, tokens)
    mine = lax.dynamic_index_in_dim(attn, line.c, 1, keepdims=False)
    attn_t = line.swap_z(mine.transpose(1, 0, 2)).reshape(MODEL_WIDTH, tokens)

    subsets = tab[:, :, :, HEAD_SIZE].reshape(heads * hashes, BUCKETS)
    sub_hi, sub_rest = parts_of(subsets)
    sub_mid, sub_lo = parts_of(subsets - sub_hi.astype(F32))
    signs = hadamard()
    own_counts = contract(sub_hi, signs, 1, 0) + contract(sub_mid, signs, 1, 0) + contract(sub_lo, signs, 1, 0)
    own_counts = own_counts.reshape(heads, groups, own_hashes, BUCKETS).transpose(1, 0, 2, 3)
    counts = line.swap_z(own_counts).reshape(HEAD_COUNT, own_hashes, BUCKETS)

    output, d_attn_t, d_pre, grads = dense(
        x, attn_t, out_grad[0], w_out, b_out, gain_one, bias_one, w_up, b_up, w_down, b_down, gain_two, bias_two
    )
    d_line = line.swap_z(d_attn_t.reshape(groups, feats, tokens))
    d_all = line.gather_c(d_line).transpose(2, 0, 1, 3).reshape(heads, HEAD_SIZE, width)

    first_c = jnp.where(line.c == 0, 1.0, 0.0)
    d_q, d_k, d_v, d_t = attend_back(qkv, valid, proj, num, d_all, tab, taps * first_c, groups, inner)
    d_qkv = jnp.stack([d_q, d_k, d_v]).reshape(3 * feats, inner, groups * tokens)
    d_mine = line.share_c(d_qkv.transpose(1, 0, 2))
    d_taps = jnp.sum(d_t[:, :CONV], axis=2) * first_c

    back = line.swap_z(d_mine.reshape(3 * feats, groups, tokens).transpose(1, 0, 2))
    back = back.reshape(groups, 3, feats, tokens)
    d_x = d_pre
    for i, w in enumerate((w_query, w_key, w_value)):
        d_x = d_x + by_weight(back[:, i].reshape(MODEL_WIDTH, tokens), w, 0, 1)

    dh, dl = parts_of(d_mine)
    xh, xl = parts_of(x_line.reshape(groups * tokens, MODEL_WIDTH))
    d_w = contract(xh, dh, 0, 1) + contract(xl, dh, 0, 1) + contract(xh, dl, 0, 1)
    d_b = jnp.sum(d_mine, axis=1)
    d_cols = jnp.concatenate([d_w, d_b[None, :]], axis=0)
    placed = jnp.zeros((groups, MODEL_WIDTH + 1, 3 * feats), F32)
    placed = lax.dynamic_update_index_in_dim(placed, d_cols, line.z, 0)
    taps_placed = lax.dynamic_update_index_in_dim(
        jnp.zeros((groups, heads, CONV), F32), d_taps, line.z, 0
    )
    both = ("item", "seq")
    summed = lax.psum(placed, both)
    d_conv_taps = lax.psum(taps_placed, both).reshape(HEAD_COUNT, CONV)
    summed = summed.reshape(groups, MODEL_WIDTH + 1, 3, feats).transpose(2, 1, 0, 3)
    summed = summed.reshape(3, MODEL_WIDTH + 1, MODEL_WIDTH)
    names = (
        "w_out", "b_out", "gain_one", "bias_one", "w_up", "b_up", "w_down", "b_down", "gain_two", "bias_two",
    )
    grads = lax.psum(grads, both)
    result = []
    for i in range(3):
        result += [summed[i, :MODEL_WIDTH], summed[i, MODEL_WIDTH]]
    result += [d_conv_taps] + [grads[name] for name in names]
    return (output[None], d_x[None], counts[None], *result)


def solution(mesh):
    tokens = P("item", "seq", None)
    in_specs = (tokens, P("item"), P("item", "seq")) + (P(),) * 18 + (tokens,)
    out_specs = (tokens, tokens, P("item", None, "seq", None)) + (P(),) * 17
    return jax.shard_map(
        per_device, mesh=mesh, in_specs=in_specs, out_specs=out_specs, check_vma=False
    )
```

time: 5890 us -> 1030 us (0.17)
  local copies, waits for them, and re-layouts: 2020 us -> 90.9 us
  waiting for transfers between devices: 2170 us -> 458 us
  matrix products: 993 us -> 49.1 us
  other arithmetic: 564 us -> 35 us
  Pallas kernels: 0 us -> 227 us
    unnamed x10 -> x1, waiting for transfers between devices: 1850 us -> 0.02 us
    dot_general x118 -> x29, matrix products: 993 us -> 49.1 us  [contract(): lax.dot_general(a, b, (((i,), (j,)), ((), ())), preferred_element_type=F32)]
    another operation x318 -> x3, local copies, waits for them, and re-layouts: 739 us -> 17.9 us  [the longest x300 709 us: member(): jnp.stack([weights * upper[:, None], weights * lower[:, None]], axis=2)]
    reshape x78 -> x6, local copies, waits for them, and re-layouts: 714 us -> 14.8 us  [the longest x1 7.51 us: per_device(): jnp.stack([d_q, d_k, d_v]).reshape(3 * feats, inner, groups * tokens)]
    psum x0 -> x1, waiting for transfers between devices: none -> 368 us  [per_device(): summed = lax.psum(placed, both)]
    all_gather x2 -> x0, waiting for transfers between devices: 314 us -> none  [the longest x1 180 us: per_device(): lax.all_gather(own_tab, 'seq', axis=1, tiled=True)]
    mul x554 -> x3, other arithmetic: 314 us -> 1.28 us  [the longest x1 1.27 us: per_device(): taps * first_c]
    concatenate x1 -> x0, local copies, waits for them, and re-layouts: 236 us -> none  [per_device(): jnp.concatenate([grad_piece.reshape(-1) for grad_piece in grad_list])]
  transfers between devices with their start and end apart: 10 -> 30, of which waited for: 6 -> 13; matrix products, arithmetic and copies ran while one was open for 28% -> 5% of each run, Pallas kernels for 0% -> 0%
where the time goes in v1:
time: 1030 us; the launch traced here: 1010 us
  waiting for transfers between devices  458 us (44%)
  Pallas kernels  227 us (22%)
  blocking collectives  97.9 us (10%)
  local copies, waits for them, and re-layouts  90.9 us (9%)
  matrix products  49.1 us (5%)
  starting transfers between devices  39 us (4%)
  other arithmetic  35 us (3%)
  between operations  16.7 us (2%)
    psum x1, waiting for transfers between devices, per_device(): summed = lax.psum(placed, both)  368 us
    pallas_call x1, Pallas kernels, attend_back(): pl.pallas_call(functools.partial(bwd_kernel, hashes, groups, inner), grid...  133 us
    psum x1, blocking collectives, per_device(): d_conv_taps = lax.psum(taps_placed, both).reshape(HEAD_COUNT, CONV)  97.9 us
    pallas_call x1, Pallas kernels, attend(): pl.pallas_call(functools.partial(fwd_kernel, hashes, groups, inner), grid...  93.3 us
    ppermute x29, waiting for transfers between devices, send(): return lax.ppermute(x, 'seq', pairs)  90.1 us
    dot_general x29, matrix products, contract(): lax.dot_general(a, b, (((i,), (j,)), ((), ())), preferred_element_type=F32)  49.1 us
    ppermute x29, starting transfers between devices, send(): return lax.ppermute(x, 'seq', pairs)  39 us
    unnamed x119, local copies, waits for them, and re-layouts  31.3 us
  transfers between devices with their start and end apart: 30, of which 13 were waited for; matrix products, arithmetic and copies ran while one was open for 5% of the time, Pallas kernels for 0%

profile of v1, /device:TPU:25, one launch (start us, length us, event | category | flops | bytes accessed | tf_op | source)
XLA Modules:
  0.0 1013.0 jit_solution(14083930771599766635)
XLA Ops:
  7.3 2.3 collective-permute-start.1
  10.8 15.2 %collective-permute-done.1 = f32[256,768]{1,0:T(8,128)S(1)} collective-permute-done((f32[256,768]{1,0:T(8,128)}, f32[256,768]{1,0:T(8,128)S(1)}, u32[]{:S(2)}, u32[]{:S(2)}) %collective-permute-start.1) | collective-permute-done | bytes 786464 | tf_op jit(solution)/shard_map/ppermute | solution.py:332
  26.7 3.0 collective-permute-done
  31.0 1.6 collective-permute-start.3
  32.6 16.3 %collective-permute-done.4 = f32[256,768]{1,0:T(8,128)} collective-permute-done((f32[256,768]{1,0:T(8,128)S(1)}, f32[256,768]{1,0:T(8,128)}, u32[]{:S(2)}, u32[]{:S(2)}) %collective-permute-start.4) | collective-permute-done | bytes 786464 | tf_op jit(solution)/shard_map/ppermute | solution.py:332
  52.8 14.5 %collective-permute-done.5 = f32[256,768]{1,0:T(8,128)} collective-permute-done((f32[256,768]{1,0:T(8,128)}, f32[256,768]{1,0:T(8,128)}, u32[]{:S(2)}, u32[]{:S(2)}) %collective-permute-start.5) | collective-permute-done | bytes 786464 | tf_op jit(solution)/shard_map/ppermute | solution.py:332
  69.2 3.2 pad_maximum_fusion.3
  72.4 3.7 collective-permute-start.6
  80.7 1.5 constant_dynamic-slice_fusion.45
  87.9 4.2 collective-permute-done.11
  93.4 3.0 collective-permute-done.12
  96.5 2.6 collective-permute-start.13
  101.2 3.9 fusion.23
  106.7 2.5 fusion.76
  109.3 5.3 select_multiply_fusion
  114.6 93.3 %attend.1 = (f32[3,80,2048]{2,1,0:T(8,128)}, f32[3,16,256,128]{3,2,1,0:T(8,128)}, f32[3,64,2048]{2,1,0:T(8,128)}) custom-call(f32[9,64,2048]{2,1,0:T(8,128)} %bitcast.219, f32[9,64,2048]{2,1,0:T(8,128)} %bitcast.220, f32[9,64,2048]{2,1,0:T(8,128)} %bitcast.221, f32[1,2048]{1,0:T(1,128)} %and_convert_fusion.valid_ref, f32[128,64]{1,0:T(8,128)} %bitcast.244, ...), custom_call_target="tpu_custom_call" | custom-call | tf_op jit(solution)/shard_map/attend/pallas_call | solution.py:277
  208.0 4.2 collective-permute-done.14
  212.2 2.4 add.471.num_ref
  214.6 1.7 fusion.26
  216.4 3.1 reshape.268
  219.5 2.9 constant_dynamic-slice_fusion.32
  224.0 5.0 collective-permute-done.15
  229.1 11.6 %collective-permute-done.16 = f32[192,256]{1,0:T(8,128)S(1)} collective-permute-done((f32[192,256]{1,0:T(8,128)S(1)}, f32[192,256]{1,0:T(8,128)S(1)}, u32[]{:S(2)}, u32[]{:S(2)}) %collective-permute-start.16) | collective-permute-done | bytes 196640 | tf_op jit(solution)/shard_map/ppermute | solution.py:332
  243.5 1.4 fusion.114
  244.9 2.8 fusion.15
  247.8 1.4 fusion.115
  249.4 1.6 fusion.112
  251.7 1.8 fusion.106
  253.6 1.4 fusion.116
  255.1 3.4 fusion.109
  258.5 1.4 fusion.117
  260.2 2.3 multiply_reduce_fusion
  266.7 2.0 collective-permute-start.19
  268.7 2.7 collective-permute-start.18
  271.4 2.0 collective-permute-done.20
  273.4 9.2 collective-permute-done.19
  284.2 1.9 collective-permute-done.21
  287.5 2.0 reshape.271.da_ref
  289.5 133.3 %attend_back.1 = (f32[3,64,2048]{2,1,0:T(8,128)}, f32[3,64,2048]{2,1,0:T(8,128)}, f32[3,64,2048]{2,1,0:T(8,128)}, f32[3,16,2048]{2,1,0:T(8,128)}) custom-call(f32[9,64,2048]{2,1,0:T(8,128)} %bitcast.222, f32[9,64,2048]{2,1,0:T(8,128)} %bitcast.223, f32[9,64,2048]{2,1,0:T(8,128)} %bitcast.224, f32[1,2048]{1,0:T(1,128)} %and_convert_fusion.valid_ref, ...), custom_call_target="tpu_custom_call" | custom-call | tf_op jit(solution)/shard_map/attend_back/pallas_call | solution.py:299
  422.8 5.1 pad_maximum_fusion.1
  427.9 7.5 reshape.272
  435.4 8.6 constant_dynamic-slice_fusion.17
  445.0 2.3 fusion.17
  447.5 2.5 fusion.41
  450.0 6.4 fusion.7
  456.5 6.5 fusion.1
  467.8 3.8 copy.63
  473.5 6.1 slice_reduce_fusion
  480.8 4.0 collective-permute-start.28
  484.8 2.6 collective-permute-start.27
  487.4 2.1 reshape.273
  489.5 6.3 constant_dynamic-slice_fusion.15
  498.8 1.5 collective-permute-start.24
  501.9 97.9 %all-reduce = (f32[12,9]{1,0:T(8,128)}, f32[768]{0:T(1024)}, f32[768]{0:T(1024)}, f32[768]{0:T(1024)}, f32[3072]{0:T(1024)}, /*index=5*/f32[768]{0:T(1024)}, f32[768]{0:T(1024)}, f32[768]{0:T(1024)}) all-reduce(f32[12,9]{1,0:T(8,128)S(1)} %reshape.279, f32[768]{0:T(1024)} %get-tuple-element.98, ...), channel_id=1, replica_groups=mesh['item'=4,'seq'=8] {'item','seq'}, use_global_device_ids=true, to_apply=%region_11.12 | all-reduce | flops 7788 | bytes 62304 | tf_op jit(solution)/shard_map/psum | solution.py:522
  604.8 1.4 fusion.28
  606.2 367.5 %all-reduce.4.cloned.1.call-done = (f32[3,769,768]{1,2,0:T(8,128)}, f32[768,768]{1,0:T(8,128)}, f32[768,3072]{1,0:T(8,128)}, f32[3072,768]{1,0:T(8,128)}) async-done(((f32[3,769,768]{1,2,0:T(8,128)}, f32[768,768]{1,0:T(8,128)}, f32[768,3072]{1,0:T(8,128)}, f32[3072,768]{1,0:T(8,128)}), (f32[3,769,768]{1,2,0:T(8,128)}, f32[768,768]{1,0:T(8,128)}, f32[768,3072]{1,0:T(8,128)}, ...) | async-done | bytes 28320784 | tf_op jit(solution)/shard_map/psum | solution.py:521
  973.8 2.2 slice_reduce_fusion.1
  976.0 5.7 slice_bitcast_fusion
  981.7 3.0 copy.66
  984.8 3.0 copy.65
  987.8 1.9 copy.64
  989.8 3.4 copy.107
  993.1 8.8 copy.108
  1001.9 3.7 copy.109
  (252 shorter events, 54.3 us)
Async XLA Ops:
  7.2 233.8 %copy-start = (bf16[768,768]{1,0:T(8,128)(2,1)S(1)}, bf16[768,768]{1,0:T(8,128)(2,1)}, u32[]{:S(2)}) copy-start(bf16[768,768]{1,0:T(8,128)(2,1)} %param.33) | copy-start | bytes 3538948
  7.2 966.6 %all-reduce.4.cloned.1.call-start = ((), (), s32[]{:S(2)}) async-start(), calls=%async_computation | async-start | bytes 58982400 | tf_op jit(solution)/shard_map/psum | solution.py:521
  7.3 18.7 %collective-permute-start.1 = (f32[256,768]{1,0:T(8,128)}, f32[256,768]{1,0:T(8,128)S(1)}, u32[]{:S(2)}, u32[]{:S(2)}) collective-permute-start(f32[256,768]{1,0:T(8,128)} %bitcast.234), channel_id=1, source_target_pairs={{2,0},{3,1},{4,2},{5,3},{6,4},{7,5},{10,8},{11,9},{12,10},{13,11},... | collective-permute-start | bytes 2359304 | tf_op jit(solution)/shard_map/ppermute | solution.py:332
  9.5 20.2 %collective-permute-start = (f32[256,768]{1,0:T(8,128)}, f32[256,768]{1,0:T(8,128)S(1)}, u32[]{:S(2)}, u32[]{:S(2)}) collective-permute-start(f32[256,768]{1,0:T(8,128)} %bitcast.235), channel_id=1, source_target_pairs={{0,2},{1,3},{2,4},{3,5},{4,6},{5,7},{8,10},{9,11},{10,12},{11,13},... | collective-permute-start | bytes 2359304 | tf_op jit(solution)/shard_map/ppermute | solution.py:332
  26.0 5.0 collective-permute-start.2
  29.7 19.2 %collective-permute-start.4 = (f32[256,768]{1,0:T(8,128)S(1)}, f32[256,768]{1,0:T(8,128)}, u32[]{:S(2)}, u32[]{:S(2)}) collective-permute-start(f32[256,768]{1,0:T(8,128)S(1)} %collective-permute-done), channel_id=1, source_target_pairs={{2,4},{3,5},{4,6},{5,7},{10,12},{11,13},{12,14},{13,15},{18,20},{1... | collective-permute-start | bytes 2359304 | tf_op jit(solution)/shard_map/ppermute | solution.py:332
  31.0 20.5 %collective-permute-start.3 = (f32[256,768]{1,0:T(8,128)S(1)}, f32[256,768]{1,0:T(8,128)}, u32[]{:S(2)}, u32[]{:S(2)}) collective-permute-start(f32[256,768]{1,0:T(8,128)S(1)} %collective-permute-done.2), channel_id=1, source_target_pairs={{2,0},{3,1},{10,8},{11,9},{18,16},{19,17},{26,24},{27,25}} | collective-permute-start | bytes 2359304 | tf_op jit(solution)/shard_map/ppermute | solution.py:332
  48.9 18.4 %collective-permute-start.5 = (f32[256,768]{1,0:T(8,128)}, f32[256,768]{1,0:T(8,128)}, u32[]{:S(2)}, u32[]{:S(2)}) collective-permute-start(f32[256,768]{1,0:T(8,128)} %collective-permute-done.4), channel_id=1, source_target_pairs={{4,6},{5,7},{12,14},{13,15},{20,22},{21,23},{28,30},{29,31}} | collective-permute-start | bytes 2359304 | tf_op jit(solution)/shard_map/ppermute | solution.py:332
  51.5 17.1 %copy-start.10 = (f32[1,256,768]{2,1,0:T(8,128)S(1)}, f32[1,256,768]{2,1,0:T(8,128)}, u32[]{:S(2)}) copy-start(f32[1,256,768]{2,1,0:T(8,128)} %param.22) | copy-start | bytes 2359300
  69.2 7.0 copy-start.37
  69.2 10.2 %copy-start.30 = (f32[64,256]{1,0:T(8,128)S(1)}, f32[64,256]{1,0:T(8,128)}, u32[]{:S(2)}) copy-start(f32[64,256]{1,0:T(8,128)} %param.25) | copy-start | bytes 196612
  72.4 28.7 %collective-permute-start.6 = (f32[4,256,768]{2,1,0:T(8,128)}, f32[4,256,768]{2,1,0:T(8,128)}, u32[]{:S(2)}, u32[]{:S(2)}) collective-permute-start(f32[4,256,768]{2,1,0:T(8,128)} %get-tuple-element.120), channel_id=1, source_target_pairs={{0,1},{1,0},{2,3},{3,2},{4,5},{5,4},{6,7},{7,6},{8,9},{9,8},{10,11... | collective-permute-start | bytes 9437192 | tf_op jit(solution)/shard_map/ppermute | solution.py:332
  76.2 9.0 collective-permute-start.8
  77.4 8.4 collective-permute-start.7
  85.2 2.0 collective-permute-start.9
  85.8 6.3 collective-permute-start.11
  87.2 6.2 collective-permute-start.10
  92.1 4.3 collective-permute-start.12
  96.5 4.0 collective-permute-start.13
  106.7 2.6 copy-start.39
  207.9 4.3 collective-permute-start.14
  208.0 6.6 copy-start.18
  214.6 1.8 copy-start.2
  222.5 6.5 collective-permute-start.15
  222.9 17.7 %collective-permute-start.16 = (f32[192,256]{1,0:T(8,128)S(1)}, f32[192,256]{1,0:T(8,128)S(1)}, u32[]{:S(2)}, u32[]{:S(2)}) collective-permute-start(f32[192,256]{1,0:T(8,128)S(1)} %bitcast.258), channel_id=1, source_target_pairs={{0,4},{1,5},{2,6},{3,7},{4,0},{5,1},{6,2},{7,3},{8,12},{9,13},{10,... | collective-permute-start | bytes 589832 | tf_op jit(solution)/shard_map/ppermute | solution.py:332
  223.2 17.4 %collective-permute-start.17 = (f32[192,256]{1,0:T(8,128)S(1)}, f32[192,256]{1,0:T(8,128)S(1)}, u32[]{:S(2)}, u32[]{:S(2)}) collective-permute-start(f32[192,256]{1,0:T(8,128)S(1)} %bitcast.257), channel_id=1, source_target_pairs={{0,6},{1,7},{2,0},{3,1},{4,2},{5,3},{6,4},{7,5},{8,14},{9,15},{10,... | collective-permute-start | bytes 589832 | tf_op jit(solution)/shard_map/ppermute | solution.py:332
  240.7 2.7 slice-start.5
  241.0 2.4 slice-start.6
  243.4 1.5 copy-start.26
  243.4 4.3 slice-start.3
  244.9 2.9 slice-start.4
  247.7 1.5 copy-start.21
  247.8 1.7 copy-start.19
  247.8 1.6 copy-start.38
  249.4 1.8 copy-start.3
  249.4 1.8 copy-start.31
  258.5 1.7 copy-start.40
  266.1 7.3 collective-permute-start.20
  266.7 15.8 %collective-permute-start.19 = (f32[192,256]{1,0:T(8,128)S(1)}, f32[192,256]{1,0:T(8,128)S(1)}, u32[]{:S(2)}, u32[]{:S(2)}) collective-permute-start(f32[192,256]{1,0:T(8,128)S(1)} %get-tuple-element.162), channel_id=1, source_target_pairs={{0,4},{1,5},{2,6},{3,7},{4,0},{5,1},{6,2},{7,3},{8,12},{9,13},{10,... | collective-permute-start | bytes 589832 | tf_op jit(solution)/shard_map/ppermute | solution.py:332
  268.7 13.8 %collective-permute-start.18 = (f32[192,256]{1,0:T(8,128)S(1)}, f32[192,256]{1,0:T(8,128)S(1)}, u32[]{:S(2)}, u32[]{:S(2)}) collective-permute-start(f32[192,256]{1,0:T(8,128)S(1)} %get-tuple-element.163), channel_id=1, source_target_pairs={{0,2},{1,3},{2,4},{3,5},{4,6},{5,7},{6,0},{7,1},{8,10},{9,11},{10,... | collective-permute-start | bytes 589832 | tf_op jit(solution)/shard_map/ppermute | solution.py:332
  282.8 3.3 collective-permute-start.21
  444.6 2.9 copy-start.15
  444.6 2.9 copy-start.17
  444.6 18.4 %collective-permute-start.22 = (f32[576,1024]{1,0:T(8,128)S(1)}, f32[576,1024]{1,0:T(8,128)S(1)}, u32[]{:S(2)}, u32[]{:S(2)}) collective-permute-start(f32[576,1024]{1,0:T(8,128)S(1)} %bitcast.238), channel_id=1, source_target_pairs={{0,1},{1,0},{2,3},{3,2},{4,5},{5,4},{6,7},{7,6},{8,9},{9,8},{10,11... | collective-permute-start | bytes 7077896 | tf_op jit(solution)/shard_map/ppermute | solution.py:332
  447.5 2.5 copy-start.13
  447.5 2.5 copy-start.20
  447.5 2.5 copy-start.22
  447.5 2.5 copy-start.29
  450.0 6.5 copy-start.24
  450.0 6.5 copy-start.27
  450.0 6.5 copy-start.41
  450.0 6.5 copy-start.43
  480.8 19.5 %collective-permute-start.28 = (f32[3,4,256]{2,1,0:T(4,128)}, f32[3,4,256]{2,1,0:T(4,128)}, u32[]{:S(2)}, u32[]{:S(2)}) collective-permute-start(f32[3,4,256]{2,1,0:T(4,128)} %get-tuple-element.179), channel_id=1, source_target_pairs={{0,6},{1,7},{2,0},{3,1},{4,2},{5,3},{6,4},{7,5},{8,14},{9,15},{10,... | collective-permute-start | bytes 36872 | tf_op jit(solution)/shard_map/ppermute | solution.py:332
  484.8 15.5 %collective-permute-start.27 = (f32[3,4,256]{2,1,0:T(4,128)}, f32[3,4,256]{2,1,0:T(4,128)}, u32[]{:S(2)}, u32[]{:S(2)}) collective-permute-start(f32[3,4,256]{2,1,0:T(4,128)} %get-tuple-element.180), channel_id=1, source_target_pairs={{0,4},{1,5},{2,6},{3,7},{4,0},{5,1},{6,2},{7,3},{8,12},{9,13},{10,... | collective-permute-start | bytes 36872 | tf_op jit(solution)/shard_map/ppermute | solution.py:332
  487.4 12.9 %collective-permute-start.26 = (f32[3,4,256]{2,1,0:T(4,128)}, f32[3,4,256]{2,1,0:T(4,128)}, u32[]{:S(2)}, u32[]{:S(2)}) collective-permute-start(f32[3,4,256]{2,1,0:T(4,128)} %get-tuple-element.181), channel_id=1, source_target_pairs={{0,2},{1,3},{2,4},{3,5},{4,6},{5,7},{6,0},{7,1},{8,10},{9,11},{10,... | collective-permute-start | bytes 36872 | tf_op jit(solution)/shard_map/ppermute | solution.py:332
  495.9 5.9 copy-start.25
  497.6 102.2 %collective-permute-start.23 = (f32[576,256]{1,0:T(8,128)}, f32[576,256]{1,0:T(8,128)S(1)}, u32[]{:S(2)}, u32[]{:S(2)}) collective-permute-start(f32[576,256]{1,0:T(8,128)} %bitcast.211), channel_id=1, source_target_pairs={{0,2},{1,3},{2,4},{3,5},{4,6},{5,7},{6,0},{7,1},{8,10},{9,11},{10,... | collective-permute-start | bytes 1769480 | tf_op jit(solution)/shard_map/ppermute | solution.py:332
  498.8 101.0 %collective-permute-start.24 = (f32[576,256]{1,0:T(8,128)}, f32[576,256]{1,0:T(8,128)S(1)}, u32[]{:S(2)}, u32[]{:S(2)}) collective-permute-start(f32[576,256]{1,0:T(8,128)} %bitcast.210), channel_id=1, source_target_pairs={{0,4},{1,5},{2,6},{3,7},{4,0},{5,1},{6,2},{7,3},{8,12},{9,13},{10,... | collective-permute-start | bytes 1769480 | tf_op jit(solution)/shard_map/ppermute | solution.py:332
  500.3 99.6 %collective-permute-start.25 = (f32[576,256]{1,0:T(8,128)S(1)}, f32[576,256]{1,0:T(8,128)S(1)}, u32[]{:S(2)}, u32[]{:S(2)}) collective-permute-start(f32[576,256]{1,0:T(8,128)S(1)} %bitcast.249), channel_id=1, source_target_pairs={{0,6},{1,7},{2,0},{3,1},{4,2},{5,3},{6,4},{7,5},{8,14},{9,15},{10,... | collective-permute-start | bytes 1769480 | tf_op jit(solution)/shard_map/ppermute | solution.py:332
  600.8 1.6 copy-start.8
  989.8 12.1 %slice-start = ((s8[9437184]{0:T(1024)(128)(4,1)}), s8[4194304]{0:T(1024)(128)(4,1)S(1)}, s32[]{:S(2)}) async-start(s8[9437184]{0:T(1024)(128)(4,1)} %bitcast.227), calls=%async_computation.1 | async-start | bytes 8388608
  993.1 8.8 slice-start.1
  993.1 8.8 slice-start.2
  1001.9 3.8 copy-start.1
  (17 other events, 20.1 us)
Sparse Core Ops, SparseCore 0:
  471.8 501.9 all-reduce.3

commit v2 on v1

v2 whole, which is shorter than its diff:
```python
import functools
import itertools
import math

import jax
import jax.numpy as jnp
from jax import lax
from jax.experimental import pallas as pl
from jax.experimental.pallas import tpu as pltpu
from jax.sharding import Mesh
from jax.sharding import PartitionSpec as P

MODEL_WIDTH = 768
HEAD_COUNT = 12
HEAD_SIZE = 64
HASH_COUNT = 32
HASH_BITS = 8
BUCKETS = 256
EXTRA = 32
CONV = 9
HALF = CONV // 2
ROWS = 80
CHUNK = 256
VMEM_BYTES = 32 * 1024 * 1024
BACK_VMEM = 24 * 1024 * 1024
OUTER_VMEM = 16 * 1024 * 1024
BACK_PARTS = 2

BF = jnp.bfloat16
F32 = jnp.float32


def split(x):
    hi = x.astype(BF)
    return hi, (x - hi.astype(F32)).astype(BF)


def parts_of(x):
    hi = lax.reduce_precision(x, 8, 7)
    return hi.astype(BF), (x - hi).astype(BF)


def dot(a, b):
    return jnp.dot(a, b, preferred_element_type=F32)


def dot3(a, b):
    ah, al = split(a)
    bh, bl = split(b)
    return dot(ah, bh) + dot(ah, bl) + dot(al, bh)


def contract(a, b, i, j):
    return lax.dot_general(a, b, (((i,), (j,)), ((), ())), preferred_element_type=F32)


def by_weight(x, w, i, j):
    hi, lo = parts_of(x)
    return contract(hi, w, i, j) + contract(lo, w, i, j)


def outer_sum(a, b):
    ah, al = parts_of(a)
    bh, bl = parts_of(b)
    return contract(
        jnp.concatenate([ah, al, ah], axis=0), jnp.concatenate([bh, bh, bl], axis=0), 0, 0
    )


def factors(s8):
    w = s8.shape[1]
    r = lax.broadcasted_iota(jnp.int32, (8, w), 0)
    rows = [jnp.broadcast_to(s8[j : j + 1], (8, w)) for j in range(8)]
    low = [jnp.where((r & m) != 0, rows[j], 1.0) for j, m in ((5, 4), (6, 2), (7, 1))]
    return r, rows, low


def monomials(rows, low):
    out = [low[0] * low[1] * low[2]]
    for j in (4, 3, 2, 1, 0):
        out = out + [rows[j] * x for x in out]
    return out


def row_sums(r, parts):
    step = 1
    while len(parts) > 1:
        bit = (r & step) != 0
        parts = [
            jnp.where(bit, b, a) + pltpu.roll(jnp.where(bit, a, b), step, 0)
            for a, b in zip(parts[0::2], parts[1::2])
        ]
        step *= 2
    return parts[0]


def sign_grad(r, rows, low, phi, d):
    c = [d[8 * v : 8 * v + 8] for v in range(32)]
    parts = []
    for j in range(5):
        half = len(c) // 2
        acc = phi[0] * c[half]
        for n in range(1, half):
            acc = acc + phi[n] * c[half + n]
        parts.append(acc)
        c = [c[n] + rows[j] * c[half + n] for n in range(half)]
    m = c[0]
    zero = jnp.zeros_like(m)
    parts.append(jnp.where((r & 4) != 0, m * low[1] * low[2], zero))
    parts.append(jnp.where((r & 2) != 0, m * low[0] * low[2], zero))
    parts.append(jnp.where((r & 1) != 0, m * low[0] * low[1], zero))
    return row_sums(r, parts)


def norm_scale(u):
    return lax.rsqrt(jnp.mean(u * u, axis=0, keepdims=True) + 1e-06)


def signs_of(u, proj):
    return jnp.tanh(2.0 * dot3(proj, u * (norm_scale(u) * 0.125)))


def columns(rows64, row):
    t = jnp.concatenate([rows64, row, jnp.zeros((63, row.shape[1]), F32)], axis=0).T
    return jnp.concatenate(split(t), axis=1)


def stacked(rows64, row):
    width = row.shape[1]
    hi, lo = split(jnp.concatenate([rows64, row, jnp.zeros((15, width), F32)], axis=0))
    return jnp.concatenate([hi, hi, lo, jnp.zeros((16, width), BF)], axis=0)


def beside(tab):
    hi = tab.astype(BF).astype(F32)
    lo = pltpu.roll(tab - hi, ROWS, 1)
    again = pltpu.roll(hi, 2 * ROWS - 128, 1)
    lane = lax.broadcasted_iota(jnp.int32, tab.shape, 1)
    return jnp.concatenate(
        [jnp.where(lane < ROWS, hi, lo), jnp.where(lane < 2 * ROWS - 128, lo, again)], axis=1
    ).astype(BF)


def halves(tab):
    return jnp.concatenate(split(tab.T[:ROWS]), axis=0)


def shifted(x, offset):
    if offset == 0:
        return x
    width = x.shape[1]
    t = lax.broadcasted_iota(jnp.int32, x.shape, 1) + offset
    return jnp.where((t >= 0) & (t < width), pltpu.roll(x, (-offset) % width, 1), 0.0)


def reorder(x, outer, inner, block):
    return jnp.concatenate(
        [
            x[:, (o * inner + i) * block : (o * inner + i + 1) * block]
            for i in range(inner)
            for o in range(outer)
        ],
        axis=1,
    )


def fill_kernel(k_ref, v_ref, valid_ref, proj_ref, *refs):
    tab_ref, sk, cols = refs[-3:]
    hashes, width = tab_ref.shape[1], k_ref.shape[2]
    part = pl.program_id(1)

    @pl.when(part == 0)
    def _():
        sk[...] = signs_of(k_ref[0], proj_ref[...])
        cols[...] = columns(v_ref[0], valid_ref[...])

    for g in range(hashes):
        base = pl.multiple_of((part * hashes + g) * 8, 8)
        acc = None
        for c in range(0, width, CHUNK):
            _, rows, low = factors(sk[pl.ds(base, 8), c : c + CHUNK])
            hi, lo = split(jnp.concatenate(monomials(rows, low), axis=0))
            value = cols[c : c + CHUNK, :]
            p = dot(hi, value) + dot(lo, value)
            acc = p if acc is None else acc + p
        tab = acc[:, :128] + acc[:, 128:]
        if len(refs) > 3:
            tab = tab + refs[0][0, g]
        tab_ref[0, g] = tab


def read_kernel(
    hashes, groups, inner, q_ref, v_ref, tab_ref, proj_ref, taps_ref, num_ref, conv_ref, cnt_ref, sq,
):
    head = pl.program_id(0)
    width = q_ref.shape[2]
    block = width // (groups * inner)
    sq[...] = signs_of(q_ref[0], proj_ref[...])
    num_ref[0] = jnp.zeros(num_ref.shape[1:], F32)
    natural = reorder(v_ref[0], inner, groups, block)
    conv = jnp.zeros(natural.shape, F32)
    for j in range(CONV):
        conv = conv + shifted(natural, j - HALF) * taps_ref[head, j]
    conv_ref[0] = reorder(conv, groups, inner, block)

    @pl.loop(0, hashes)
    def _(g):
        base = pl.multiple_of(g * 8, 8)
        flat = (tab_ref[0, g] * (1.0 / BUCKETS)).T[:ROWS]
        cnt_ref[0, pl.ds(g, 1), :] = flat[64:65]
        ext = jnp.concatenate(split(flat), axis=0)
        for c in range(0, width, CHUNK):
            _, rows, low = factors(sq[pl.ds(base, 8), c : c + CHUNK])
            hi, lo = split(jnp.concatenate(monomials(rows, low), axis=0))
            p = dot(ext, hi)
            num_ref[0, :, c : c + CHUNK] += p[:ROWS] + p[ROWS:] + dot(ext[:ROWS], lo)


def bwd_kernel(
    hashes, groups, inner, with_conv, q_ref, k_ref, v_ref, valid_ref, proj_ref, num_ref, da_ref, tab_ref, taps_ref,
    dq_ref, dk_ref, dv_ref, dt_ref, sq, sk, gq, gk, cols, xq, xk, dv,
):
    width = q_ref.shape[2]
    block = width // (groups * inner)
    sq[...] = signs_of(q_ref[0], proj_ref[...])
    sk[...] = signs_of(k_ref[0], proj_ref[...])
    da = da_ref[0]
    v = v_ref[0]
    inv = 1.0 / (num_ref[0, 64:65, :] + HASH_COUNT)
    dn = da * inv
    dd = -jnp.sum(dn * num_ref[0, :64, :], axis=0, keepdims=True) * inv
    cols[...] = columns(dn, dd)
    xq[...] = stacked(dn, dd)
    xk[...] = stacked(v, valid_ref[...])
    dv[...] = jnp.zeros(dv.shape, F32)

    @pl.loop(0, hashes)
    def _(g):
        base = pl.multiple_of(g * 8, 8)
        tabs = beside(tab_ref[0, g] * (1.0 / BUCKETS))
        acc = None
        for c in range(0, width, CHUNK):
            s8 = sq[pl.ds(base, 8), c : c + CHUNK]
            r, rows, low = factors(s8)
            phi = monomials(rows, low)
            hi, lo = split(jnp.concatenate(phi, axis=0))
            value = cols[c : c + CHUNK, :]
            p = dot(hi, value) + dot(lo, value)
            acc = p if acc is None else acc + p
            d = dot(tabs, xq[:, c : c + CHUNK])
            gq[pl.ds(base, 8), c : c + CHUNK] = sign_grad(r, rows, low, phi, d) * (2.0 - 2.0 * s8 * s8)
        tab = (acc[:, :128] + acc[:, 128:]) * (1.0 / BUCKETS)
        ext = halves(tab)
        tabs = beside(tab)
        for c in range(0, width, CHUNK):
            s8 = sk[pl.ds(base, 8), c : c + CHUNK]
            r, rows, low = factors(s8)
            phi = monomials(rows, low)
            hi, lo = split(jnp.concatenate(phi, axis=0))
            p = dot(ext, hi)
            dv[:, c : c + CHUNK] += p[:ROWS] + p[ROWS:] + dot(ext[:ROWS], lo)
            d = dot(tabs, xk[:, c : c + CHUNK])
            gk[pl.ds(base, 8), c : c + CHUNK] = sign_grad(r, rows, low, phi, d) * (2.0 - 2.0 * s8 * s8)

    back = proj_ref[...].T
    for u_ref, g_ref, o_ref in ((q_ref, gq, dq_ref), (k_ref, gk, dk_ref)):
        u = u_ref[0]
        scale = norm_scale(u)
        g = dot3(back, g_ref[...])
        inside = g - u * (scale * scale * jnp.mean(g * u, axis=0, keepdims=True))
        o_ref[0] = (scale * 0.125) * inside
    total = dv[:64, :]
    if with_conv:
        natural = reorder(v, inner, groups, block)
        grad = reorder(da, inner, groups, block)
        conv = jnp.zeros(natural.shape, F32)
        for j in range(CONV):
            conv = conv + shifted(grad, HALF - j) * taps_ref[0, j]
            moved = grad * shifted(natural, j - HALF)
            dt_ref[j : j + 1, :] = jnp.sum(moved, axis=0, keepdims=True)
        total = total + reorder(conv, groups, inner, block)
    dv_ref[0] = total * valid_ref[...]


def one(*shape, at=0):
    return pl.BlockSpec((1,) + shape, lambda h: (h + at,) + (0,) * len(shape))


def same(*shape):
    return pl.BlockSpec(shape, lambda h: (0,) * len(shape))


SMEM = pl.BlockSpec(memory_space=pltpu.SMEM)


def fill(qkv, valid, proj, tab):
    heads, width = qkv.shape[0] // 3, qkv.shape[2]
    hashes = proj.shape[0] // 8
    parts = 4
    ins = [qkv, qkv, valid, proj] + [tab] * (tab is not None)

    def rows(at):
        return pl.BlockSpec((1, 64, width), lambda h, p: (h + at, 0, 0))

    table = pl.BlockSpec((1, hashes // parts, BUCKETS, 128), lambda h, p: (h, p, 0, 0))
    specs = [
        rows(heads), rows(2 * heads), pl.BlockSpec((1, width), lambda h, p: (0, 0)),
        pl.BlockSpec(proj.shape, lambda h, p: (0, 0)), table,
    ]
    return pl.pallas_call(
        fill_kernel,
        grid=(heads, parts),
        in_specs=specs[: len(ins)],
        out_specs=table,
        out_shape=jax.ShapeDtypeStruct((heads, hashes, BUCKETS, 128), F32),
        scratch_shapes=[pltpu.VMEM((hashes * 8, width), F32), pltpu.VMEM((width, 256), BF)],
        compiler_params=pltpu.CompilerParams(vmem_limit_bytes=OUTER_VMEM),
        cost_estimate=pl.CostEstimate(flops=0, bytes_accessed=0, transcendentals=0),
        name="fill",
    )(*ins)


def read(qkv, tab, proj, taps, groups, inner):
    heads, width = qkv.shape[0] // 3, qkv.shape[2]
    hashes = proj.shape[0] // 8
    return pl.pallas_call(
        functools.partial(read_kernel, hashes, groups, inner),
        grid=(heads,),
        in_specs=[
            one(64, width), one(64, width, at=2 * heads), one(hashes, BUCKETS, 128), same(*proj.shape), SMEM,
        ],
        out_specs=[one(ROWS, width), one(64, width), one(hashes, BUCKETS)],
        out_shape=[
            jax.ShapeDtypeStruct((heads, ROWS, width), F32),
            jax.ShapeDtypeStruct((heads, 64, width), F32),
            jax.ShapeDtypeStruct((heads, hashes, BUCKETS), F32),
        ],
        scratch_shapes=[pltpu.VMEM((hashes * 8, width), F32)],
        compiler_params=pltpu.CompilerParams(vmem_limit_bytes=VMEM_BYTES),
        cost_estimate=pl.CostEstimate(flops=0, bytes_accessed=0, transcendentals=0),
        name="read",
    )(qkv, qkv, tab, proj, taps)


def attend_back(head, part, parts, qkv, valid, proj, num, d_attn, tab, taps, groups, inner):
    heads, width = qkv.shape[0] // 3, qkv.shape[2]
    hashes = proj.shape[0] // 8 // parts

    def pick(*shape, at):
        return pl.BlockSpec((1,) + shape, lambda _: (at,) + (0,) * len(shape))

    return pl.pallas_call(
        functools.partial(bwd_kernel, hashes, groups, inner, part == 0),
        grid=(1,),
        in_specs=[
            pick(64, width, at=head), pick(64, width, at=heads + head), pick(64, width, at=2 * heads + head),
            same(1, width), pl.BlockSpec((hashes * 8, 64), lambda _: (part, 0)),
            pick(ROWS, width, at=head), pick(64, width, at=head),
            pl.BlockSpec((1, hashes, BUCKETS, 128), lambda _: (head, part, 0, 0)), SMEM,
        ],
        out_specs=[pick(64, width, at=0)] * 3 + [same(16, width)],
        out_shape=[jax.ShapeDtypeStruct((1, 64, width), F32)] * 3
        + [jax.ShapeDtypeStruct((16, width), F32)],
        scratch_shapes=[pltpu.VMEM((hashes * 8, width), F32)] * 4
        + [pltpu.VMEM((width, 256), BF)]
        + [pltpu.VMEM((256, width), BF)] * 2
        + [pltpu.VMEM((ROWS, width), F32)],
        compiler_params=pltpu.CompilerParams(vmem_limit_bytes=BACK_VMEM),
        cost_estimate=pl.CostEstimate(flops=0, bytes_accessed=0, transcendentals=0),
        name="attend_back",
    )(qkv, qkv, qkv, valid, proj, num, d_attn, tab, taps)


def copy_kernel(x_ref, o_ref):
    o_ref[...] = x_ref[...]


def widened(x, columns):
    size = MODEL_WIDTH
    return pl.pallas_call(
        copy_kernel,
        grid=(columns // size, 2),
        in_specs=[pl.BlockSpec((size // 2, size), lambda j, i: (j * 2 + i, 0))],
        out_specs=pl.BlockSpec((size // 2, size), lambda j, i: (i, j)),
        out_shape=jax.ShapeDtypeStruct((size, columns), x.dtype),
        compiler_params=pltpu.CompilerParams(vmem_limit_bytes=OUTER_VMEM),
        cost_estimate=pl.CostEstimate(flops=0, bytes_accessed=0, transcendentals=0),
        name="widened",
    )(x)


def rejoin_kernel(c_ref, *refs):
    count = len(refs) - 3
    rows = refs[-1].shape[0]
    for s in range(count):

        @pl.when(pl.program_id(0) == s)
        def _():
            for i in range(3):
                refs[count + i][...] = refs[s][i, :rows]


def rejoined(parts, rows, c):
    count, columns = len(parts), parts[0].shape[2]
    out = pl.BlockSpec((rows, columns), lambda s, c_ref: (lax.rem(c_ref[0] + count - s, count), 0))
    return pl.pallas_call(
        rejoin_kernel,
        grid_spec=pltpu.PrefetchScalarGridSpec(
            num_scalar_prefetch=1,
            grid=(count,),
            in_specs=[pl.BlockSpec(t.shape, lambda *_: (0, 0, 0)) for t in parts],
            out_specs=[out] * 3,
        ),
        out_shape=[jax.ShapeDtypeStruct((count * rows, columns), F32)] * 3,
        compiler_params=pltpu.CompilerParams(vmem_limit_bytes=VMEM_BYTES),
        cost_estimate=pl.CostEstimate(flops=0, bytes_accessed=0, transcendentals=0),
        name="rejoined",
    )(c.reshape(1), *parts)


def copied(x):
    rows, columns = x.shape
    block = rows // 8
    spec = pl.BlockSpec((block, columns), lambda i: (i, 0))
    return pl.pallas_call(
        copy_kernel,
        grid=(8,),
        in_specs=[spec],
        out_specs=spec,
        out_shape=jax.ShapeDtypeStruct(x.shape, x.dtype),
        compiler_params=pltpu.CompilerParams(vmem_limit_bytes=OUTER_VMEM),
        cost_estimate=pl.CostEstimate(flops=0, bytes_accessed=0, transcendentals=0),
        name="copied",
    )(x)


def outer_kernel(inner, c_ref, a_ref, b_ref, *refs):
    *out_refs, whole = refs
    items, rows = out_refs[0].shape[:2]
    ah, al = split(a_ref[...])
    bh, bl = split(b_ref[...])
    dims = (((0,), (0,)), ((), ()))
    whole[...] = (
        lax.dot_general(ah, bh, dims, preferred_element_type=F32)
        + lax.dot_general(al, bh, dims, preferred_element_type=F32)
        + lax.dot_general(ah, bl, dims, preferred_element_type=F32)
    )
    for s, out_ref in enumerate(out_refs):
        start = lax.rem(c_ref[0] + s, inner) * rows
        for i in range(items):
            out_ref[i] = whole[pl.ds(pl.multiple_of(i * inner * rows + start, 8), rows), :]


def outer_blocks(a, b, items, inner, c):
    tokens, wide = a.shape
    block, columns = wide // items, b.shape[1]
    each = 1 if block % 128 == 0 else items
    width = min(columns, MODEL_WIDTH)
    return pl.pallas_call(
        functools.partial(outer_kernel, inner),
        grid=(items // each, columns // width),
        in_specs=[
            SMEM,
            pl.BlockSpec((tokens, each * block), lambda i, j: (0, i)),
            pl.BlockSpec((tokens, width), lambda i, j: (0, j)),
        ],
        out_specs=[pl.BlockSpec((each, block // inner, width), lambda i, j: (i, 0, j))] * inner,
        out_shape=[jax.ShapeDtypeStruct((items, block // inner, columns), F32)] * inner,
        scratch_shapes=[pltpu.VMEM((each * block, width), F32)],
        compiler_params=pltpu.CompilerParams(vmem_limit_bytes=OUTER_VMEM),
        cost_estimate=pl.CostEstimate(flops=0, bytes_accessed=0, transcendentals=0),
        name="outer_blocks",
    )(c.reshape(1), a, b)


def rows_kernel(
    inner, c_ref, first_ref, hidden_ref, attn_ref, pre_ref, second_ref, d_first_ref, n1_ref, n2_ref, grad_ref, *out_refs
):
    s, item, k = (pl.program_id(i) for i in range(3))
    block = (item * inner + lax.rem(c_ref[0] + s, inner)) * pl.num_programs(2) + k
    size = out_refs[0].shape[0]
    each = MODEL_WIDTH // size
    ups = hidden_ref.shape[1] // MODEL_WIDTH * each

    def product(a, b, dims):
        ah, al = split(a)
        bh, bl = split(b)
        return sum(
            lax.dot_general(x, y, (dims, ((), ())), preferred_element_type=F32)
            for x, y in ((ah, bh), (al, bh), (ah, bl))
        )

    def put(value):
        for i, out_ref in enumerate(out_refs):

            @pl.when(s == i)
            def _():
                out_ref[...] = value

    @pl.when(block < ups)
    def _():
        at = pl.multiple_of(lax.rem(block, each) * size, size)
        to = pl.multiple_of(lax.div(block, each) * MODEL_WIDTH, MODEL_WIDTH)
        put(product(first_ref[:, pl.ds(at, size)], hidden_ref[:, pl.ds(to, MODEL_WIDTH)], ((0,), (0,))))

    @pl.when((block >= ups) & (block < ups + each))
    def _():
        at = pl.multiple_of((block - ups) * size, size)
        put(product(attn_ref[pl.ds(at, size), :], pre_ref[...], ((1,), (0,))))

    @pl.when(block == ups + each)
    def _():
        def down(t):
            return jnp.sum(t, axis=0, keepdims=True)

        rows = [
            down(pre_ref[...]), down(d_first_ref[...] * n1_ref[...]), down(d_first_ref[...]), down(second_ref[...]),
            down(grad_ref[...] * n2_ref[...]), down(grad_ref[...]),
        ]
        wide = hidden_ref.shape[1]
        rows += [down(hidden_ref[:, j : j + MODEL_WIDTH]) for j in range(0, wide, MODEL_WIDTH)]
        rows.append(jnp.zeros((size - len(rows), MODEL_WIDTH), F32))
        put(jnp.concatenate(rows))

    @pl.when(block > ups + each)
    def _():
        put(jnp.zeros((size, MODEL_WIDTH), F32))


def outer_rows(first, d_hidden, attn_t, d_pre, others, items, inner, c):
    rows = (d_hidden.shape[1] + MODEL_WIDTH + 256) // (items * inner)
    size = 256 if rows % 256 == 0 else 128
    blocks = rows // size

    def place(i):
        last = items * blocks - 1

        def index(s, item, k, _):
            at = item * blocks + k
            return jnp.where(s == i, at, jnp.where(s > i, last, 0)), 0

        return pl.BlockSpec((size, MODEL_WIDTH), index)

    ins = [first, d_hidden, attn_t, d_pre, *others]
    shape = jax.ShapeDtypeStruct((items * rows, MODEL_WIDTH), F32)
    parts = pl.pallas_call(
        functools.partial(rows_kernel, inner),
        grid_spec=pltpu.PrefetchScalarGridSpec(
            num_scalar_prefetch=1,
            grid=(inner, items, blocks),
            in_specs=[pl.BlockSpec(t.shape, lambda *_: (0, 0)) for t in ins],
            out_specs=[place(i) for i in range(inner)],
        ),
        out_shape=[shape] * inner,
        compiler_params=pltpu.CompilerParams(vmem_limit_bytes=VMEM_BYTES),
        cost_estimate=pl.CostEstimate(flops=0, bytes_accessed=0, transcendentals=0),
        name="outer_rows",
    )(c.reshape(1), *ins)
    return [t.reshape(items, -1, MODEL_WIDTH) for t in parts]


AXES = ("item", "z", "core")
ITEM, Z, C = range(3)


class Grid:
    def __init__(self, sizes):
        self.sizes = sizes
        self.place = tuple(lax.axis_index(name) for name in AXES)
        self.found = []

    def send(self, x, axis, target):
        sizes = self.sizes
        pairs = []
        for source in itertools.product(*(range(n) for n in sizes)):
            to = target(source[axis])
            if to is None:
                continue
            there = source[:axis] + (to,) + source[axis + 1 :]
            flat = [functools.reduce(lambda t, ni: t * ni[0] + ni[1], zip(sizes, p), 0) for p in (source, there)]
            pairs.append(tuple(flat))
        return lax.ppermute(x, AXES, pairs)

    def ordered(self, parts, axis):
        count, own = len(parts), self.place[axis]
        if count == 1:
            return parts
        if count == 2:
            swap = own == 1
            return [jnp.where(swap, parts[1], parts[0]), jnp.where(swap, parts[0], parts[1])]
        whole = jnp.stack(parts)
        return [lax.dynamic_index_in_dim(whole, (own - s) % count, 0, keepdims=False) for s in range(count)]

    def offer(self, x, axis):
        count = self.sizes[axis]
        return [x] + [self.send(x, axis, lambda i: (i + s) % count) for s in range(1, count)]

    def collect(self, parts, axis, dim=None):
        parts = self.ordered(parts, axis)
        return parts if dim is None else jnp.concatenate(parts, axis=dim)

    def spread(self, x, axis):
        return jnp.stack(self.collect(self.offer(x, axis), axis))

    def deal(self, x, axis, dim=0):
        count, own = self.sizes[axis], self.place[axis]
        size = x.shape[dim] // count
        parts = [x]
        for s in range(1, count):
            block = lax.dynamic_slice_in_dim(x, (own + s) % count * size, size, dim)
            parts.append(self.send(block, axis, lambda i: (i + s) % count))
        return parts

    def own_block(self, x, axis, dim):
        size = x.shape[dim] // self.sizes[axis]
        return lax.dynamic_slice_in_dim(x, self.place[axis] * size, size, dim)

    def add(self, parts, axis, dim=0):
        total = self.own_block(parts[0], axis, dim)
        for part in parts[1:]:
            total = total + part
        return total

    def take(self, parts, axis, dim=0):
        return self.ordered([self.own_block(parts[0], axis, dim)] + parts[1:], axis)

    def arrivals(self, axis):
        count = self.sizes[axis]
        return [
            sorted((s, d) for s in range(1, count) for d in (-1, 1) if 0 <= i + d * s < count) for i in range(count)
        ]

    def step_on(self, up, down, axis, step):
        count = self.sizes[axis]
        up = self.send(up, axis, lambda i: i + 1 if step - 1 <= i < count - 1 else None)
        down = self.send(down, axis, lambda i: i - 1 if 0 < i <= count - step else None)
        return up, down

    def arrived(self, came, axis, k):
        own, result = self.place[axis], None
        for i, moves in enumerate(self.arrivals(axis)):
            step, way = moves[k - 1]
            candidate = came[step][(way + 1) // 2]
            result = candidate if result is None else jnp.where(own == i, candidate, result)
        return result

    def places(self, axis):
        count, own = self.sizes[axis], self.place[axis]
        j = lax.iota(jnp.int32, count)
        s = jnp.abs(j - own)
        before = jnp.minimum(s - 1, own) + jnp.minimum(s - 1, count - 1 - own)
        both = ((j > own) & (own >= s)).astype(jnp.int32)
        places = jnp.where(j == own, 0, before + both + 1)
        return [places[i] for i in range(count)]

    def by_index(self, parts, places):
        whole = jnp.stack(parts)
        return [lax.dynamic_index_in_dim(whole, place, 0, keepdims=False) for place in places]


    def dealing(self, x, axis, dim=0):
        count, own = self.sizes[axis], self.place[axis]
        size = x.shape[dim] // count
        blocks = [lax.dynamic_slice_in_dim(x, (own + s) % count * size, size, dim) for s in range(count)]
        return (yield from self.moving(axis, blocks))

    def moving(self, axis, blocks):
        yield axis, blocks
        return (yield)

    def applying(self, function, x):
        yield function, [x]
        return (yield)

    def move(self, axis, blocks_of):
        count = self.sizes[axis]
        result = [[blocks[0]] for blocks in blocks_of]
        for s in range(1, count):
            out = [blocks[s] if len(blocks) > 1 else blocks[0] for blocks in blocks_of]
            if len(out) == 1:
                result[0].append(self.send(out[0], axis, lambda i: (i + s) % count))
                continue
            lane = functools.reduce(math.gcd, (t.shape[1] for t in out))
            lanes = [[t[:, k : k + lane] for k in range(0, t.shape[1], lane)] for t in out]
            whole = self.send(jnp.concatenate(sum(lanes, [])), axis, lambda i: (i + s) % count)
            row = 0
            for t, into in zip(out, result):
                rows, wide = t.shape[0], t.shape[1] // lane
                pieces = [whole[row + k * rows : row + (k + 1) * rows] for k in range(wide)]
                into.append(jnp.concatenate(pieces, axis=1))
                row += rows * wide
        return result

    def reduce(self, blocks):
        blocks = yield blocks
        x = sum((yield from self.moving(C, blocks)))
        scatter = functools.partial(lax.psum_scatter, axis_name="item", scatter_dimension=0, tiled=True)
        x = (yield from self.applying(scatter, x))[0][0]
        x = sum((yield from self.dealing(x, Z)))
        x = self.collect((yield from self.moving(Z, [x])), Z, 0)
        gather = functools.partial(lax.all_gather, axis_name=("item", "core"), axis=0, tiled=True)
        return (yield from self.applying(gather, x))

    def head(self, d_parts, x_parts):
        d_parts = yield d_parts
        d_part = jnp.concatenate([sum(parts) for parts in zip(*d_parts)])
        full = sum(self.collect((yield from self.moving(C, [d_part])), C))
        dh, dl = parts_of(full)
        xh, xl = x_parts
        d_w = contract(xh, dh, 0, 1) + contract(xl, dh, 0, 1) + contract(xh, dl, 0, 1)
        d_b = jnp.sum(full, axis=1)
        self.found.append((d_w, d_b, self.own_block(full, C, 1)))

    def home(self, mine):
        mine = yield mine
        return (yield from self.dealing(mine, Z, 1))

    def tail(self, d_w):
        d_w = yield d_w
        feats = d_w.shape[1] // 3
        x = sum((yield from self.dealing(d_w, ITEM)))
        x = self.collect((yield from self.moving(Z, [x])), Z)
        x = [jnp.concatenate([t[:, i * feats : (i + 1) * feats] for t in x], axis=1) for i in range(3)]
        x = yield from self.moving(ITEM, [jnp.stack(x)])
        return (yield from self.moving(C, [self.collect(x, ITEM, 1)]))


class Steps:
    def __init__(self, grid):
        self.grid, self.live, self.state, self.done = grid, {}, {}, {}

    def add(self, name, sequence):
        self.live[name], self.state[name] = sequence, next(sequence)

    def advance(self, states):
        ready = {}
        for name, state in states.items():
            try:
                ready[name] = self.live[name].send(state)
            except StopIteration as end:
                self.done[name] = end.value
                del self.live[name], self.state[name]
        return {name: how for name, (how, _) in ready.items()}, {name: blocks for name, (_, blocks) in ready.items()}

    def carry(self, hows, blocks):
        came = {}
        for axis in (C, Z, ITEM):
            names = [name for name, how in hows.items() if how == axis]
            alike = [name for name in names if axis == Z and blocks[name][0].shape[1] % 128 == 0 and name != "up"]
            groups = [alike] * bool(alike) + [[name] for name in names if name not in alike]
            for group in groups:
                came.update(zip(group, self.grid.move(axis, [blocks[name] for name in group])))
        for name, how in hows.items():
            if callable(how):
                came[name] = how(blocks[name][0])
                came[name] = [came[name]] if how.func is lax.psum_scatter else came[name]
            next(self.live[name])
            self.state[name] = came[name]

    def start(self, name):
        self.carry(*self.advance({name: self.state[name]}))

    def stage(self, names, held=(), beside=()):
        names = [name for name in names if name in self.live]
        states, held = lax.optimization_barrier(({name: self.state[name] for name in names}, held))
        hows, blocks = self.advance(states)
        blocks, beside = lax.optimization_barrier((blocks, beside))
        self.carry(hows, blocks)
        return held, beside


def normalize(x):
    centered = x - jnp.mean(x, axis=-1, keepdims=True)
    scale = lax.rsqrt(jnp.mean(centered * centered, axis=-1, keepdims=True) + 1e-05)
    return centered * scale, scale


def normalize_back(grad, normed, scale):
    mean = jnp.mean(grad, axis=-1, keepdims=True)
    along = jnp.mean(grad * normed, axis=-1, keepdims=True)
    return scale * (grad - mean - normed * along)


def dense(x, attn_t, out_grad, w_out, b_out, gain_one, bias_one, w_up, b_up, w_down, b_down, gain_two, bias_two):
    n1, scale1 = normalize(x + by_weight(attn_t, w_out, 0, 0) + b_out)
    first = n1 * gain_one + bias_one
    hidden = by_weight(first, w_up, 1, 0) + b_up
    cdf = 0.5 + 0.5 * lax.erf(hidden * math.sqrt(0.5))
    inner = hidden * cdf
    n2, scale2 = normalize(first + by_weight(inner, w_down, 1, 0) + b_down)
    output = n2 * gain_two + bias_two
    d_second = normalize_back(out_grad * gain_two, n2, scale2)
    slope = cdf + hidden * (jnp.exp(-0.5 * hidden * hidden) * (1.0 / math.sqrt(2.0 * math.pi)))
    d_hidden = by_weight(d_second, w_down, 1, 1) * slope
    d_first = d_second + by_weight(d_hidden, w_up, 1, 1)
    d_pre = normalize_back(d_first * gain_one, n1, scale1)
    d_hi, d_lo = parts_of(d_pre)
    d_attn_t = contract(w_out, d_hi, 1, 1) + contract(w_out, d_lo, 1, 1)
    return output, d_attn_t, (d_second, first, d_hidden, attn_t, d_pre, d_first, n1, n2, out_grad, inner)


def hadamard():
    index = lax.iota(jnp.int32, BUCKETS)
    both = lax.population_count(index[:, None] & index[None, :])
    return jnp.where((both & 1) == 0, 1.0, -1.0).astype(BF)


def per_device(
    sizes, inputs, lengths, pad_mask, hash_proj, w_query, b_query, w_key, b_key, w_value, b_value, conv_taps,
    w_out, b_out, gain_one, bias_one, w_up, b_up, w_down, b_down, gain_two, bias_two, out_grad,
):
    grid = Grid(sizes)
    items, groups, inner = sizes
    count = groups * inner
    _, z, c = grid.place
    heads = HEAD_COUNT // groups
    feats = heads * HEAD_SIZE
    own_hashes = HASH_COUNT // count
    hashes = own_hashes * groups
    tokens = inputs.shape[1]
    width = count * tokens
    x = inputs[0]

    position = (z * inner + c) * tokens + lax.iota(jnp.int32, tokens)
    valid = ((position < lengths[0]) & (pad_mask[0] == 1)).astype(F32)
    mask_rows = jnp.pad(valid.reshape(1, tokens), ((0, 7), (0, MODEL_WIDTH - tokens)))

    def head_columns(w):
        return lax.dynamic_slice_in_dim(w, z * feats, feats, axis=w.ndim - 1)

    w_qkv = jnp.concatenate([head_columns(w) for w in (w_query, w_key, w_value)], axis=1)
    b_qkv = jnp.concatenate([head_columns(b) for b in (b_query, b_key, b_value)])

    is_value = lax.iota(jnp.int32, 3 * feats)[:, None] >= 2 * feats

    def project(rows):
        hi, lo = parts_of(rows[:tokens])
        here = rows[tokens : tokens + 1, :tokens]
        products = contract(w_qkv, hi, 0, 1) + contract(w_qkv, lo, 0, 1) + b_qkv[:, None]
        products = jnp.where(is_value, products * here, products)
        products = jnp.concatenate([products, jnp.broadcast_to(here, (8, tokens))])
        return grid.collect(grid.offer(products, C), C, 1)

    proj = lax.dynamic_index_in_dim(
        hash_proj.reshape(HEAD_SIZE, groups, inner, own_hashes * HASH_BITS), c, 2, keepdims=False
    )
    proj = proj.reshape(HEAD_SIZE, hashes * HASH_BITS).T
    taps = lax.dynamic_slice_in_dim(conv_taps, z * heads, heads, axis=0)
    up = down = jnp.concatenate([x, mask_rows])
    came, lines, chunks, tab = [(up, down)], [up], [], None
    places = grid.places(Z)
    for k in range(groups):
        if k:
            up, down, tab, chunks, places = lax.optimization_barrier((up, down, tab, chunks, places))
            came.append((up, down))
            lines.append(grid.arrived(came, Z, k))
        if k < groups - 1:
            up, down = grid.step_on(up, down, Z, k + 1)
        chunk = project(lines[-1])
        chunks.append(chunk)
        per_head = chunk[: 3 * feats].reshape(3 * heads, HEAD_SIZE, -1)
        tab = fill(per_head, chunk[3 * feats : 3 * feats + 1], proj, tab)
    chunks = grid.by_index(chunks, places)
    chunks = jnp.concatenate(
        [t[:, i * tokens : (i + 1) * tokens] for i in range(inner) for t in chunks], axis=1
    )
    qkv, valid = chunks[: 3 * feats].reshape(3 * heads, HEAD_SIZE, width), chunks[3 * feats : 3 * feats + 1]

    num_part, conv, subsets = read(qkv, tab, proj, taps, groups, inner)
    num, step = num_part, 1
    while step < inner:
        num = num + grid.send(num, C, lambda i: i ^ step)
        step *= 2
    lines, num = lax.optimization_barrier((lines, num))
    x_line = jnp.stack(grid.by_index(lines, places))
    half = groups * tokens
    own_num, own_conv = (lax.dynamic_slice_in_dim(t, c * half, half, 2) for t in (num, conv))
    attn = own_num[:, :HEAD_SIZE] / (own_num[:, HEAD_SIZE : HEAD_SIZE + 1] + HASH_COUNT) + own_conv
    attn = grid.deal(attn.reshape(feats, half), Z, dim=1)

    rows = MODEL_WIDTH // inner
    x_line = x_line[:, :tokens].reshape(half, MODEL_WIDTH)
    x_half = parts_of(jnp.concatenate(grid.take(grid.deal(x_line, C, dim=1), C, dim=1)))
    attn, x_half = lax.optimization_barrier((attn, x_half))
    attn_t = jnp.concatenate(grid.take(attn, Z, dim=1))

    subsets = subsets.reshape(heads * hashes, BUCKETS)
    sub_hi, sub_rest = parts_of(subsets)
    sub_mid, sub_lo = parts_of(subsets - sub_hi.astype(F32))
    signs = hadamard()
    own_counts = contract(sub_hi, signs, 1, 0) + contract(sub_mid, signs, 1, 0) + contract(sub_lo, signs, 1, 0)
    own_counts = own_counts.reshape(heads, groups, own_hashes, BUCKETS).transpose(1, 0, 2, 3)

    steps = Steps(grid)
    output, d_attn_t, held = dense(
        x, attn_t, out_grad[0],
        w_out, b_out, gain_one, bias_one, w_up, b_up, w_down, b_down, gain_two, bias_two,
    )
    d_line = jnp.concatenate([d_attn_t.reshape(groups, feats, tokens), own_counts.reshape(groups, -1, tokens)], axis=1)
    d_line = [lax.dynamic_index_in_dim(d_line, (z + s) % groups, 0, keepdims=False) for s in range(groups)]
    d_line, held = lax.optimization_barrier((d_line, held))
    d_line = [d_line[0]] + [grid.send(t, Z, lambda i: (i + s) % groups) for s, t in enumerate(d_line[1:], 1)]
    d_second, first, d_hidden, attn_t, d_pre, d_first, n1, n2, cotangent, inside = held
    steps.add("down", grid.reduce(outer_blocks(inside, d_second, items, inner, c)))
    steps.start("down")
    others = (d_second, d_first, n1, n2, cotangent)
    rest = outer_rows(first, d_hidden, attn_t, d_pre, others, items, inner, c)
    d_line, rest, steps.state["down"] = lax.optimization_barrier((d_line, rest, steps.state["down"]))
    steps.add("rest", grid.reduce(rest))
    steps.start("rest")

    def enter(d_line):
        d_line = grid.ordered(d_line, Z)
        own = jnp.concatenate([t[:feats] for t in d_line], axis=1)
        counts = jnp.stack([t[feats:] for t in d_line]).reshape(HEAD_COUNT, own_hashes, BUCKETS)
        return grid.collect(grid.offer(own, C), C, 1).reshape(heads, HEAD_SIZE, width), counts

    d_all, counts = enter(d_line)

    plan = [["down"], ["rest"], ["down", "head0"], ["down"], ["down", "rest", "head0", "head1"], ["rest"]]
    first_c = jnp.where(c == 0, 1.0, 0.0)
    found, last = [], ()
    for call in range(heads * BACK_PARTS):
        head, part = call // BACK_PARTS, call % BACK_PARTS
        if call < len(plan):
            last, d_all = steps.stage(plan[call], last, d_all)
            if call:
                found.append(last)
        own_taps = taps[head : head + 1] * first_c
        last = attend_back(head, part, BACK_PARTS, qkv, valid, proj, num, d_all, tab, own_taps, groups, inner)
        if part == BACK_PARTS - 1:
            whole_head = [f[:3] for f in found[head * BACK_PARTS :]] + [last[:3]]
            steps.add(f"head{head}", grid.head([[t[0] for t in f] for f in whole_head], x_half))
    found.append(last)
    d_t = [jnp.sum(found[head * BACK_PARTS][3][:CONV], axis=1) * first_c for head in range(heads)]
    last_head = f"head{heads - 1}"
    steps.stage(["head1", last_head])
    steps.stage([last_head])
    d_w = [t[0].reshape(-1, 3, HEAD_SIZE) for t in grid.found]
    d_w = jnp.stack(d_w, axis=2).reshape(-1, 3 * feats)
    d_b = jnp.stack([t[1].reshape(3, HEAD_SIZE) for t in grid.found], axis=1).reshape(-1)
    d_t = jnp.pad(jnp.concatenate(d_t), (0, 3 * feats - heads * CONV))
    rows = MODEL_WIDTH // inner
    below = jnp.pad(jnp.stack([d_b, d_t]), ((0, EXTRA - 2), (0, 0)))
    steps.add("tail", grid.tail(jnp.concatenate([d_w, below])))
    mine = jnp.concatenate([t[2] for t in grid.found])
    steps.add("home", grid.home(mine))
    steps.stage(["tail", "rest"])
    steps.stage(["tail", "home"])
    steps.stage(["tail", "down"])
    d_down = copied(steps.done["down"])
    steps.stage(["tail", "home", "rest"], d_down)
    rest, wide, back = steps.done["rest"], w_up.shape[1], steps.done["home"]
    d_up = widened(rest, wide)
    d_out, last_rows = rest[wide : wide + MODEL_WIDTH], rest[wide + MODEL_WIDTH :]
    back = [t.reshape(heads, 3, HEAD_SIZE, tokens) for t in grid.ordered(back, Z)]
    back = [jnp.concatenate([t[:, i] for t in back]).reshape(MODEL_WIDTH, tokens) for i in range(3)]
    d_x = held[4]
    for i, w in enumerate((w_query, w_key, w_value)):
        d_x = d_x + by_weight(back[i], w, 0, 1)
    (d_x, d_up, d_out), _ = steps.stage(["tail"], (d_x, d_up, d_out))
    tail = steps.done["tail"]
    weights = rejoined(tail, rows, c)
    below = tail[0][:, rows:]
    for s in range(1, inner):
        below = jnp.where(c == s, tail[s][:, rows:], below)
    d_b = below[:, 0]
    d_conv_taps = below[0, 1].reshape(groups, feats)[:, : heads * CONV].reshape(HEAD_COUNT, CONV)
    names = ("b_out", "gain_one", "bias_one", "b_down", "gain_two", "bias_two")
    vectors = dict(zip(names, last_rows))
    vectors["b_up"] = last_rows[len(names) : len(names) + wide // MODEL_WIDTH].reshape(-1)

    result = []
    for i in range(3):
        result += [weights[i], d_b[i]]
    result += [
        d_conv_taps, d_out, vectors["b_out"], vectors["gain_one"], vectors["bias_one"], d_up, vectors["b_up"],
        d_down, vectors["b_down"], vectors["gain_two"], vectors["bias_two"],
    ]
    return (output[None], d_x[None], counts[None], *result)


def solution(mesh):
    items, count = mesh.shape["item"], mesh.shape["seq"]
    groups = math.gcd(HEAD_COUNT, count)
    sizes = (items, groups, count // groups)
    seq = ("z", "core")
    tokens = P("item", seq, None)
    in_specs = (tokens, P("item"), P("item", seq)) + (P(),) * 18 + (tokens,)
    out_specs = (tokens, tokens, P("item", None, seq, None)) + (P(),) * 17
    return jax.shard_map(
        functools.partial(per_device, sizes),
        mesh=Mesh(mesh.devices.reshape(sizes), AXES),
        in_specs=in_specs,
        out_specs=out_specs,
        check_vma=False,
    )
```

time: 1030 us -> 679 us (0.66)
  waiting for transfers between devices: 458 us -> 104 us
  blocking collectives: 97.9 us -> 0 us
  starting transfers between devices: 39 us -> 77.5 us
  other arithmetic: 35 us -> 66.6 us
  local copies, waits for them, and re-layouts: 90.9 us -> 118 us
  Pallas kernels: 227 us -> 243 us
  matrix products: 49.1 us -> 34.6 us
    psum x1 -> x0, waiting for transfers between devices: 368 us -> none  [per_device(): summed = lax.psum(placed, both)]
    psum x1 -> x0, blocking collectives: 97.9 us -> none  [per_device(): d_conv_taps = lax.psum(taps_placed, both).reshape(HEAD_COUNT, CONV)]
    unnamed x119 -> x279, local copies, waits for them, and re-layouts: 31.3 us -> 85.9 us
    ppermute x29 -> x49, starting transfers between devices: 39 us -> 76.9 us  [send(): return lax.ppermute(x, AXES, pairs)]
    add x3 -> x18, other arithmetic: 4.07 us -> 22.3 us  [the longest x2 13.4 us: reduce(): x = sum((yield from self.moving(C, blocks)))]
    concatenate x0 -> x31, other arithmetic: none -> 16.5 us  [the longest x15 10 us: collect(): return parts if dim is None else jnp.concatenate(parts, axis=dim)]
    pallas_call x2 -> x16, Pallas kernels: 227 us -> 243 us  [the longest x6 137 us: attend_back(): pl.pallas_call(functools.partial(bwd_kernel, hashes, groups, inner, part...]
    another operation x3 -> x10, local copies, waits for them, and re-layouts: 17.9 us -> 2.84 us  [the longest x1 1.62 us: per_device(): vectors = dict(zip(names, last_rows))]
  transfers between devices with their start and end apart: 30 -> 53, of which waited for: 13 -> 15; matrix products, arithmetic and copies ran while one was open for 5% -> 10% of each run, Pallas kernels for 0% -> 27%
where the time goes in v2:
time: 679 us; the launch traced here: 669 us
  Pallas kernels  243 us (36%)
  local copies, waits for them, and re-layouts  118 us (17%)
  waiting for transfers between devices  104 us (15%)
  starting transfers between devices  77.5 us (11%)
  other arithmetic  66.6 us (10%)
  matrix products  34.6 us (5%)
  between operations  24.9 us (4%)
    pallas_call x6, Pallas kernels, attend_back(): pl.pallas_call(functools.partial(bwd_kernel, hashes, groups, inner, part...  137 us
    ppermute x49, waiting for transfers between devices, send(): return lax.ppermute(x, AXES, pairs)  104 us
    unnamed x279, local copies, waits for them, and re-layouts  85.9 us
    ppermute x49, starting transfers between devices, send(): return lax.ppermute(x, AXES, pairs)  76.9 us
    pallas_call x4, Pallas kernels, fill(): pl.pallas_call(fill_kernel, grid=(heads, parts), in_specs=specs[:len(ins)...  39.3 us
    pallas_call x1, Pallas kernels, read(): pl.pallas_call(functools.partial(read_kernel, hashes, groups, inner), gri...  36.7 us
    dot_general x38, matrix products, contract(): lax.dot_general(a, b, (((i,), (j,)), ((), ())), preferred_element_type=F32)  34.6 us
  transfers between devices with their start and end apart: 53, of which 15 were waited for; matrix products, arithmetic and copies ran while one was open for 10% of the time, Pallas kernels for 27%

profile of v2, /device:TPU:25, one launch (start us, length us, event | category | flops | bytes accessed | tf_op | source)
XLA Modules:
  0.0 669.1 jit_solution(13924691614235614696)
XLA Ops:
  18.4 2.3 collective-permute-start.1
  25.6 9.8 %fill.4.refs_0_ = f32[3,16,256,128]{3,2,1,0:T(8,128)S(1)} custom-call(f32[9,64,512]{2,1,0:T(8,128)S(1)} %bitcast.332, f32[9,64,512]{2,1,0:T(8,128)S(1)} %bitcast.333, f32[1,512]{1,0:T(1,128)S(1)} %fusion.97.valid_ref, f32[128,64]{1,0:T(8,128)S(1)} %bitcast.340), custom_call_target="tpu_custom_call" | custom-call | tf_op jit(solution)/shard_map/fill/pallas_call | solution.py:310
  38.2 4.0 collective-permute-done
  48.5 9.8 %fill.5.refs_0_ = f32[3,16,256,128]{3,2,1,0:T(8,128)S(1)} custom-call(f32[9,64,512]{2,1,0:T(8,128)S(1)} %bitcast.336, f32[9,64,512]{2,1,0:T(8,128)S(1)} %bitcast.337, f32[1,512]{1,0:T(1,128)S(1)} %fusion.96.valid_ref, f32[128,64]{1,0:T(8,128)S(1)} %bitcast.341, f32[3,16,256,128]{3,2,1,0:T(8,128)S(1)} %fill.4.refs_0_), custom_call_target="tpu_custom_call" | custom-call | tf_op jit(solution)/shard_map/fill/pallas_call | solution.py:310
  59.5 8.5 %collective-permute-done.3 = f32[264,768]{1,0:T(8,128)S(1)} collective-permute-done((f32[264,768]{1,0:T(8,128)}, f32[264,768]{1,0:T(8,128)S(1)}, u32[]{:S(2)}, u32[]{:S(2)}) %collective-permute-start.3) | collective-permute-done | bytes 811040 | tf_op jit(solution)/shard_map/ppermute | solution.py:582
  73.5 9.8 %fill.6.refs_0_ = f32[3,16,256,128]{3,2,1,0:T(8,128)S(1)} custom-call(f32[9,64,512]{2,1,0:T(8,128)S(1)} %bitcast.338, f32[9,64,512]{2,1,0:T(8,128)S(1)} %bitcast.339, f32[1,512]{1,0:T(1,128)S(1)} %fusion.95.valid_ref, f32[128,64]{1,0:T(8,128)S(1)} %bitcast.342, f32[3,16,256,128]{3,2,1,0:T(8,128)S(1)} %fill.5.refs_0_), custom_call_target="tpu_custom_call" | custom-call | tf_op jit(solution)/shard_map/fill/pallas_call | solution.py:310
  84.6 7.7 %collective-permute-done.6 = f32[264,768]{1,0:T(8,128)S(1)} collective-permute-done((f32[264,768]{1,0:T(8,128)S(1)}, f32[264,768]{1,0:T(8,128)S(1)}, u32[]{:S(2)}, u32[]{:S(2)}) %collective-permute-start.6) | collective-permute-done | bytes 811040 | tf_op jit(solution)/shard_map/ppermute | solution.py:582
  110.7 2.4 slice-done
  114.5 9.8 %fill.7.tab_ref = f32[3,16,256,128]{3,2,1,0:T(8,128)S(1)} custom-call(f32[9,64,512]{2,1,0:T(8,128)S(1)} %bitcast.334, f32[9,64,512]{2,1,0:T(8,128)S(1)} %bitcast.335, f32[1,512]{1,0:T(1,128)S(1)} %fusion.94.valid_ref, f32[128,64]{1,0:T(8,128)S(1)} %bitcast.343, f32[3,16,256,128]{3,2,1,0:T(8,128)S(1)} %bitcast.331), custom_call_target="tpu_custom_call" | custom-call | tf_op jit(solution)/shard_map/fill/pallas_call | solution.py:310
  124.3 36.7 %read.1 = (f32[3,80,2048]{2,1,0:T(8,128)S(1)}, f32[3,64,2048]{2,1,0:T(8,128)S(1)}, f32[3,16,256]{2,1,0:T(8,128)S(1)}) custom-call(f32[9,64,2048]{2,1,0:T(8,128)S(1)} %bitcast.304, f32[9,64,2048]{2,1,0:T(8,128)S(1)} %bitcast.305, f32[3,16,256,128]{3,2,1,0:T(8,128)S(1)} %fill.7.tab_ref, f32[128,64]{1,0:T(8,128)S(1)} %bitcast.344, ...), custom_call_target="tpu_custom_call" | custom-call | tf_op jit(solution)/shard_map/read/pallas_call | solution.py:326
  163.5 2.8 collective-permute-done.10
  166.3 2.4 add.594.num_ref
  174.2 3.8 collective-permute-start.12
  179.9 2.1 fusion.2
  182.7 8.9 %collective-permute-done.12 = f32[192,256]{1,0:T(8,128)S(1)} collective-permute-done((f32[192,256]{1,0:T(8,128)S(1)}, f32[192,256]{1,0:T(8,128)S(1)}, u32[]{:S(2)}, u32[]{:S(2)}) %collective-permute-start.12) | collective-permute-done | bytes 196640 | tf_op jit(solution)/shard_map/ppermute | solution.py:582
  196.5 1.9 fusion.110
  204.9 1.9 fusion.hidden_ref
  212.9 2.4 copy.88
  218.5 7.0 %outer_blocks.1 = (f32[4,384,768]{2,1,0:T(8,128)S(1)}, f32[4,384,768]{2,1,0:T(8,128)}) custom-call(s32[1]{0:T(128)} %bitcast.52.c_ref, f32[256,3072]{1,0:T(8,128)S(1)} %copy-done.24, f32[256,768]{1,0:T(8,128)S(1)} %copy-done.20), custom_call_target="tpu_custom_call" | custom-call | tf_op jit(solution)/shard_map/outer_blocks/pallas_call | solution.py:459
  226.1 4.5 collective-permute-start.15
  236.2 9.8 %outer_rows.1 = (f32[2048,768]{1,0:T(8,128)S(1)}, f32[2048,768]{1,0:T(8,128)S(1)}) custom-call(s32[1]{0:T(128)} %bitcast.52.c_ref, f32[256,768]{1,0:T(8,128)S(1)} %copy-done.26, f32[256,3072]{1,0:T(8,128)S(1)} %copy-done.22, f32[768,256]{1,0:T(8,128)S(1)} %copy-done.43, f32[256,768]{1,0:T(8,128)S(1)} %copy-done.29, f32[256,768]{1,0:T(8,128)S(1)} %copy-done.20, ...), custom_call_target="tpu_custom_call" | custom-call | tf_op jit(solution)/shard_map/outer_rows/pallas_call | solution.py:546
  246.1 2.7 copy-done.42
  248.8 2.6 copy-done.79
  253.4 5.1 add.650
  262.6 2.3 copy-done.3
  264.9 2.8 copy-done.9
  269.1 23.8 %attend_back.6 = (f32[1,64,2048]{2,1,0:T(8,128)S(1)}, f32[1,64,2048]{2,1,0:T(8,128)S(1)}, f32[1,64,2048]{2,1,0:T(8,128)S(1)}, f32[16,2048]{1,0:T(8,128)S(1)}) custom-call(f32[9,64,2048]{2,1,0:T(8,128)S(1)} %bitcast.306, f32[9,64,2048]{2,1,0:T(8,128)S(1)} %bitcast.307, f32[9,64,2048]{2,1,0:T(8,128)S(1)} %bitcast.308, f32[1,2048]{1,0:T(1,128)S(1)} %slice.382.valid_ref, ...), custom_call_target="tpu_custom_call" | custom-call | tf_op jit(solution)/shard_map/attend_back/pallas_call | solution.py:352
  294.5 8.4 %add.651 = f32[4,512,768]{2,1,0:T(8,128)} add(f32[4,512,768]{2,1,0:T(8,128)} %bitcast.352, f32[4,512,768]{2,1,0:T(8,128)} %collective-permute-done.20) | non-fusion elementwise | flops 1572864 | bytes 18874368 | tf_op jit(solution)/shard_map/add | solution.py:696
  303.0 3.1 copy-done.4
  306.1 2.8 copy-done.10
  310.3 22.1 %attend_back.7 = (f32[1,64,2048]{2,1,0:T(8,128)S(1)}, f32[1,64,2048]{2,1,0:T(8,128)S(1)}, f32[1,64,2048]{2,1,0:T(8,128)S(1)}, f32[16,2048]{1,0:T(8,128)}) custom-call(f32[9,64,2048]{2,1,0:T(8,128)S(1)} %bitcast.309, f32[9,64,2048]{2,1,0:T(8,128)S(1)} %bitcast.310, f32[9,64,2048]{2,1,0:T(8,128)S(1)} %bitcast.311, f32[1,2048]{1,0:T(1,128)S(1)} %slice.382.valid_ref, ...), custom_call_target="tpu_custom_call" | custom-call | tf_op jit(solution)/shard_map/attend_back/pallas_call | solution.py:352
  339.5 3.6 collective-permute-start.21
  343.5 2.3 copy-done.5
  345.9 2.9 copy-done.11
  348.8 23.8 %attend_back.8 = (f32[1,64,2048]{2,1,0:T(8,128)S(1)}, f32[1,64,2048]{2,1,0:T(8,128)S(1)}, f32[1,64,2048]{2,1,0:T(8,128)S(1)}, f32[16,2048]{1,0:T(8,128)S(1)}) custom-call(f32[9,64,2048]{2,1,0:T(8,128)S(1)} %bitcast.312, f32[9,64,2048]{2,1,0:T(8,128)S(1)} %bitcast.313, f32[9,64,2048]{2,1,0:T(8,128)S(1)} %bitcast.314, f32[1,2048]{1,0:T(1,128)S(1)} %slice.382.valid_ref, ...), custom_call_target="tpu_custom_call" | custom-call | tf_op jit(solution)/shard_map/attend_back/pallas_call | solution.py:352
  374.3 2.8 collective-permute-start.26
  379.2 2.5 copy-done.6
  381.7 2.8 copy-done.12
  385.9 22.1 %attend_back.9 = (f32[1,64,2048]{2,1,0:T(8,128)S(1)}, f32[1,64,2048]{2,1,0:T(8,128)S(1)}, f32[1,64,2048]{2,1,0:T(8,128)S(1)}, f32[16,2048]{1,0:T(8,128)}) custom-call(f32[9,64,2048]{2,1,0:T(8,128)S(1)} %bitcast.315, f32[9,64,2048]{2,1,0:T(8,128)S(1)} %bitcast.316, f32[9,64,2048]{2,1,0:T(8,128)S(1)} %bitcast.317, f32[1,2048]{1,0:T(1,128)S(1)} %slice.382.valid_ref, ...), custom_call_target="tpu_custom_call" | custom-call | tf_op jit(solution)/shard_map/attend_back/pallas_call | solution.py:352
  416.0 2.5 dynamic-slice_bitcast_fusion.12
  422.4 2.3 copy-done.7
  424.7 2.8 copy-done.13
  429.2 23.8 %attend_back.10 = (f32[1,64,2048]{2,1,0:T(8,128)S(1)}, f32[1,64,2048]{2,1,0:T(8,128)S(1)}, f32[1,64,2048]{2,1,0:T(8,128)S(1)}, f32[16,2048]{1,0:T(8,128)S(1)}) custom-call(f32[9,64,2048]{2,1,0:T(8,128)S(1)} %bitcast.318, f32[9,64,2048]{2,1,0:T(8,128)S(1)} %bitcast.319, f32[9,64,2048]{2,1,0:T(8,128)S(1)} %bitcast.320, f32[1,2048]{1,0:T(1,128)S(1)} %slice.382.valid_ref, ...), custom_call_target="tpu_custom_call" | custom-call | tf_op jit(solution)/shard_map/attend_back/pallas_call | solution.py:352
  456.8 2.3 collective-permute-start.35
  461.9 22.1 %attend_back.11 = (f32[1,64,2048]{2,1,0:T(8,128)S(1)}, f32[1,64,2048]{2,1,0:T(8,128)S(1)}, f32[1,64,2048]{2,1,0:T(8,128)S(1)}, f32[16,2048]{1,0:T(8,128)}) custom-call(f32[9,64,2048]{2,1,0:T(8,128)S(1)} %bitcast.321, f32[9,64,2048]{2,1,0:T(8,128)S(1)} %bitcast.322, f32[9,64,2048]{2,1,0:T(8,128)S(1)} %bitcast.323, f32[1,2048]{1,0:T(1,128)S(1)} %slice.382.valid_ref, ...), custom_call_target="tpu_custom_call" | custom-call | tf_op jit(solution)/shard_map/attend_back/pallas_call | solution.py:352
  485.7 4.6 fusion.111
  500.4 2.6 fusion.78
  514.6 3.9 collective-permute-done.36
  518.4 12.4 %collective-permute-done.37 = f32[104,576]{0,1:T(8,128)S(1)} collective-permute-done((f32[104,576]{0,1:T(8,128)S(1)}, f32[104,576]{0,1:T(8,128)S(1)}, u32[]{:S(2)}, u32[]{:S(2)}) %collective-permute-start.37) | collective-permute-done | bytes 239648 | tf_op jit(solution)/shard_map/ppermute | solution.py:582
  532.5 2.1 collective-permute-start.43
  536.1 3.8 collective-permute-done.44
  539.8 14.5 %collective-permute-done.43 = f32[104,576]{0,1:T(8,128)S(1)} collective-permute-done((f32[104,576]{0,1:T(8,128)S(1)}, f32[104,576]{0,1:T(8,128)S(1)}, u32[]{:S(2)}, u32[]{:S(2)}) %collective-permute-start.43) | collective-permute-done | bytes 239648 | tf_op jit(solution)/shard_map/ppermute | solution.py:582
  558.9 5.6 collective-permute-start.40
  564.4 2.0 collective-permute-done.39
  566.5 17.5 %collective-permute-start.41 = (f32[576,256]{1,0:T(8,128)}, f32[576,256]{1,0:T(8,128)}, u32[]{:S(2)}, u32[]{:S(2)}) collective-permute-start(f32[576,256]{1,0:T(8,128)} %get-tuple-element.404), channel_id=1, source_target_pairs={{0,6},{1,7},{2,0},{3,1},{4,2},{5,3},{6,4},{7,5},{8,14},{9,15},{10,... | collective-permute-start | bytes 1769480 | tf_op jit(solution)/shard_map/ppermute | solution.py:582
  585.4 3.7 copy-done.35
  589.1 4.7 copied.1
  593.8 13.5 %collective-permute-done.41 = f32[576,256]{1,0:T(8,128)} collective-permute-done((f32[576,256]{1,0:T(8,128)}, f32[576,256]{1,0:T(8,128)}, u32[]{:S(2)}, u32[]{:S(2)}) %collective-permute-start.41) | collective-permute-done | bytes 589856 | tf_op jit(solution)/shard_map/ppermute | solution.py:582
  607.4 19.1 %collective-permute-done.45 = f32[3,104,768]{2,1,0:T(8,128)} collective-permute-done((f32[3,104,768]{2,1,0:T(8,128)S(1)}, f32[3,104,768]{2,1,0:T(8,128)}, u32[]{:S(2)}, u32[]{:S(2)}) %collective-permute-start.45) | collective-permute-done | bytes 958496 | tf_op jit(solution)/shard_map/ppermute | solution.py:582
  627.3 3.2 slice.338
  630.5 4.6 copy-done.31
  635.1 4.7 widened.1
  641.9 2.2 pad_maximum_fusion.2.refs_0_
  657.7 3.2 rejoined.1
  (561 shorter events, 173.8 us)
Async XLA Ops:
  7.2 185.5 %copy-start = (bf16[768,768]{1,0:T(8,128)(2,1)S(1)}, bf16[768,768]{1,0:T(8,128)(2,1)}, u32[]{:S(2)}) copy-start(bf16[768,768]{1,0:T(8,128)(2,1)} %param.33) | copy-start | bytes 3538948
  7.2 327.6 %reduce-scatter.7.cloned.1.call-start = ((), (), s32[]{:S(2)}) async-start(), calls=%async_computation.4 | async-start | bytes 5898240
  17.6 6.6 collective-permute-start.2
  18.4 19.8 %collective-permute-start.1 = (f32[264,768]{1,0:T(8,128)S(1)}, f32[264,768]{1,0:T(8,128)S(1)}, u32[]{:S(2)}, u32[]{:S(2)}) collective-permute-start(f32[264,768]{1,0:T(8,128)S(1)} %select_maximum_fusion.1), channel_id=1, source_target_pairs={{2,0},{3,1},{4,2},{5,3},{6,4},{7,5},{10,8},{11,9},{12,10},{13,11},... | collective-permute-start | bytes 2433032 | tf_op jit(solution)/shard_map/ppermute | solution.py:582
  20.7 21.4 %collective-permute-start = (f32[264,768]{1,0:T(8,128)S(1)}, f32[264,768]{1,0:T(8,128)}, u32[]{:S(2)}, u32[]{:S(2)}) collective-permute-start(f32[264,768]{1,0:T(8,128)S(1)} %select_maximum_fusion.1), channel_id=1, source_target_pairs={{0,2},{1,3},{2,4},{3,5},{4,6},{5,7},{8,10},{9,11},{10,12},{11,13},... | collective-permute-start | bytes 2433032 | tf_op jit(solution)/shard_map/ppermute | solution.py:582
  45.1 3.2 collective-permute-start.5
  46.2 21.8 %collective-permute-start.3 = (f32[264,768]{1,0:T(8,128)}, f32[264,768]{1,0:T(8,128)S(1)}, u32[]{:S(2)}, u32[]{:S(2)}) collective-permute-start(f32[264,768]{1,0:T(8,128)} %collective-permute-done), channel_id=1, source_target_pairs={{2,4},{3,5},{4,6},{5,7},{10,12},{11,13},{12,14},{13,15},{18,20},{1... | collective-permute-start | bytes 2433032 | tf_op jit(solution)/shard_map/ppermute | solution.py:582
  47.5 20.5 %collective-permute-start.4 = (f32[264,768]{1,0:T(8,128)S(1)}, f32[264,768]{1,0:T(8,128)S(1)}, u32[]{:S(2)}, u32[]{:S(2)}) collective-permute-start(f32[264,768]{1,0:T(8,128)S(1)} %collective-permute-done.1), channel_id=1, source_target_pairs={{2,0},{3,1},{4,2},{5,3},{10,8},{11,9},{12,10},{13,11},{18,16},{19,... | collective-permute-start | bytes 2433032 | tf_op jit(solution)/shard_map/ppermute | solution.py:582
  69.9 3.3 collective-permute-start.8
  70.7 21.6 %collective-permute-start.6 = (f32[264,768]{1,0:T(8,128)S(1)}, f32[264,768]{1,0:T(8,128)S(1)}, u32[]{:S(2)}, u32[]{:S(2)}) collective-permute-start(f32[264,768]{1,0:T(8,128)S(1)} %collective-permute-done.3), channel_id=1, source_target_pairs={{4,6},{5,7},{12,14},{13,15},{20,22},{21,23},{28,30},{29,31}} | collective-permute-start | bytes 2433032 | tf_op jit(solution)/shard_map/ppermute | solution.py:582
  72.0 20.3 %collective-permute-start.7 = (f32[264,768]{1,0:T(8,128)S(1)}, f32[264,768]{1,0:T(8,128)S(1)}, u32[]{:S(2)}, u32[]{:S(2)}) collective-permute-start(f32[264,768]{1,0:T(8,128)S(1)} %collective-permute-done.4), channel_id=1, source_target_pairs={{2,0},{3,1},{10,8},{11,9},{18,16},{19,17},{26,24},{27,25}} | collective-permute-start | bytes 2433032 | tf_op jit(solution)/shard_map/ppermute | solution.py:582
  94.2 9.3 %collective-permute-start.9 = (f32[584,256]{1,0:T(8,128)S(1)}, f32[584,256]{1,0:T(8,128)}, u32[]{:S(2)}, u32[]{:S(2)}) collective-permute-start(f32[584,256]{1,0:T(8,128)S(1)} %pad_maximum_fusion.36), channel_id=1, source_target_pairs={{0,1},{1,0},{2,3},{3,2},{4,5},{5,4},{6,7},{7,6},{8,9},{9,8},{10,11... | collective-permute-start | bytes 1794056 | tf_op jit(solution)/shard_map/ppermute | solution.py:582
  110.7 13.6 %copy-start.2 = (f32[576,2048]{1,0:T(8,128)}, f32[576,2048]{1,0:T(8,128)S(1)}, u32[]{:S(2)}) copy-start(f32[576,2048]{1,0:T(8,128)S(1)} %slice.377) | copy-start | bytes 14155780
  124.3 36.8 %copy-start.8 = (f32[3,16,256,128]{3,2,1,0:T(8,128)}, f32[3,16,256,128]{3,2,1,0:T(8,128)S(1)}, u32[]{:S(2)}) copy-start(f32[3,16,256,128]{3,2,1,0:T(8,128)S(1)} %fill.7.tab_ref) | copy-start | bytes 18874372
  162.2 4.1 collective-permute-start.10
  171.9 6.4 collective-permute-start.14
  174.2 8.5 %collective-permute-start.13 = (f32[192,256]{1,0:T(8,128)S(1)}, f32[192,256]{1,0:T(8,128)S(1)}, u32[]{:S(2)}, u32[]{:S(2)}) collective-permute-start(f32[192,256]{1,0:T(8,128)S(1)} %get-tuple-element.535), channel_id=1, source_target_pairs={{0,6},{1,7},{2,0},{3,1},{4,2},{5,3},{6,4},{7,5},{8,14},{9,15},{10,... | collective-permute-start | bytes 589832 | tf_op jit(solution)/shard_map/ppermute | solution.py:582
  174.2 17.3 %collective-permute-start.12 = (f32[192,256]{1,0:T(8,128)S(1)}, f32[192,256]{1,0:T(8,128)S(1)}, u32[]{:S(2)}, u32[]{:S(2)}) collective-permute-start(f32[192,256]{1,0:T(8,128)S(1)} %get-tuple-element.536), channel_id=1, source_target_pairs={{0,4},{1,5},{2,6},{3,7},{4,0},{5,1},{6,2},{7,3},{8,12},{9,13},{10,... | collective-permute-start | bytes 589832 | tf_op jit(solution)/shard_map/ppermute | solution.py:582
  178.0 13.6 %collective-permute-start.11 = (f32[192,256]{1,0:T(8,128)S(1)}, f32[192,256]{1,0:T(8,128)S(1)}, u32[]{:S(2)}, u32[]{:S(2)}) collective-permute-start(f32[192,256]{1,0:T(8,128)S(1)} %get-tuple-element.537), channel_id=1, source_target_pairs={{0,2},{1,3},{2,4},{3,5},{4,6},{5,7},{6,0},{7,1},{8,10},{9,11},{10,... | collective-permute-start | bytes 589832 | tf_op jit(solution)/shard_map/ppermute | solution.py:582
  179.9 15.0 %slice-start.2 = ((s8[4718592]{0:T(1024)(128)(4,1)}), s8[4194304]{0:T(1024)(128)(4,1)S(1)}, s32[]{:S(2)}) async-start(s8[4718592]{0:T(1024)(128)(4,1)} %bitcast.372), calls=%async_computation.8 | async-start | bytes 8388608
  194.9 15.4 %copy-start.33 = (f32[256,768]{1,0:T(8,128)}, f32[256,768]{1,0:T(8,128)S(1)}, u32[]{:S(2)}) copy-start(f32[256,768]{1,0:T(8,128)S(1)} %get-tuple-element.274.n1_ref) | copy-start | bytes 2359300
  215.2 16.4 %copy-start.29 = (f32[256,768]{1,0:T(8,128)S(1)}, f32[256,768]{1,0:T(8,128)}, u32[]{:S(2)}) copy-start(f32[256,768]{1,0:T(8,128)} %copy-done.28) | copy-start | bytes 2359300
  215.2 16.4 %copy-start.34 = (f32[256,768]{1,0:T(8,128)S(1)}, f32[256,768]{1,0:T(8,128)}, u32[]{:S(2)}) copy-start(f32[256,768]{1,0:T(8,128)} %copy-done.33) | copy-start | bytes 2359300
  218.5 13.2 %copy-start.22 = (f32[256,3072]{1,0:T(8,128)S(1)}, f32[256,3072]{1,0:T(8,128)}, u32[]{:S(2)}) copy-start(f32[256,3072]{1,0:T(8,128)} %copy-done.21) | copy-start | bytes 9437188
  218.5 13.2 %copy-start.26 = (f32[256,768]{1,0:T(8,128)S(1)}, f32[256,768]{1,0:T(8,128)}, u32[]{:S(2)}) copy-start(f32[256,768]{1,0:T(8,128)} %copy-done.25) | copy-start | bytes 2359300
  225.6 25.9 %collective-permute-start.18 = (f32[4,384,768]{2,1,0:T(8,128)}, f32[4,384,768]{2,1,0:T(8,128)}, u32[]{:S(2)}, u32[]{:S(2)}) collective-permute-start(f32[4,384,768]{2,1,0:T(8,128)} %get-tuple-element.281), channel_id=1, source_target_pairs={{0,1},{1,0},{2,3},{3,2},{4,5},{5,4},{6,7},{7,6},{8,9},{9,8},{10,11... | collective-permute-start | bytes 14155784 | tf_op jit(solution)/shard_map/ppermute | solution.py:582
  226.1 25.3 %collective-permute-start.15 = (f32[204,256]{1,0:T(8,128)S(1)}, f32[204,256]{1,0:T(8,128)S(1)}, u32[]{:S(2)}, u32[]{:S(2)}) collective-permute-start(f32[204,256]{1,0:T(8,128)S(1)} %get-tuple-element.265), channel_id=1, source_target_pairs={{0,2},{1,3},{2,4},{3,5},{4,6},{5,7},{6,0},{7,1},{8,10},{9,11},{10,... | collective-permute-start | bytes 626696 | tf_op jit(solution)/shard_map/ppermute | solution.py:582
  230.6 20.8 %collective-permute-start.16 = (f32[204,256]{1,0:T(8,128)S(1)}, f32[204,256]{1,0:T(8,128)S(1)}, u32[]{:S(2)}, u32[]{:S(2)}) collective-permute-start(f32[204,256]{1,0:T(8,128)S(1)} %get-tuple-element.266), channel_id=1, source_target_pairs={{0,4},{1,5},{2,6},{3,7},{4,0},{5,1},{6,2},{7,3},{8,12},{9,13},{10,... | collective-permute-start | bytes 626696 | tf_op jit(solution)/shard_map/ppermute | solution.py:582
  231.7 19.7 %collective-permute-start.17 = (f32[204,256]{1,0:T(8,128)S(1)}, f32[204,256]{1,0:T(8,128)S(1)}, u32[]{:S(2)}, u32[]{:S(2)}) collective-permute-start(f32[204,256]{1,0:T(8,128)S(1)} %get-tuple-element.267), channel_id=1, source_target_pairs={{0,6},{1,7},{2,0},{3,1},{4,2},{5,3},{6,4},{7,5},{8,14},{9,15},{10,... | collective-permute-start | bytes 626696 | tf_op jit(solution)/shard_map/ppermute | solution.py:582
  252.8 5.7 collective-permute-start.19
  261.1 148.5 %reduce-scatter.9.cloned.1.call-start = ((), (), s32[]{:S(2)}) async-start(), calls=%async_computation.5 | async-start | bytes 7864320
  261.6 32.9 %collective-permute-start.20 = (f32[4,512,768]{2,1,0:T(8,128)}, f32[4,512,768]{2,1,0:T(8,128)}, u32[]{:S(2)}, u32[]{:S(2)}) collective-permute-start(f32[4,512,768]{2,1,0:T(8,128)} %bitcast.371), channel_id=1, source_target_pairs={{0,1},{1,0},{2,3},{3,2},{4,5},{5,4},{6,7},{7,6},{8,9},{9,8},{10,11... | collective-permute-start | bytes 18874376 | tf_op jit(solution)/shard_map/ppermute | solution.py:582
  302.9 251.4 %all-gather.5.cloned.1.call-start = ((), (), s32[]{:S(2)}) async-start(), calls=%async_computation.3 | async-start | bytes 10616832 | tf_op jit(solution)/shard_map/all_gather | solution.py:755
  339.0 70.5 %collective-permute-start.27 = (f32[192,2048]{1,0:T(8,128)}, f32[192,2048]{1,0:T(8,128)}, u32[]{:S(2)}, u32[]{:S(2)}) collective-permute-start(f32[192,2048]{1,0:T(8,128)} %pad_maximum_fusion.15), channel_id=1, source_target_pairs={{0,1},{1,0},{2,3},{3,2},{4,5},{5,4},{6,7},{7,6},{8,9},{9,8},{10,11... | collective-permute-start | bytes 4718600 | tf_op jit(solution)/shard_map/ppermute | solution.py:582
  339.5 33.9 %collective-permute-start.21 = (f32[96,768]{1,0:T(8,128)S(1)}, f32[96,768]{1,0:T(8,128)S(1)}, u32[]{:S(2)}, u32[]{:S(2)}) collective-permute-start(f32[96,768]{1,0:T(8,128)S(1)} %get-tuple-element.315), channel_id=1, source_target_pairs={{0,2},{1,3},{2,4},{3,5},{4,6},{5,7},{6,0},{7,1},{8,10},{9,11},{10,... | collective-permute-start | bytes 884744 | tf_op jit(solution)/shard_map/ppermute | solution.py:582
  343.1 30.3 %collective-permute-start.22 = (f32[96,768]{1,0:T(8,128)S(1)}, f32[96,768]{1,0:T(8,128)S(1)}, u32[]{:S(2)}, u32[]{:S(2)}) collective-permute-start(f32[96,768]{1,0:T(8,128)S(1)} %get-tuple-element.316), channel_id=1, source_target_pairs={{0,4},{1,5},{2,6},{3,7},{4,0},{5,1},{6,2},{7,3},{8,12},{9,13},{10,... | collective-permute-start | bytes 884744 | tf_op jit(solution)/shard_map/ppermute | solution.py:582
  343.1 30.3 %collective-permute-start.23 = (f32[96,768]{1,0:T(8,128)S(1)}, f32[96,768]{1,0:T(8,128)S(1)}, u32[]{:S(2)}, u32[]{:S(2)}) collective-permute-start(f32[96,768]{1,0:T(8,128)S(1)} %get-tuple-element.317), channel_id=1, source_target_pairs={{0,6},{1,7},{2,0},{3,1},{4,2},{5,3},{6,4},{7,5},{8,14},{9,15},{10,... | collective-permute-start | bytes 884744 | tf_op jit(solution)/shard_map/ppermute | solution.py:582
  374.3 35.3 %collective-permute-start.26 = (f32[96,768]{1,0:T(8,128)}, f32[96,768]{1,0:T(8,128)}, u32[]{:S(2)}, u32[]{:S(2)}) collective-permute-start(f32[96,768]{1,0:T(8,128)} %add_add_fusion.2), channel_id=1, source_target_pairs={{0,6},{1,7},{2,0},{3,1},{4,2},{5,3},{6,4},{7,5},{8,14},{9,15},{10,... | collective-permute-start | bytes 884744 | tf_op jit(solution)/shard_map/ppermute | solution.py:582
  377.1 32.5 %collective-permute-start.25 = (f32[96,768]{1,0:T(8,128)}, f32[96,768]{1,0:T(8,128)}, u32[]{:S(2)}, u32[]{:S(2)}) collective-permute-start(f32[96,768]{1,0:T(8,128)} %add_add_fusion.2), channel_id=1, source_target_pairs={{0,4},{1,5},{2,6},{3,7},{4,0},{5,1},{6,2},{7,3},{8,12},{9,13},{10,... | collective-permute-start | bytes 884744 | tf_op jit(solution)/shard_map/ppermute | solution.py:582
  377.8 31.8 %collective-permute-start.24 = (f32[96,768]{1,0:T(8,128)}, f32[96,768]{1,0:T(8,128)}, u32[]{:S(2)}, u32[]{:S(2)}) collective-permute-start(f32[96,768]{1,0:T(8,128)} %add_add_fusion.2), channel_id=1, source_target_pairs={{0,2},{1,3},{2,4},{3,5},{4,6},{5,7},{6,0},{7,1},{8,10},{9,11},{10,... | collective-permute-start | bytes 884744 | tf_op jit(solution)/shard_map/ppermute | solution.py:582
  418.6 207.9 %all-gather.3.cloned.1.call-start = ((), (), s32[]{:S(2)}) async-start(), calls=%async_computation.2 | async-start | bytes 14155776 | tf_op jit(solution)/shard_map/all_gather | solution.py:755
  418.6 67.0 %collective-permute-start.28 = (f32[192,2048]{1,0:T(8,128)}, f32[192,2048]{1,0:T(8,128)}, u32[]{:S(2)}, u32[]{:S(2)}) collective-permute-start(f32[192,2048]{1,0:T(8,128)} %pad_maximum_fusion.16), channel_id=1, source_target_pairs={{0,1},{1,0},{2,3},{3,2},{4,5},{5,4},{6,7},{7,6},{8,9},{9,8},{10,11... | collective-permute-start | bytes 4718600 | tf_op jit(solution)/shard_map/ppermute | solution.py:582
  420.0 35.4 %collective-permute-start.29 = (f32[128,768]{1,0:T(8,128)}, f32[128,768]{1,0:T(8,128)S(1)}, u32[]{:S(2)}, u32[]{:S(2)}) collective-permute-start(f32[128,768]{1,0:T(8,128)} %get-tuple-element.352), channel_id=1, source_target_pairs={{0,2},{1,3},{2,4},{3,5},{4,6},{5,7},{6,0},{7,1},{8,10},{9,11},{10,... | collective-permute-start | bytes 1179656 | tf_op jit(solution)/shard_map/ppermute | solution.py:582
  421.8 34.2 %collective-permute-start.30 = (f32[128,768]{1,0:T(8,128)}, f32[128,768]{1,0:T(8,128)S(1)}, u32[]{:S(2)}, u32[]{:S(2)}) collective-permute-start(f32[128,768]{1,0:T(8,128)} %get-tuple-element.353), channel_id=1, source_target_pairs={{0,4},{1,5},{2,6},{3,7},{4,0},{5,1},{6,2},{7,3},{8,12},{9,13},{10,... | collective-permute-start | bytes 1179656 | tf_op jit(solution)/shard_map/ppermute | solution.py:582
  421.8 34.2 %collective-permute-start.31 = (f32[128,768]{1,0:T(8,128)}, f32[128,768]{1,0:T(8,128)S(1)}, u32[]{:S(2)}, u32[]{:S(2)}) collective-permute-start(f32[128,768]{1,0:T(8,128)} %get-tuple-element.354), channel_id=1, source_target_pairs={{0,6},{1,7},{2,0},{3,1},{4,2},{5,3},{6,4},{7,5},{8,14},{9,15},{10,... | collective-permute-start | bytes 1179656 | tf_op jit(solution)/shard_map/ppermute | solution.py:582
  429.2 26.8 %copy-start.110 = (f32[128,768]{1,0:T(8,128)S(1)}, f32[128,768]{1,0:T(8,128)}, u32[]{:S(2)}) copy-start(f32[128,768]{1,0:T(8,128)} %get-tuple-element.363) | copy-start | bytes 1179652
  456.8 47.8 %collective-permute-start.35 = (f32[128,768]{1,0:T(8,128)}, f32[128,768]{1,0:T(8,128)}, u32[]{:S(2)}, u32[]{:S(2)}) collective-permute-start(f32[128,768]{1,0:T(8,128)} %add_add_fusion), channel_id=1, source_target_pairs={{0,6},{1,7},{2,0},{3,1},{4,2},{5,3},{6,4},{7,5},{8,14},{9,15},{10,... | collective-permute-start | bytes 1179656 | tf_op jit(solution)/shard_map/ppermute | solution.py:582
  459.1 45.6 %collective-permute-start.34 = (f32[128,768]{1,0:T(8,128)}, f32[128,768]{1,0:T(8,128)}, u32[]{:S(2)}, u32[]{:S(2)}) collective-permute-start(f32[128,768]{1,0:T(8,128)} %add_add_fusion), channel_id=1, source_target_pairs={{0,4},{1,5},{2,6},{3,7},{4,0},{5,1},{6,2},{7,3},{8,12},{9,13},{10,... | collective-permute-start | bytes 1179656 | tf_op jit(solution)/shard_map/ppermute | solution.py:582
  460.1 44.6 %collective-permute-start.33 = (f32[128,768]{1,0:T(8,128)}, f32[128,768]{1,0:T(8,128)}, u32[]{:S(2)}, u32[]{:S(2)}) collective-permute-start(f32[128,768]{1,0:T(8,128)} %add_add_fusion), channel_id=1, source_target_pairs={{0,2},{1,3},{2,4},{3,5},{4,6},{5,7},{6,0},{7,1},{8,10},{9,11},{10,... | collective-permute-start | bytes 1179656 | tf_op jit(solution)/shard_map/ppermute | solution.py:582
  461.9 23.7 %copy-start.92 = (f32[192,2048]{1,0:T(8,128)S(1)}, f32[192,2048]{1,0:T(8,128)}, u32[]{:S(2)}) copy-start(f32[192,2048]{1,0:T(8,128)} %pad_maximum_fusion.16) | copy-start | bytes 4718596
  492.1 6.9 %collective-permute-start.32 = (f32[192,2048]{1,0:T(8,128)S(1)}, f32[192,2048]{1,0:T(8,128)S(1)}, u32[]{:S(2)}, u32[]{:S(2)}) collective-permute-start(f32[192,2048]{1,0:T(8,128)S(1)} %pad_maximum_fusion.17), channel_id=1, source_target_pairs={{0,1},{1,0},{2,3},{3,2},{4,5},{5,4},{6,7},{7,6},{8,9},{9,8},{10,11... | collective-permute-start | bytes 4718600 | tf_op jit(solution)/shard_map/ppermute | solution.py:582
  510.5 7.9 %collective-permute-start.36 = (f32[104,576]{0,1:T(8,128)S(1)}, f32[104,576]{0,1:T(8,128)S(1)}, u32[]{:S(2)}, u32[]{:S(2)}) collective-permute-start(f32[104,576]{0,1:T(8,128)S(1)} %copy-done.119), channel_id=1, source_target_pairs={{0,8},{1,9},{2,10},{3,11},{4,12},{5,13},{6,14},{7,15},{8,16},{9,17... | collective-permute-start | bytes 718856 | tf_op jit(solution)/shard_map/ppermute | solution.py:582
  511.7 19.2 %collective-permute-start.37 = (f32[104,576]{0,1:T(8,128)S(1)}, f32[104,576]{0,1:T(8,128)S(1)}, u32[]{:S(2)}, u32[]{:S(2)}) collective-permute-start(f32[104,576]{0,1:T(8,128)S(1)} %copy-done.118), channel_id=1, source_target_pairs={{0,16},{1,17},{2,18},{3,19},{4,20},{5,21},{6,22},{7,23},{8,24},{9,... | collective-permute-start | bytes 718856 | tf_op jit(solution)/shard_map/ppermute | solution.py:582
  512.7 18.1 %collective-permute-start.38 = (f32[104,576]{0,1:T(8,128)S(1)}, f32[104,576]{0,1:T(8,128)S(1)}, u32[]{:S(2)}, u32[]{:S(2)}) collective-permute-start(f32[104,576]{0,1:T(8,128)S(1)} %get-tuple-element.395), channel_id=1, source_target_pairs={{0,24},{1,25},{2,26},{3,27},{4,28},{5,29},{6,30},{7,31},{8,0},{9,1... | collective-permute-start | bytes 718856 | tf_op jit(solution)/shard_map/ppermute | solution.py:582
  532.2 7.6 %collective-permute-start.44 = (f32[104,576]{0,1:T(8,128)S(1)}, f32[104,576]{0,1:T(8,128)S(1)}, u32[]{:S(2)}, u32[]{:S(2)}) collective-permute-start(f32[104,576]{0,1:T(8,128)S(1)} %add_add_fusion.1), channel_id=1, source_target_pairs={{0,6},{1,7},{2,0},{3,1},{4,2},{5,3},{6,4},{7,5},{8,14},{9,15},{10,... | collective-permute-start | bytes 718856 | tf_op jit(solution)/shard_map/ppermute | solution.py:582
  532.5 21.8 %collective-permute-start.43 = (f32[104,576]{0,1:T(8,128)S(1)}, f32[104,576]{0,1:T(8,128)S(1)}, u32[]{:S(2)}, u32[]{:S(2)}) collective-permute-start(f32[104,576]{0,1:T(8,128)S(1)} %add_add_fusion.1), channel_id=1, source_target_pairs={{0,4},{1,5},{2,6},{3,7},{4,0},{5,1},{6,2},{7,3},{8,12},{9,13},{10,... | collective-permute-start | bytes 718856 | tf_op jit(solution)/shard_map/ppermute | solution.py:582
  534.6 19.7 %collective-permute-start.42 = (f32[104,576]{0,1:T(8,128)S(1)}, f32[104,576]{0,1:T(8,128)S(1)}, u32[]{:S(2)}, u32[]{:S(2)}) collective-permute-start(f32[104,576]{0,1:T(8,128)S(1)} %add_add_fusion.1), channel_id=1, source_target_pairs={{0,2},{1,3},{2,4},{3,5},{4,6},{5,7},{6,0},{7,1},{8,10},{9,11},{10,... | collective-permute-start | bytes 718856 | tf_op jit(solution)/shard_map/ppermute | solution.py:582
  535.5 30.9 %collective-permute-start.39 = (f32[576,256]{1,0:T(8,128)}, f32[576,256]{1,0:T(8,128)S(1)}, u32[]{:S(2)}, u32[]{:S(2)}) collective-permute-start(f32[576,256]{1,0:T(8,128)} %get-tuple-element.402), channel_id=1, source_target_pairs={{0,2},{1,3},{2,4},{3,5},{4,6},{5,7},{6,0},{7,1},{8,10},{9,11},{10,... | collective-permute-start | bytes 1769480 | tf_op jit(solution)/shard_map/ppermute | solution.py:582
  556.1 51.3 %collective-permute-start.47 = (f32[3,104,768]{2,1,0:T(8,128)S(1)}, f32[3,104,768]{2,1,0:T(8,128)S(1)}, u32[]{:S(2)}, u32[]{:S(2)}) collective-permute-start(f32[3,104,768]{2,1,0:T(8,128)S(1)} %pad_maximum_fusion.24), channel_id=1, source_target_pairs={{0,24},{1,25},{2,26},{3,27},{4,28},{5,29},{6,30},{7,31},{8,0},{9,1... | collective-permute-start | bytes 2875400 | tf_op jit(solution)/shard_map/ppermute | solution.py:582
  556.1 51.3 %collective-permute-start.46 = (f32[3,104,768]{2,1,0:T(8,128)S(1)}, f32[3,104,768]{2,1,0:T(8,128)}, u32[]{:S(2)}, u32[]{:S(2)}) collective-permute-start(f32[3,104,768]{2,1,0:T(8,128)S(1)} %pad_maximum_fusion.24), channel_id=1, source_target_pairs={{0,16},{1,17},{2,18},{3,19},{4,20},{5,21},{6,22},{7,23},{8,24},{9,... | collective-permute-start | bytes 2875400 | tf_op jit(solution)/shard_map/ppermute | solution.py:582
  557.5 69.0 %collective-permute-start.45 = (f32[3,104,768]{2,1,0:T(8,128)S(1)}, f32[3,104,768]{2,1,0:T(8,128)}, u32[]{:S(2)}, u32[]{:S(2)}) collective-permute-start(f32[3,104,768]{2,1,0:T(8,128)S(1)} %pad_maximum_fusion.24), channel_id=1, source_target_pairs={{0,8},{1,9},{2,10},{3,11},{4,12},{5,13},{6,14},{7,15},{8,16},{9,17... | collective-permute-start | bytes 2875400 | tf_op jit(solution)/shard_map/ppermute | solution.py:582
  558.9 35.0 %collective-permute-start.40 = (f32[576,256]{1,0:T(8,128)}, f32[576,256]{1,0:T(8,128)}, u32[]{:S(2)}, u32[]{:S(2)}) collective-permute-start(f32[576,256]{1,0:T(8,128)} %get-tuple-element.403), channel_id=1, source_target_pairs={{0,4},{1,5},{2,6},{3,7},{4,0},{5,1},{6,2},{7,3},{8,12},{9,13},{10,... | collective-permute-start | bytes 1769480 | tf_op jit(solution)/shard_map/ppermute | solution.py:582
  566.5 40.9 %collective-permute-start.41 = (f32[576,256]{1,0:T(8,128)}, f32[576,256]{1,0:T(8,128)}, u32[]{:S(2)}, u32[]{:S(2)}) collective-permute-start(f32[576,256]{1,0:T(8,128)} %get-tuple-element.404), channel_id=1, source_target_pairs={{0,6},{1,7},{2,0},{3,1},{4,2},{5,3},{6,4},{7,5},{8,14},{9,15},{10,... | collective-permute-start | bytes 1769480 | tf_op jit(solution)/shard_map/ppermute | solution.py:582
  648.1 9.6 %collective-permute-start.48 = (f32[3,416,768]{2,1,0:T(8,128)S(1)}, f32[3,416,768]{2,1,0:T(8,128)S(1)}, u32[]{:S(2)}, u32[]{:S(2)}) collective-permute-start(f32[3,416,768]{2,1,0:T(8,128)S(1)} %copy-done.32), channel_id=1, source_target_pairs={{0,1},{1,0},{2,3},{3,2},{4,5},{5,4},{6,7},{7,6},{8,9},{9,8},{10,11... | collective-permute-start | bytes 11501576 | tf_op jit(solution)/shard_map/ppermute | solution.py:582
  (124 other events, 318.9 us)
Sparse Core Ops, SparseCore 0:
  261.2 58.3 reduce-scatter.6
  323.2 70.2 reduce-scatter.8
  418.7 60.7 all-gather.4
  508.9 103.9 all-gather.2

commit v3 on v2

--- a/solution.py
+++ b/solution.py
@@ -22,7 +22,7 @@
 ROWS = 80
 CHUNK = 256
 VMEM_BYTES = 32 * 1024 * 1024
-BACK_VMEM = 24 * 1024 * 1024
+BACK_VMEM = 60 * 1024 * 1024
 OUTER_VMEM = 16 * 1024 * 1024
 BACK_PARTS = 2
 
@@ -217,13 +217,33 @@
 
 
 def bwd_kernel(
-    hashes, groups, inner, with_conv, q_ref, k_ref, v_ref, valid_ref, proj_ref, num_ref, da_ref, tab_ref, taps_ref,
-    dq_ref, dk_ref, dv_ref, dt_ref, sq, sk, gq, gk, cols, xq, xk, dv,
+    hashes, groups, inner, head, part, qkv_hbm, valid_ref, proj_ref, num_hbm, da_hbm, tab_hbm, taps_ref, *refs
 ):
-    width = q_ref.shape[2]
+    before_hbm = refs[0] if part else None
+    out_hbm, dt_ref, q_ref, k_ref, v_ref, num_ref, da_ref, tab_ref, before_ref, sq, sk, gq, gk, cols, xq, xk, dv, sems = refs[
+        1 if part else 0 :
+    ]
+    heads, width = num_hbm.shape[0], q_ref.shape[2]
     block = width // (groups * inner)
+    sources = (
+        qkv_hbm.at[head], qkv_hbm.at[heads + head], qkv_hbm.at[2 * heads + head], num_hbm.at[head], da_hbm.at[head],
+        tab_hbm.at[head, part * hashes : (part + 1) * hashes],
+    )
+    targets = (q_ref, k_ref, v_ref, num_ref, da_ref, tab_ref)
+    copies = [
+        pltpu.make_async_copy(source, target.at[0], sems.at[i])
+        for i, (source, target) in enumerate(zip(sources, targets))
+    ]
+    if part:
+        copies.append(pltpu.make_async_copy(before_hbm, before_ref, sems.at[6]))
+    for copy in copies:
+        copy.start()
+    copies[0].wait()
     sq[...] = signs_of(q_ref[0], proj_ref[...])
+    copies[1].wait()
     sk[...] = signs_of(k_ref[0], proj_ref[...])
+    for copy in copies[2:]:
+        copy.wait()
     da = da_ref[0]
     v = v_ref[0]
     inv = 1.0 / (num_ref[0, 64:65, :] + HASH_COUNT)
@@ -263,14 +283,12 @@
             gk[pl.ds(base, 8), c : c + CHUNK] = sign_grad(r, rows, low, phi, d) * (2.0 - 2.0 * s8 * s8)
 
     back = proj_ref[...].T
-    for u_ref, g_ref, o_ref in ((q_ref, gq, dq_ref), (k_ref, gk, dk_ref)):
-        u = u_ref[0]
-        scale = norm_scale(u)
-        g = dot3(back, g_ref[...])
-        inside = g - u * (scale * scale * jnp.mean(g * u, axis=0, keepdims=True))
-        o_ref[0] = (scale * 0.125) * inside
+    copies = [
+        pltpu.make_async_copy(source.at[0], out_hbm.at[64 * i : 64 * i + 64], sems.at[i])
+        for i, source in enumerate((q_ref, k_ref, v_ref))
+    ]
     total = dv[:64, :]
-    if with_conv:
+    if part == 0:
         natural = reorder(v, inner, groups, block)
         grad = reorder(da, inner, groups, block)
         conv = jnp.zeros(natural.shape, F32)
@@ -279,7 +297,19 @@
             moved = grad * shifted(natural, j - HALF)
             dt_ref[j : j + 1, :] = jnp.sum(moved, axis=0, keepdims=True)
         total = total + reorder(conv, groups, inner, block)
-    dv_ref[0] = total * valid_ref[...]
+    total = total * valid_ref[...]
+    v_ref[0] = total + before_ref[128:, :] if part else total
+    copies[2].start()
+    for i, (u_ref, g_ref) in enumerate(((q_ref, gq), (k_ref, gk))):
+        u = u_ref[0]
+        scale = norm_scale(u)
+        g = dot3(back, g_ref[...])
+        inside = g - u * (scale * scale * jnp.mean(g * u, axis=0, keepdims=True))
+        grad = (scale * 0.125) * inside
+        u_ref[0] = grad + before_ref[64 * i : 64 * i + 64, :] if part else grad
+        copies[i].start()
+    for copy in copies:
+        copy.wait()
 
 
 def one(*shape, at=0):
@@ -342,33 +372,63 @@
     )(qkv, qkv, tab, proj, taps)
 
 
-def attend_back(head, part, parts, qkv, valid, proj, num, d_attn, tab, taps, groups, inner):
-    heads, width = qkv.shape[0] // 3, qkv.shape[2]
+def attend_back(head, part, parts, qkv, valid, proj, num, d_attn, tab, taps, before, groups, inner):
+    width = qkv.shape[2]
     hashes = proj.shape[0] // 8 // parts
-
-    def pick(*shape, at):
-        return pl.BlockSpec((1,) + shape, lambda _: (at,) + (0,) * len(shape))
-
+    hbm = pl.BlockSpec(memory_space=pltpu.HBM)
+    rows = pltpu.VMEM((1, 64, width), F32)
+    ins = [qkv, valid, proj, num, d_attn, tab, taps] + [before] * (part > 0)
+    specs = [hbm, same(1, width), pl.BlockSpec((hashes * 8, 64), lambda _: (part, 0)), hbm, hbm, hbm, SMEM, hbm]
     return pl.pallas_call(
-        functools.partial(bwd_kernel, hashes, groups, inner, part == 0),
+        functools.partial(bwd_kernel, hashes, groups, inner, head, part),
         grid=(1,),
-        in_specs=[
-            pick(64, width, at=head), pick(64, width, at=heads + head), pick(64, width, at=2 * heads + head),
-            same(1, width), pl.BlockSpec((hashes * 8, 64), lambda _: (part, 0)),
-            pick(ROWS, width, at=head), pick(64, width, at=head),
-            pl.BlockSpec((1, hashes, BUCKETS, 128), lambda _: (head, part, 0, 0)), SMEM,
-        ],
-        out_specs=[pick(64, width, at=0)] * 3 + [same(16, width)],
-        out_shape=[jax.ShapeDtypeStruct((1, 64, width), F32)] * 3
-        + [jax.ShapeDtypeStruct((16, width), F32)],
-        scratch_shapes=[pltpu.VMEM((hashes * 8, width), F32)] * 4
+        in_specs=specs[: len(ins)],
+        out_specs=[hbm, same(16, width)],
+        out_shape=[jax.ShapeDtypeStruct((192, width), F32), jax.ShapeDtypeStruct((16, width), F32)],
+        scratch_shapes=[rows] * 3
+        + [pltpu.VMEM((1, ROWS, width), F32), rows, pltpu.VMEM((1, hashes, BUCKETS, 128), F32)]
+        + [pltpu.VMEM((192, width), F32)]
+        + [pltpu.VMEM((hashes * 8, width), F32)] * 4
         + [pltpu.VMEM((width, 256), BF)]
         + [pltpu.VMEM((256, width), BF)] * 2
-        + [pltpu.VMEM((ROWS, width), F32)],
+        + [pltpu.VMEM((ROWS, width), F32), pltpu.SemaphoreType.DMA((7,))],
         compiler_params=pltpu.CompilerParams(vmem_limit_bytes=BACK_VMEM),
         cost_estimate=pl.CostEstimate(flops=0, bytes_accessed=0, transcendentals=0),
         name="attend_back",
-    )(qkv, qkv, qkv, valid, proj, num, d_attn, tab, taps)
+    )(*ins)
+
+
+def weights_kernel(count, c_ref, *refs):
+    parts, (hi_ref, lo_ref, w_ref, sum_ref, mine_ref, full_ref) = refs[:count], refs[count:]
+    full = parts[0][...]
+    for part in parts[1:]:
+        full = full + part[...]
+    full_ref[...] = full
+    fh, fl = split(full)
+    w_ref[...] = dot(fh, hi_ref[...]) + dot(fl, hi_ref[...]) + dot(fh, lo_ref[...])
+    sum_ref[...] = jnp.broadcast_to(jnp.sum(full, axis=1, keepdims=True), sum_ref.shape)
+    size = mine_ref.shape[1]
+    mine_ref[...] = full_ref[:, pl.ds(pl.multiple_of(c_ref[0] * size, 128), size)]
+
+
+def weights_of(parts, x_parts, c):
+    features, tokens = parts[0].shape
+    ins = [*parts, *x_parts]
+    vmem = pl.BlockSpec(memory_space=pltpu.VMEM)
+    return pl.pallas_call(
+        functools.partial(weights_kernel, len(parts)),
+        in_specs=[SMEM] + [vmem] * len(ins),
+        out_specs=[vmem] * 3,
+        out_shape=[
+            jax.ShapeDtypeStruct((features, x_parts[0].shape[1]), F32),
+            jax.ShapeDtypeStruct((features, 128), F32),
+            jax.ShapeDtypeStruct((features, tokens // len(parts)), F32),
+        ],
+        scratch_shapes=[pltpu.VMEM((features, tokens), F32)],
+        compiler_params=pltpu.CompilerParams(vmem_limit_bytes=VMEM_BYTES),
+        cost_estimate=pl.CostEstimate(flops=0, bytes_accessed=0, transcendentals=0),
+        name="weights_of",
+    )(c.reshape(1), *ins)
 
 
 def copy_kernel(x_ref, o_ref):
@@ -701,15 +761,10 @@
         gather = functools.partial(lax.all_gather, axis_name=("item", "core"), axis=0, tiled=True)
         return (yield from self.applying(gather, x))
 
-    def head(self, d_parts, x_parts):
-        d_parts = yield d_parts
-        d_part = jnp.concatenate([sum(parts) for parts in zip(*d_parts)])
-        full = sum(self.collect((yield from self.moving(C, [d_part])), C))
-        dh, dl = parts_of(full)
-        xh, xl = x_parts
-        d_w = contract(xh, dh, 0, 1) + contract(xl, dh, 0, 1) + contract(xh, dl, 0, 1)
-        d_b = jnp.sum(full, axis=1)
-        self.found.append((d_w, d_b, self.own_block(full, C, 1)))
+    def head(self, d_part, x_parts):
+        d_part = yield d_part
+        parts = yield from self.moving(C, [d_part])
+        self.found.append(weights_of(parts, x_parts, self.place[C]))
 
     def home(self, mine):
         mine = yield mine
@@ -851,7 +906,7 @@
     places = grid.places(Z)
     for k in range(groups):
         if k:
-            up, down, tab, chunks, places = lax.optimization_barrier((up, down, tab, chunks, places))
+            up, down, tab, chunks, places, taps = lax.optimization_barrier((up, down, tab, chunks, places, taps))
             came.append((up, down))
             lines.append(grid.arrived(came, Z, k))
         if k < groups - 1:
@@ -860,6 +915,7 @@
         chunks.append(chunk)
         per_head = chunk[: 3 * feats].reshape(3 * heads, HEAD_SIZE, -1)
         tab = fill(per_head, chunk[3 * feats : 3 * feats + 1], proj, tab)
+    tab, chunks = lax.optimization_barrier((tab, chunks))
     chunks = grid.by_index(chunks, places)
     chunks = jnp.concatenate(
         [t[:, i * tokens : (i + 1) * tokens] for i in range(inner) for t in chunks], axis=1
@@ -919,46 +975,59 @@
 
     plan = [["down"], ["rest"], ["down", "head0"], ["down"], ["down", "rest", "head0", "head1"], ["rest"]]
     first_c = jnp.where(c == 0, 1.0, 0.0)
+
+    def staged(names, held=(), beside=()):
+        before, count = grid.found, len(grid.found)
+        (held, ready), beside = steps.stage(names, (held, before), beside)
+        grid.found = ready + before[count:]
+        return held, beside
+
     found, last = [], ()
     for call in range(heads * BACK_PARTS):
         head, part = call // BACK_PARTS, call % BACK_PARTS
         if call < len(plan):
-            last, d_all = steps.stage(plan[call], last, d_all)
+            last, d_all = staged(plan[call], last, d_all)
             if call:
                 found.append(last)
         own_taps = taps[head : head + 1] * first_c
-        last = attend_back(head, part, BACK_PARTS, qkv, valid, proj, num, d_all, tab, own_taps, groups, inner)
+        before = last[0] if part else None
+        last = attend_back(head, part, BACK_PARTS, qkv, valid, proj, num, d_all, tab, own_taps, before, groups, inner)
         if part == BACK_PARTS - 1:
-            whole_head = [f[:3] for f in found[head * BACK_PARTS :]] + [last[:3]]
-            steps.add(f"head{head}", grid.head([[t[0] for t in f] for f in whole_head], x_half))
+            steps.add(f"head{head}", grid.head(last[0], x_half))
     found.append(last)
-    d_t = [jnp.sum(found[head * BACK_PARTS][3][:CONV], axis=1) * first_c for head in range(heads)]
+    d_t = [jnp.sum(found[head * BACK_PARTS][1][:CONV], axis=1) * first_c for head in range(heads)]
     last_head = f"head{heads - 1}"
-    steps.stage(["head1", last_head])
-    steps.stage([last_head])
-    d_w = [t[0].reshape(-1, 3, HEAD_SIZE) for t in grid.found]
-    d_w = jnp.stack(d_w, axis=2).reshape(-1, 3 * feats)
-    d_b = jnp.stack([t[1].reshape(3, HEAD_SIZE) for t in grid.found], axis=1).reshape(-1)
+    others = [name for name in steps.live if name.startswith("head") and name != last_head]
+    staged(others + [last_head, "rest"])
+    staged([last_head])
+    steps.add("home", grid.home(jnp.concatenate([t[2] for t in grid.found])))
+    d_w = jnp.stack([t[0].reshape(3, HEAD_SIZE, -1) for t in grid.found], axis=1).reshape(3 * feats, -1).T
+    d_b = jnp.stack([t[1][:, 0].reshape(3, HEAD_SIZE) for t in grid.found], axis=1).reshape(-1)
     d_t = jnp.pad(jnp.concatenate(d_t), (0, 3 * feats - heads * CONV))
     rows = MODEL_WIDTH // inner
     below = jnp.pad(jnp.stack([d_b, d_t]), ((0, EXTRA - 2), (0, 0)))
     steps.add("tail", grid.tail(jnp.concatenate([d_w, below])))
-    mine = jnp.concatenate([t[2] for t in grid.found])
-    steps.add("home", grid.home(mine))
-    steps.stage(["tail", "rest"])
-    steps.stage(["tail", "home"])
-    steps.stage(["tail", "down"])
+    def input_part(blocks, first_head):
+        count = blocks[0].shape[0] // (3 * HEAD_SIZE)
+        total = 0.0
+        for i, w in enumerate((w_query, w_key, w_value)):
+            spans = [slice((k * 3 + i) * HEAD_SIZE, (k * 3 + i + 1) * HEAD_SIZE) for k in range(count)]
+            d = jnp.concatenate([t[span] for t in blocks for span in spans])
+            w = w.reshape(MODEL_WIDTH, groups, heads, HEAD_SIZE)[:, :, first_head : first_head + count]
+            total = total + by_weight(d, w.reshape(MODEL_WIDTH, -1), 0, 1)
+        return total
+
+    steps.stage(["tail"])
+    steps.stage(["tail"])
+    steps.stage(["tail", "down", "home"])
     d_down = copied(steps.done["down"])
-    steps.stage(["tail", "home", "rest"], d_down)
-    rest, wide, back = steps.done["rest"], w_up.shape[1], steps.done["home"]
+    steps.advance({"rest": steps.state["rest"]})
+    rest, wide = steps.done["rest"], w_up.shape[1]
     d_up = widened(rest, wide)
     d_out, last_rows = rest[wide : wide + MODEL_WIDTH], rest[wide + MODEL_WIDTH :]
-    back = [t.reshape(heads, 3, HEAD_SIZE, tokens) for t in grid.ordered(back, Z)]
-    back = [jnp.concatenate([t[:, i] for t in back]).reshape(MODEL_WIDTH, tokens) for i in range(3)]
-    d_x = held[4]
-    for i, w in enumerate((w_query, w_key, w_value)):
-        d_x = d_x + by_weight(back[i], w, 0, 1)
-    (d_x, d_up, d_out), _ = steps.stage(["tail"], (d_x, d_up, d_out))
+    (d_down, d_up, d_out, last_rows), _ = steps.stage(["tail", "home"], (d_down, d_up, d_out, last_rows))
+    d_x = held[4] + input_part(grid.ordered(steps.done["home"], Z), 0)
+    d_x, _ = steps.stage(["tail"], d_x)
     tail = steps.done["tail"]
     weights = rejoined(tail, rows, c)
     below = tail[0][:, rows:]

time: 679 us -> 653 us (0.962)
  local copies, waits for them, and re-layouts: 118 us -> 71.9 us
  Pallas kernels: 243 us -> 278 us
  matrix products: 34.6 us -> 26.4 us
  starting transfers between devices: 77.5 us -> 85.1 us
  waiting for transfers between devices: 104 us -> 96.5 us
    unnamed x279 -> x196, local copies, waits for them, and re-layouts: 85.9 us -> 38.7 us
    pallas_call x6 -> x9, Pallas kernels: 137 us -> 169 us  [the longest x6 161 us: attend_back(): pl.pallas_call(functools.partial(bwd_kernel, hashes, groups, inner, head,...]
    ppermute x49, waiting for transfers between devices: 104 us -> 93.3 us  [send(): return lax.ppermute(x, AXES, pairs)]
    dot_general x38 -> x29, matrix products: 34.6 us -> 26.4 us  [contract(): lax.dot_general(a, b, (((i,), (j,)), ((), ())), preferred_element_type=F32)]
    ppermute x49, starting transfers between devices: 76.9 us -> 84.8 us  [send(): return lax.ppermute(x, AXES, pairs)]
  transfers between devices with their start and end apart: 53 -> 53, of which waited for: 15 -> 16; matrix products, arithmetic and copies ran while one was open for 10% -> 10% of each run, Pallas kernels for 27% -> 34%
where the time goes in v3:
time: 653 us; the launch traced here: 644 us
  Pallas kernels  278 us (43%)
  waiting for transfers between devices  96.5 us (15%)
  starting transfers between devices  85.1 us (13%)
  local copies, waits for them, and re-layouts  71.9 us (11%)
  other arithmetic  61.3 us (9%)
  matrix products  26.4 us (4%)
  between operations  24.7 us (4%)
    pallas_call x6, Pallas kernels, attend_back(): pl.pallas_call(functools.partial(bwd_kernel, hashes, groups, inner, head,...  161 us
    ppermute x49, waiting for transfers between devices, send(): return lax.ppermute(x, AXES, pairs)  93.3 us
    ppermute x49, starting transfers between devices, send(): return lax.ppermute(x, AXES, pairs)  84.8 us
    pallas_call x4, Pallas kernels, fill(): pl.pallas_call(fill_kernel, grid=(heads, parts), in_specs=specs[:len(ins)...  39.3 us
    unnamed x196, local copies, waits for them, and re-layouts  38.7 us
    pallas_call x1, Pallas kernels, read(): pl.pallas_call(functools.partial(read_kernel, hashes, groups, inner), gri...  36.5 us
    dot_general x29, matrix products, contract(): lax.dot_general(a, b, (((i,), (j,)), ((), ())), preferred_element_type=F32)  26.4 us
    add x2, other arithmetic, reduce(): x = sum((yield from self.moving(C, blocks)))  13.2 us
  transfers between devices with their start and end apart: 53, of which 16 were waited for; matrix products, arithmetic and copies ran while one was open for 10% of the time, Pallas kernels for 34%

profile of v3, /device:TPU:25, one launch (start us, length us, event | category | flops | bytes accessed | tf_op | source)
XLA Modules:
  0.0 644.0 jit_solution(15782386381663848244)
XLA Ops:
  16.4 3.2 collective-permute-start.1
  23.8 9.8 %fill.4.refs_0_ = f32[3,16,256,128]{3,2,1,0:T(8,128)S(1)} custom-call(f32[9,64,512]{2,1,0:T(8,128)S(1)} %bitcast.369, f32[9,64,512]{2,1,0:T(8,128)S(1)} %bitcast.370, f32[1,512]{1,0:T(1,128)S(1)} %fusion.87.valid_ref, f32[128,64]{1,0:T(8,128)S(1)} %bitcast.377), custom_call_target="tpu_custom_call" | custom-call | tf_op jit(solution)/shard_map/fill/pallas_call | solution.py:340
  36.1 4.8 collective-permute-done
  47.4 9.9 %fill.5.refs_0_ = f32[3,16,256,128]{3,2,1,0:T(8,128)S(1)} custom-call(f32[9,64,512]{2,1,0:T(8,128)S(1)} %bitcast.373, f32[9,64,512]{2,1,0:T(8,128)S(1)} %bitcast.374, f32[1,512]{1,0:T(1,128)S(1)} %fusion.86.valid_ref, f32[128,64]{1,0:T(8,128)S(1)} %bitcast.378, f32[3,16,256,128]{3,2,1,0:T(8,128)S(1)} %fill.4.refs_0_), custom_call_target="tpu_custom_call" | custom-call | tf_op jit(solution)/shard_map/fill/pallas_call | solution.py:340
  58.4 8.4 %collective-permute-done.3 = f32[264,768]{1,0:T(8,128)S(1)} collective-permute-done((f32[264,768]{1,0:T(8,128)}, f32[264,768]{1,0:T(8,128)S(1)}, u32[]{:S(2)}, u32[]{:S(2)}) %collective-permute-start.3) | collective-permute-done | bytes 811040 | tf_op jit(solution)/shard_map/ppermute | solution.py:642
  73.0 9.9 %fill.6.refs_0_ = f32[3,16,256,128]{3,2,1,0:T(8,128)S(1)} custom-call(f32[9,64,512]{2,1,0:T(8,128)S(1)} %bitcast.375, f32[9,64,512]{2,1,0:T(8,128)S(1)} %bitcast.376, f32[1,512]{1,0:T(1,128)S(1)} %fusion.85.valid_ref, f32[128,64]{1,0:T(8,128)S(1)} %bitcast.379, f32[3,16,256,128]{3,2,1,0:T(8,128)S(1)} %fill.5.refs_0_), custom_call_target="tpu_custom_call" | custom-call | tf_op jit(solution)/shard_map/fill/pallas_call | solution.py:340
  84.2 7.9 %collective-permute-done.6 = f32[264,768]{1,0:T(8,128)S(1)} collective-permute-done((f32[264,768]{1,0:T(8,128)S(1)}, f32[264,768]{1,0:T(8,128)S(1)}, u32[]{:S(2)}, u32[]{:S(2)}) %collective-permute-start.6) | collective-permute-done | bytes 811040 | tf_op jit(solution)/shard_map/ppermute | solution.py:642
  103.0 2.8 copy-done.9
  105.8 9.8 %fill.7.tab_ref.tab_hbm = f32[3,16,256,128]{3,2,1,0:T(8,128)S(1)} custom-call(f32[9,64,512]{2,1,0:T(8,128)S(1)} %bitcast.371, f32[9,64,512]{2,1,0:T(8,128)S(1)} %bitcast.372, f32[1,512]{1,0:T(1,128)S(1)} %fusion.84.valid_ref, f32[128,64]{1,0:T(8,128)S(1)} %bitcast.380, f32[3,16,256,128]{3,2,1,0:T(8,128)S(1)} %copy-done.9), custom_call_target="tpu_custom_call" | custom-call | tf_op jit(solution)/shard_map/fill/pallas_call | solution.py:340
  117.8 2.0 copy-done.50
  119.8 36.5 %read.1 = (f32[3,80,2048]{2,1,0:T(8,128)S(1)}, f32[3,64,2048]{2,1,0:T(8,128)S(1)}, f32[3,16,256]{2,1,0:T(8,128)S(1)}) custom-call(f32[9,64,2048]{2,1,0:T(8,128)S(1)} %bitcast.361, f32[9,64,2048]{2,1,0:T(8,128)S(1)} %bitcast.362, f32[3,16,256,128]{3,2,1,0:T(8,128)S(1)} %fill.7.tab_ref.tab_hbm, f32[128,64]{1,0:T(8,128)S(1)} %bitcast.381, ...), custom_call_target="tpu_custom_call" | custom-call | tf_op jit(solution)/shard_map/read/pallas_call | solution.py:356
  157.5 4.1 collective-permute-done.10
  161.6 3.0 add.537.num_hbm
  165.5 1.7 copy-done.44
  172.4 3.1 collective-permute-start.12
  177.5 2.1 fusion.2
  180.3 8.9 %collective-permute-done.12 = f32[192,256]{1,0:T(8,128)S(1)} collective-permute-done((f32[192,256]{1,0:T(8,128)S(1)}, f32[192,256]{1,0:T(8,128)S(1)}, u32[]{:S(2)}, u32[]{:S(2)}) %collective-permute-start.12) | collective-permute-done | bytes 196640 | tf_op jit(solution)/shard_map/ppermute | solution.py:642
  193.6 1.9 fusion.100
  202.0 1.9 fusion.hidden_ref
  205.6 2.1 multiply_reduce_fusion.4
  210.0 2.4 copy.72
  213.7 1.9 copy-done.7
  215.6 7.0 %outer_blocks.1 = (f32[4,384,768]{2,1,0:T(8,128)S(1)}, f32[4,384,768]{2,1,0:T(8,128)}) custom-call(s32[1]{0:T(128)} %bitcast.52.c_ref, f32[256,3072]{1,0:T(8,128)S(1)} %copy-done.7, f32[256,768]{1,0:T(8,128)S(1)} %get-tuple-element.277.second_ref.b_ref), custom_call_target="tpu_custom_call" | custom-call | tf_op jit(solution)/shard_map/outer_blocks/pallas_call | solution.py:519
  223.5 4.1 collective-permute-start.15
  230.1 9.9 %outer_rows.1 = (f32[2048,768]{1,0:T(8,128)S(1)}, f32[2048,768]{1,0:T(8,128)S(1)}) custom-call(s32[1]{0:T(128)} %bitcast.52.c_ref, f32[256,768]{1,0:T(8,128)S(1)} %get-tuple-element.273.first_ref, f32[256,3072]{1,0:T(8,128)S(1)} %copy-done.5, f32[768,256]{1,0:T(8,128)S(1)} %copy-done.26, f32[256,768]{1,0:T(8,128)S(1)} %subtract_multiply_fusion.pre_ref, ...), custom_call_target="tpu_custom_call" | custom-call | tf_op jit(solution)/shard_map/outer_rows/pallas_call | solution.py:606
  240.0 2.7 copy-done.25
  242.7 2.6 copy-done.43
  245.3 2.8 collective-permute-done.16
  250.0 5.0 add.593
  258.8 27.3 %attend_back.6 = (f32[192,2048]{1,0:T(8,128)}, f32[16,2048]{1,0:T(8,128)}) custom-call(f32[9,64,2048]{2,1,0:T(8,128)} %bitcast.363, f32[1,2048]{1,0:T(1,128)} %slice.630.valid_ref, f32[128,64]{1,0:T(8,128)} %bitcast.382, f32[3,80,2048]{2,1,0:T(8,128)} %add.537.num_hbm, f32[3,64,2048]{2,1,0:T(8,128)} %bitcast.394, f32[3,16,256,128]{3,2,1,0:T(8,128)} %copy-done.2, ...), custom_call_target="tpu_custom_call" | custom-call | tf_op jit(solution)/shard_map/attend_back/pallas_call | solution.py:382
  286.1 8.2 %add.594 = f32[4,512,768]{2,1,0:T(8,128)} add(f32[4,512,768]{2,1,0:T(8,128)} %bitcast.389, f32[4,512,768]{2,1,0:T(8,128)} %collective-permute-done.20) | non-fusion elementwise | flops 1572864 | bytes 18874368 | tf_op jit(solution)/shard_map/add | solution.py:756
  294.4 26.3 %attend_back.7 = (f32[192,2048]{1,0:T(8,128)}, f32[16,2048]{1,0:T(8,128)}) custom-call(f32[9,64,2048]{2,1,0:T(8,128)} %bitcast.364, f32[1,2048]{1,0:T(1,128)} %slice.630.valid_ref, f32[128,64]{1,0:T(8,128)} %bitcast.383, f32[3,80,2048]{2,1,0:T(8,128)} %add.537.num_hbm, f32[3,64,2048]{2,1,0:T(8,128)} %bitcast.395, f32[3,16,256,128]{3,2,1,0:T(8,128)} %copy-done.2, ...), custom_call_target="tpu_custom_call" | custom-call | tf_op jit(solution)/shard_map/attend_back/pallas_call | solution.py:382
  320.8 2.2 dynamic-slice_bitcast_fusion.20
  325.7 27.3 %attend_back.8 = (f32[192,2048]{1,0:T(8,128)}, f32[16,2048]{1,0:T(8,128)}) custom-call(f32[9,64,2048]{2,1,0:T(8,128)} %bitcast.365, f32[1,2048]{1,0:T(1,128)} %slice.630.valid_ref, f32[128,64]{1,0:T(8,128)} %bitcast.384, f32[3,80,2048]{2,1,0:T(8,128)} %add.537.num_hbm, f32[3,64,2048]{2,1,0:T(8,128)} %bitcast.396, f32[3,16,256,128]{3,2,1,0:T(8,128)} %copy-done.2, ...), custom_call_target="tpu_custom_call" | custom-call | tf_op jit(solution)/shard_map/attend_back/pallas_call | solution.py:382
  356.4 2.1 collective-permute-start.24
  358.5 26.4 %attend_back.9 = (f32[192,2048]{1,0:T(8,128)}, f32[16,2048]{1,0:T(8,128)}) custom-call(f32[9,64,2048]{2,1,0:T(8,128)} %bitcast.366, f32[1,2048]{1,0:T(1,128)} %slice.630.valid_ref, f32[128,64]{1,0:T(8,128)} %bitcast.385, f32[3,80,2048]{2,1,0:T(8,128)} %add.537.num_hbm, f32[3,64,2048]{2,1,0:T(8,128)} %bitcast.397, f32[3,16,256,128]{3,2,1,0:T(8,128)} %copy-done.2, ...), custom_call_target="tpu_custom_call" | custom-call | tf_op jit(solution)/shard_map/attend_back/pallas_call | solution.py:382
  384.9 3.1 reduce-scatter.9.cloned.1.call-done
  395.2 27.5 %attend_back.10 = (f32[192,2048]{1,0:T(8,128)}, f32[16,2048]{1,0:T(8,128)}) custom-call(f32[9,64,2048]{2,1,0:T(8,128)} %bitcast.367, f32[1,2048]{1,0:T(1,128)} %slice.630.valid_ref, f32[128,64]{1,0:T(8,128)} %bitcast.386, f32[3,80,2048]{2,1,0:T(8,128)} %add.537.num_hbm, f32[3,64,2048]{2,1,0:T(8,128)} %bitcast.398, f32[3,16,256,128]{3,2,1,0:T(8,128)} %copy-done.2, ...), custom_call_target="tpu_custom_call" | custom-call | tf_op jit(solution)/shard_map/attend_back/pallas_call | solution.py:382
  422.7 1.9 copy-done.29
  431.5 2.6 collective-permute-start.33
  435.0 26.4 %attend_back.11 = (f32[192,2048]{1,0:T(8,128)}, f32[16,2048]{1,0:T(8,128)}) custom-call(f32[9,64,2048]{2,1,0:T(8,128)} %bitcast.368, f32[1,2048]{1,0:T(1,128)} %slice.630.valid_ref, f32[128,64]{1,0:T(8,128)} %bitcast.387, f32[3,80,2048]{2,1,0:T(8,128)} %add.537.num_hbm, f32[3,64,2048]{2,1,0:T(8,128)} %bitcast.399, f32[3,16,256,128]{3,2,1,0:T(8,128)} %copy-done.2, ...), custom_call_target="tpu_custom_call" | custom-call | tf_op jit(solution)/shard_map/attend_back/pallas_call | solution.py:382
  464.2 2.0 collective-permute-start.35
  469.4 3.6 weights_of.4
  475.3 3.0 weights_of.5
  484.6 2.2 collective-permute-start.38
  486.8 12.7 %collective-permute-done.36 = f32[104,576]{0,1:T(8,128)S(1)} collective-permute-done((f32[104,576]{0,1:T(8,128)S(1)}, f32[104,576]{0,1:T(8,128)S(1)}, u32[]{:S(2)}, u32[]{:S(2)}) %collective-permute-start.36) | collective-permute-done | bytes 239648 | tf_op jit(solution)/shard_map/ppermute | solution.py:642
  499.6 6.5 %collective-permute-done.37 = f32[104,576]{0,1:T(8,128)S(1)} collective-permute-done((f32[104,576]{0,1:T(8,128)S(1)}, f32[104,576]{0,1:T(8,128)S(1)}, u32[]{:S(2)}, u32[]{:S(2)}) %collective-permute-start.37) | collective-permute-done | bytes 239648 | tf_op jit(solution)/shard_map/ppermute | solution.py:642
  506.1 5.5 collective-permute-done.38
  512.7 2.3 collective-permute-start.39
  516.6 5.2 collective-permute-done.41
  521.8 13.2 %collective-permute-done.40 = f32[104,576]{0,1:T(8,128)S(1)} collective-permute-done((f32[104,576]{0,1:T(8,128)S(1)}, f32[104,576]{0,1:T(8,128)S(1)}, u32[]{:S(2)}, u32[]{:S(2)}) %collective-permute-start.40) | collective-permute-done | bytes 239648 | tf_op jit(solution)/shard_map/ppermute | solution.py:642
  539.1 5.6 collective-permute-start.42
  546.8 2.1 collective-permute-start.43
  548.9 10.3 %collective-permute-done.42 = f32[576,256]{1,0:T(8,128)} collective-permute-done((f32[576,256]{1,0:T(8,128)S(1)}, f32[576,256]{1,0:T(8,128)}, u32[]{:S(2)}, u32[]{:S(2)}) %collective-permute-start.42) | collective-permute-done | bytes 589856 | tf_op jit(solution)/shard_map/ppermute | solution.py:642
  559.1 26.6 %collective-permute-start.44 = (f32[576,256]{1,0:T(8,128)}, f32[576,256]{1,0:T(8,128)}, u32[]{:S(2)}, u32[]{:S(2)}) collective-permute-start(f32[576,256]{1,0:T(8,128)} %get-tuple-element.402), channel_id=1, source_target_pairs={{0,6},{1,7},{2,0},{3,1},{4,2},{5,3},{6,4},{7,5},{8,14},{9,15},{10,... | collective-permute-start | bytes 1769480 | tf_op jit(solution)/shard_map/ppermute | solution.py:642
  585.8 3.7 copy-done.18
  589.4 4.7 copied.1
  594.2 2.1 slice.644
  596.2 3.2 slice.643
  599.5 4.6 copy-done.14
  604.0 4.7 widened.1
  610.5 2.2 pad_maximum_fusion.2.refs_0_
  612.8 2.6 collective-permute-start.48
  629.3 6.5 %rejoined.1 = (f32[768,768]{1,0:T(8,128)}, f32[768,768]{1,0:T(8,128)}, f32[768,768]{1,0:T(8,128)}) custom-call(s32[1]{0:T(128)} %bitcast.52.c_ref, f32[3,416,768]{2,1,0:T(8,128)} %pad_maximum_fusion.2.refs_0_, f32[3,416,768]{2,1,0:T(8,128)} %collective-permute-done.48.refs_1_), custom_call_target="tpu_custom_call" | custom-call | tf_op jit(solution)/shard_map/rejoined/pallas_call | solution.py:466
  (449 shorter events, 130.7 us)
Async XLA Ops:
  7.2 183.2 %copy-start = (bf16[768,768]{1,0:T(8,128)(2,1)S(1)}, bf16[768,768]{1,0:T(8,128)(2,1)}, u32[]{:S(2)}) copy-start(bf16[768,768]{1,0:T(8,128)(2,1)} %param.33) | copy-start | bytes 3538948
  7.2 313.6 %reduce-scatter.7.cloned.1.call-start = ((), (), s32[]{:S(2)}) async-start(), calls=%async_computation.4 | async-start | bytes 5898240
  15.6 6.7 %collective-permute-start.2 = (f32[584,256]{1,0:T(8,128)}, f32[584,256]{1,0:T(8,128)}, u32[]{:S(2)}, u32[]{:S(2)}) collective-permute-start(f32[584,256]{1,0:T(8,128)} %pad_maximum_fusion.27), channel_id=1, source_target_pairs={{0,1},{1,0},{2,3},{3,2},{4,5},{5,4},{6,7},{7,6},{8,9},{9,8},{10,11... | collective-permute-start | bytes 1794056 | tf_op jit(solution)/shard_map/ppermute | solution.py:642
  16.4 19.7 %collective-permute-start.1 = (f32[264,768]{1,0:T(8,128)S(1)}, f32[264,768]{1,0:T(8,128)}, u32[]{:S(2)}, u32[]{:S(2)}) collective-permute-start(f32[264,768]{1,0:T(8,128)S(1)} %select_maximum_fusion.1), channel_id=1, source_target_pairs={{2,0},{3,1},{4,2},{5,3},{6,4},{7,5},{10,8},{11,9},{12,10},{13,11},... | collective-permute-start | bytes 2433032 | tf_op jit(solution)/shard_map/ppermute | solution.py:642
  19.5 21.3 %collective-permute-start = (f32[264,768]{1,0:T(8,128)S(1)}, f32[264,768]{1,0:T(8,128)}, u32[]{:S(2)}, u32[]{:S(2)}) collective-permute-start(f32[264,768]{1,0:T(8,128)S(1)} %select_maximum_fusion.1), channel_id=1, source_target_pairs={{0,2},{1,3},{2,4},{3,5},{4,6},{5,7},{8,10},{9,11},{10,12},{11,13},... | collective-permute-start | bytes 2433032 | tf_op jit(solution)/shard_map/ppermute | solution.py:642
  22.2 97.5 %copy-start.17 = (f32[64,4,1,32]{0,3,2,1:T(8,128)}, f32[64,4,1,32]{0,3,2,1:T(8,128)S(1)}, u32[]{:S(2)}) copy-start(f32[64,4,1,32]{0,3,2,1:T(8,128)S(1)} %constant_dynamic-slice_fusion.26) | copy-start | bytes 98308
  43.9 3.2 collective-permute-start.5
  45.1 21.8 %collective-permute-start.3 = (f32[264,768]{1,0:T(8,128)}, f32[264,768]{1,0:T(8,128)S(1)}, u32[]{:S(2)}, u32[]{:S(2)}) collective-permute-start(f32[264,768]{1,0:T(8,128)} %collective-permute-done), channel_id=1, source_target_pairs={{2,4},{3,5},{4,6},{5,7},{10,12},{11,13},{12,14},{13,15},{18,20},{1... | collective-permute-start | bytes 2433032 | tf_op jit(solution)/shard_map/ppermute | solution.py:642
  46.4 20.5 %collective-permute-start.4 = (f32[264,768]{1,0:T(8,128)}, f32[264,768]{1,0:T(8,128)S(1)}, u32[]{:S(2)}, u32[]{:S(2)}) collective-permute-start(f32[264,768]{1,0:T(8,128)} %collective-permute-done.1), channel_id=1, source_target_pairs={{2,0},{3,1},{4,2},{5,3},{10,8},{11,9},{12,10},{13,11},{18,16},{19,... | collective-permute-start | bytes 2433032 | tf_op jit(solution)/shard_map/ppermute | solution.py:642
  69.7 3.1 collective-permute-start.8
  70.6 21.6 %collective-permute-start.6 = (f32[264,768]{1,0:T(8,128)S(1)}, f32[264,768]{1,0:T(8,128)S(1)}, u32[]{:S(2)}, u32[]{:S(2)}) collective-permute-start(f32[264,768]{1,0:T(8,128)S(1)} %collective-permute-done.3), channel_id=1, source_target_pairs={{4,6},{5,7},{12,14},{13,15},{20,22},{21,23},{28,30},{29,31}} | collective-permute-start | bytes 2433032 | tf_op jit(solution)/shard_map/ppermute | solution.py:642
  71.9 20.3 %collective-permute-start.7 = (f32[264,768]{1,0:T(8,128)S(1)}, f32[264,768]{1,0:T(8,128)S(1)}, u32[]{:S(2)}, u32[]{:S(2)}) collective-permute-start(f32[264,768]{1,0:T(8,128)S(1)} %collective-permute-done.4), channel_id=1, source_target_pairs={{2,0},{3,1},{10,8},{11,9},{18,16},{19,17},{26,24},{27,25}} | collective-permute-start | bytes 2433032 | tf_op jit(solution)/shard_map/ppermute | solution.py:642
  93.9 8.6 %collective-permute-start.9 = (f32[584,256]{1,0:T(8,128)S(1)}, f32[584,256]{1,0:T(8,128)S(1)}, u32[]{:S(2)}, u32[]{:S(2)}) collective-permute-start(f32[584,256]{1,0:T(8,128)S(1)} %pad_maximum_fusion.30), channel_id=1, source_target_pairs={{0,1},{1,0},{2,3},{3,2},{4,5},{5,4},{6,7},{7,6},{8,9},{9,8},{10,11... | collective-permute-start | bytes 1794056 | tf_op jit(solution)/shard_map/ppermute | solution.py:642
  119.8 36.5 %copy-start.3 = (f32[576,2048]{1,0:T(8,128)}, f32[576,2048]{1,0:T(8,128)S(1)}, u32[]{:S(2)}) copy-start(f32[576,2048]{1,0:T(8,128)S(1)} %slice.629) | copy-start | bytes 14155780
  157.5 4.1 collective-permute-start.10
  168.4 7.5 %collective-permute-start.14 = (f32[1024,384]{1,0:T(8,128)}, f32[1024,384]{1,0:T(8,128)}, u32[]{:S(2)}, u32[]{:S(2)}) collective-permute-start(f32[1024,384]{1,0:T(8,128)} %constant_dynamic-slice_fusion.16), channel_id=1, source_target_pairs={{0,1},{1,0},{2,3},{3,2},{4,5},{5,4},{6,7},{7,6},{8,9},{9,8},{10,11... | collective-permute-start | bytes 4718600 | tf_op jit(solution)/shard_map/ppermute | solution.py:642
  172.3 8.0 %collective-permute-start.13 = (f32[192,256]{1,0:T(8,128)S(1)}, f32[192,256]{1,0:T(8,128)S(1)}, u32[]{:S(2)}, u32[]{:S(2)}) collective-permute-start(f32[192,256]{1,0:T(8,128)S(1)} %get-tuple-element.549), channel_id=1, source_target_pairs={{0,6},{1,7},{2,0},{3,1},{4,2},{5,3},{6,4},{7,5},{8,14},{9,15},{10,... | collective-permute-start | bytes 589832 | tf_op jit(solution)/shard_map/ppermute | solution.py:642
  172.4 16.8 %collective-permute-start.12 = (f32[192,256]{1,0:T(8,128)S(1)}, f32[192,256]{1,0:T(8,128)S(1)}, u32[]{:S(2)}, u32[]{:S(2)}) collective-permute-start(f32[192,256]{1,0:T(8,128)S(1)} %get-tuple-element.550), channel_id=1, source_target_pairs={{0,4},{1,5},{2,6},{3,7},{4,0},{5,1},{6,2},{7,3},{8,12},{9,13},{10,... | collective-permute-start | bytes 589832 | tf_op jit(solution)/shard_map/ppermute | solution.py:642
  175.5 13.7 %collective-permute-start.11 = (f32[192,256]{1,0:T(8,128)S(1)}, f32[192,256]{1,0:T(8,128)S(1)}, u32[]{:S(2)}, u32[]{:S(2)}) collective-permute-start(f32[192,256]{1,0:T(8,128)S(1)} %get-tuple-element.551), channel_id=1, source_target_pairs={{0,2},{1,3},{2,4},{3,5},{4,6},{5,7},{6,0},{7,1},{8,10},{9,11},{10,... | collective-permute-start | bytes 589832 | tf_op jit(solution)/shard_map/ppermute | solution.py:642
  207.9 21.0 %copy-start.12 = (f32[256,768]{1,0:T(8,128)}, f32[256,768]{1,0:T(8,128)S(1)}, u32[]{:S(2)}) copy-start(f32[256,768]{1,0:T(8,128)S(1)} %subtract_multiply_fusion.pre_ref) | copy-start | bytes 2359300
  210.0 19.0 %copy-start.26 = (f32[768,256]{1,0:T(8,128)S(1)}, f32[768,256]{1,0:T(8,128)}, u32[]{:S(2)}) copy-start(f32[768,256]{1,0:T(8,128)} %pad_maximum_fusion.25.attn_ref) | copy-start | bytes 2359300
  212.3 16.6 %copy-start.24 = (f32[256,768]{1,0:T(8,128)S(1)}, f32[256,768]{1,0:T(8,128)}, u32[]{:S(2)}) copy-start(f32[256,768]{1,0:T(8,128)} %copy-done.23) | copy-start | bytes 2359300
  222.7 25.4 %collective-permute-start.18 = (f32[4,384,768]{2,1,0:T(8,128)}, f32[4,384,768]{2,1,0:T(8,128)}, u32[]{:S(2)}, u32[]{:S(2)}) collective-permute-start(f32[4,384,768]{2,1,0:T(8,128)} %get-tuple-element.286), channel_id=1, source_target_pairs={{0,1},{1,0},{2,3},{3,2},{4,5},{5,4},{6,7},{7,6},{8,9},{9,8},{10,11... | collective-permute-start | bytes 14155784 | tf_op jit(solution)/shard_map/ppermute | solution.py:642
  223.5 21.8 %collective-permute-start.15 = (f32[204,256]{1,0:T(8,128)S(1)}, f32[204,256]{1,0:T(8,128)S(1)}, u32[]{:S(2)}, u32[]{:S(2)}) collective-permute-start(f32[204,256]{1,0:T(8,128)S(1)} %get-tuple-element.270), channel_id=1, source_target_pairs={{0,2},{1,3},{2,4},{3,5},{4,6},{5,7},{6,0},{7,1},{8,10},{9,11},{10,... | collective-permute-start | bytes 626696 | tf_op jit(solution)/shard_map/ppermute | solution.py:642
  227.6 20.4 %collective-permute-start.16 = (f32[204,256]{1,0:T(8,128)S(1)}, f32[204,256]{1,0:T(8,128)S(1)}, u32[]{:S(2)}, u32[]{:S(2)}) collective-permute-start(f32[204,256]{1,0:T(8,128)S(1)} %get-tuple-element.271), channel_id=1, source_target_pairs={{0,4},{1,5},{2,6},{3,7},{4,0},{5,1},{6,2},{7,3},{8,12},{9,13},{10,... | collective-permute-start | bytes 626696 | tf_op jit(solution)/shard_map/ppermute | solution.py:642
  228.9 19.1 %collective-permute-start.17 = (f32[204,256]{1,0:T(8,128)S(1)}, f32[204,256]{1,0:T(8,128)S(1)}, u32[]{:S(2)}, u32[]{:S(2)}) collective-permute-start(f32[204,256]{1,0:T(8,128)S(1)} %get-tuple-element.272), channel_id=1, source_target_pairs={{0,6},{1,7},{2,0},{3,1},{4,2},{5,3},{6,4},{7,5},{8,14},{9,15},{10,... | collective-permute-start | bytes 626696 | tf_op jit(solution)/shard_map/ppermute | solution.py:642
  249.2 5.9 collective-permute-start.19
  256.5 131.5 %reduce-scatter.9.cloned.1.call-start = ((), (), s32[]{:S(2)}) async-start(), calls=%async_computation.5 | async-start | bytes 7864320
  256.7 29.4 %collective-permute-start.20 = (f32[4,512,768]{2,1,0:T(8,128)}, f32[4,512,768]{2,1,0:T(8,128)}, u32[]{:S(2)}, u32[]{:S(2)}) collective-permute-start(f32[4,512,768]{2,1,0:T(8,128)} %bitcast.393), channel_id=1, source_target_pairs={{0,1},{1,0},{2,3},{3,2},{4,5},{5,4},{6,7},{7,6},{8,9},{9,8},{10,11... | collective-permute-start | bytes 18874376 | tf_op jit(solution)/shard_map/ppermute | solution.py:642
  294.3 240.6 %all-gather.3.cloned.1.call-start = ((), (), s32[]{:S(2)}) async-start(), calls=%async_computation.2 | async-start | bytes 10616832 | tf_op jit(solution)/shard_map/all_gather | solution.py:810
  323.0 61.9 %collective-permute-start.27 = (f32[192,2048]{1,0:T(8,128)S(1)}, f32[192,2048]{1,0:T(8,128)S(1)}, u32[]{:S(2)}, u32[]{:S(2)}) collective-permute-start(f32[192,2048]{1,0:T(8,128)S(1)} %copy-done.28), channel_id=1, source_target_pairs={{0,1},{1,0},{2,3},{3,2},{4,5},{5,4},{6,7},{7,6},{8,9},{9,8},{10,11... | collective-permute-start | bytes 4718600 | tf_op jit(solution)/shard_map/ppermute | solution.py:642
  323.5 29.5 %collective-permute-start.21 = (f32[96,768]{1,0:T(8,128)}, f32[96,768]{1,0:T(8,128)}, u32[]{:S(2)}, u32[]{:S(2)}) collective-permute-start(f32[96,768]{1,0:T(8,128)} %get-tuple-element.309), channel_id=1, source_target_pairs={{0,2},{1,3},{2,4},{3,5},{4,6},{5,7},{6,0},{7,1},{8,10},{9,11},{10,... | collective-permute-start | bytes 884744 | tf_op jit(solution)/shard_map/ppermute | solution.py:642
  324.0 29.0 %collective-permute-start.22 = (f32[96,768]{1,0:T(8,128)}, f32[96,768]{1,0:T(8,128)}, u32[]{:S(2)}, u32[]{:S(2)}) collective-permute-start(f32[96,768]{1,0:T(8,128)} %get-tuple-element.310), channel_id=1, source_target_pairs={{0,4},{1,5},{2,6},{3,7},{4,0},{5,1},{6,2},{7,3},{8,12},{9,13},{10,... | collective-permute-start | bytes 884744 | tf_op jit(solution)/shard_map/ppermute | solution.py:642
  324.0 29.0 %collective-permute-start.23 = (f32[96,768]{1,0:T(8,128)S(1)}, f32[96,768]{1,0:T(8,128)}, u32[]{:S(2)}, u32[]{:S(2)}) collective-permute-start(f32[96,768]{1,0:T(8,128)S(1)} %get-tuple-element.311), channel_id=1, source_target_pairs={{0,6},{1,7},{2,0},{3,1},{4,2},{5,3},{6,4},{7,5},{8,14},{9,15},{10,... | collective-permute-start | bytes 884744 | tf_op jit(solution)/shard_map/ppermute | solution.py:642
  354.3 30.6 %collective-permute-start.26 = (f32[96,768]{1,0:T(8,128)S(1)}, f32[96,768]{1,0:T(8,128)}, u32[]{:S(2)}, u32[]{:S(2)}) collective-permute-start(f32[96,768]{1,0:T(8,128)S(1)} %add_add_fusion.2), channel_id=1, source_target_pairs={{0,6},{1,7},{2,0},{3,1},{4,2},{5,3},{6,4},{7,5},{8,14},{9,15},{10,... | collective-permute-start | bytes 884744 | tf_op jit(solution)/shard_map/ppermute | solution.py:642
  355.5 29.4 %collective-permute-start.25 = (f32[96,768]{1,0:T(8,128)S(1)}, f32[96,768]{1,0:T(8,128)}, u32[]{:S(2)}, u32[]{:S(2)}) collective-permute-start(f32[96,768]{1,0:T(8,128)S(1)} %add_add_fusion.2), channel_id=1, source_target_pairs={{0,4},{1,5},{2,6},{3,7},{4,0},{5,1},{6,2},{7,3},{8,12},{9,13},{10,... | collective-permute-start | bytes 884744 | tf_op jit(solution)/shard_map/ppermute | solution.py:642
  356.4 28.5 %collective-permute-start.24 = (f32[96,768]{1,0:T(8,128)S(1)}, f32[96,768]{1,0:T(8,128)}, u32[]{:S(2)}, u32[]{:S(2)}) collective-permute-start(f32[96,768]{1,0:T(8,128)S(1)} %add_add_fusion.2), channel_id=1, source_target_pairs={{0,2},{1,3},{2,4},{3,5},{4,6},{5,7},{6,0},{7,1},{8,10},{9,11},{10,... | collective-permute-start | bytes 884744 | tf_op jit(solution)/shard_map/ppermute | solution.py:642
  392.3 201.9 %all-gather.5.cloned.1.call-start = ((), (), s32[]{:S(2)}) async-start(), calls=%async_computation.3 | async-start | bytes 14155776 | tf_op jit(solution)/shard_map/all_gather | solution.py:810
  392.3 69.1 %collective-permute-start.28 = (f32[192,2048]{1,0:T(8,128)}, f32[192,2048]{1,0:T(8,128)}, u32[]{:S(2)}, u32[]{:S(2)}) collective-permute-start(f32[192,2048]{1,0:T(8,128)} %get-tuple-element.367.refs_0_), channel_id=1, source_target_pairs={{0,1},{1,0},{2,3},{3,2},{4,5},{5,4},{6,7},{7,6},{8,9},{9,8},{10,11... | collective-permute-start | bytes 4718600 | tf_op jit(solution)/shard_map/ppermute | solution.py:642
  393.1 35.3 %collective-permute-start.29 = (f32[128,768]{1,0:T(8,128)}, f32[128,768]{1,0:T(8,128)S(1)}, u32[]{:S(2)}, u32[]{:S(2)}) collective-permute-start(f32[128,768]{1,0:T(8,128)} %get-tuple-element.334), channel_id=1, source_target_pairs={{0,2},{1,3},{2,4},{3,5},{4,6},{5,7},{6,0},{7,1},{8,10},{9,11},{10,... | collective-permute-start | bytes 1179656 | tf_op jit(solution)/shard_map/ppermute | solution.py:642
  393.3 36.0 %collective-permute-start.30 = (f32[128,768]{1,0:T(8,128)}, f32[128,768]{1,0:T(8,128)}, u32[]{:S(2)}, u32[]{:S(2)}) collective-permute-start(f32[128,768]{1,0:T(8,128)} %get-tuple-element.335), channel_id=1, source_target_pairs={{0,4},{1,5},{2,6},{3,7},{4,0},{5,1},{6,2},{7,3},{8,12},{9,13},{10,... | collective-permute-start | bytes 1179656 | tf_op jit(solution)/shard_map/ppermute | solution.py:642
  394.5 34.8 %collective-permute-start.31 = (f32[128,768]{1,0:T(8,128)}, f32[128,768]{1,0:T(8,128)}, u32[]{:S(2)}, u32[]{:S(2)}) collective-permute-start(f32[128,768]{1,0:T(8,128)} %get-tuple-element.336), channel_id=1, source_target_pairs={{0,6},{1,7},{2,0},{3,1},{4,2},{5,3},{6,4},{7,5},{8,14},{9,15},{10,... | collective-permute-start | bytes 1179656 | tf_op jit(solution)/shard_map/ppermute | solution.py:642
  395.2 27.5 %copy-start.10 = (bf16[2048,384]{1,0:T(8,128)(2,1)S(1)}, bf16[2048,384]{1,0:T(8,128)(2,1)}, u32[]{:S(2)}) copy-start(bf16[2048,384]{1,0:T(8,128)(2,1)} %get-tuple-element.343.refs_3_) | copy-start | bytes 4718596
  395.2 27.5 %copy-start.11 = (bf16[2048,384]{1,0:T(8,128)(2,1)S(1)}, bf16[2048,384]{1,0:T(8,128)(2,1)}, u32[]{:S(2)}) copy-start(bf16[2048,384]{1,0:T(8,128)(2,1)} %get-tuple-element.342.refs_2_) | copy-start | bytes 4718596
  430.7 30.7 %collective-permute-start.34 = (f32[128,768]{1,0:T(8,128)S(1)}, f32[128,768]{1,0:T(8,128)}, u32[]{:S(2)}, u32[]{:S(2)}) collective-permute-start(f32[128,768]{1,0:T(8,128)S(1)} %add_add_fusion), channel_id=1, source_target_pairs={{0,6},{1,7},{2,0},{3,1},{4,2},{5,3},{6,4},{7,5},{8,14},{9,15},{10,... | collective-permute-start | bytes 1179656 | tf_op jit(solution)/shard_map/ppermute | solution.py:642
  431.5 30.0 %collective-permute-start.33 = (f32[128,768]{1,0:T(8,128)S(1)}, f32[128,768]{1,0:T(8,128)}, u32[]{:S(2)}, u32[]{:S(2)}) collective-permute-start(f32[128,768]{1,0:T(8,128)S(1)} %add_add_fusion), channel_id=1, source_target_pairs={{0,4},{1,5},{2,6},{3,7},{4,0},{5,1},{6,2},{7,3},{8,12},{9,13},{10,... | collective-permute-start | bytes 1179656 | tf_op jit(solution)/shard_map/ppermute | solution.py:642
  434.1 27.3 %collective-permute-start.32 = (f32[128,768]{1,0:T(8,128)S(1)}, f32[128,768]{1,0:T(8,128)}, u32[]{:S(2)}, u32[]{:S(2)}) collective-permute-start(f32[128,768]{1,0:T(8,128)S(1)} %add_add_fusion), channel_id=1, source_target_pairs={{0,2},{1,3},{2,4},{3,5},{4,6},{5,7},{6,0},{7,1},{8,10},{9,11},{10,... | collective-permute-start | bytes 1179656 | tf_op jit(solution)/shard_map/ppermute | solution.py:642
  464.2 10.3 %collective-permute-start.35 = (f32[192,2048]{1,0:T(8,128)}, f32[192,2048]{1,0:T(8,128)}, u32[]{:S(2)}, u32[]{:S(2)}) collective-permute-start(f32[192,2048]{1,0:T(8,128)} %get-tuple-element.374.refs_0_), channel_id=1, source_target_pairs={{0,1},{1,0},{2,3},{3,2},{4,5},{5,4},{6,7},{7,6},{8,9},{9,8},{10,11... | collective-permute-start | bytes 4718600 | tf_op jit(solution)/shard_map/ppermute | solution.py:642
  483.0 32.0 %copy-start.33 = (f32[192,1024]{1,0:T(8,128)S(1)}, f32[192,1024]{1,0:T(8,128)}, u32[]{:S(2)}) copy-start(f32[192,1024]{1,0:T(8,128)} %copy-done.32) | copy-start | bytes 2359300
  483.0 32.0 %copy-start.35 = (f32[192,1024]{1,0:T(8,128)S(1)}, f32[192,1024]{1,0:T(8,128)}, u32[]{:S(2)}) copy-start(f32[192,1024]{1,0:T(8,128)} %copy-done.34) | copy-start | bytes 2359300
  483.0 32.0 %copy-start.37 = (f32[192,1024]{1,0:T(8,128)S(1)}, f32[192,1024]{1,0:T(8,128)}, u32[]{:S(2)}) copy-start(f32[192,1024]{1,0:T(8,128)} %copy-done.36) | copy-start | bytes 2359300
  483.4 16.1 %collective-permute-start.36 = (f32[104,576]{0,1:T(8,128)S(1)}, f32[104,576]{0,1:T(8,128)S(1)}, u32[]{:S(2)}, u32[]{:S(2)}) collective-permute-start(f32[104,576]{0,1:T(8,128)S(1)} %get-tuple-element.387), channel_id=1, source_target_pairs={{0,8},{1,9},{2,10},{3,11},{4,12},{5,13},{6,14},{7,15},{8,16},{9,17... | collective-permute-start | bytes 718856 | tf_op jit(solution)/shard_map/ppermute | solution.py:642
  484.5 21.6 %collective-permute-start.37 = (f32[104,576]{0,1:T(8,128)S(1)}, f32[104,576]{0,1:T(8,128)S(1)}, u32[]{:S(2)}, u32[]{:S(2)}) collective-permute-start(f32[104,576]{0,1:T(8,128)S(1)} %get-tuple-element.388), channel_id=1, source_target_pairs={{0,16},{1,17},{2,18},{3,19},{4,20},{5,21},{6,22},{7,23},{8,24},{9,... | collective-permute-start | bytes 718856 | tf_op jit(solution)/shard_map/ppermute | solution.py:642
  484.6 27.0 %collective-permute-start.38 = (f32[104,576]{0,1:T(8,128)S(1)}, f32[104,576]{0,1:T(8,128)S(1)}, u32[]{:S(2)}, u32[]{:S(2)}) collective-permute-start(f32[104,576]{0,1:T(8,128)S(1)} %get-tuple-element.389), channel_id=1, source_target_pairs={{0,24},{1,25},{2,26},{3,27},{4,28},{5,29},{6,30},{7,31},{8,0},{9,1... | collective-permute-start | bytes 718856 | tf_op jit(solution)/shard_map/ppermute | solution.py:642
  511.7 10.0 %collective-permute-start.41 = (f32[104,576]{0,1:T(8,128)S(1)}, f32[104,576]{0,1:T(8,128)S(1)}, u32[]{:S(2)}, u32[]{:S(2)}) collective-permute-start(f32[104,576]{0,1:T(8,128)S(1)} %add_add_fusion.1), channel_id=1, source_target_pairs={{0,6},{1,7},{2,0},{3,1},{4,2},{5,3},{6,4},{7,5},{8,14},{9,15},{10,... | collective-permute-start | bytes 718856 | tf_op jit(solution)/shard_map/ppermute | solution.py:642
  512.5 22.4 %collective-permute-start.40 = (f32[104,576]{0,1:T(8,128)S(1)}, f32[104,576]{0,1:T(8,128)S(1)}, u32[]{:S(2)}, u32[]{:S(2)}) collective-permute-start(f32[104,576]{0,1:T(8,128)S(1)} %add_add_fusion.1), channel_id=1, source_target_pairs={{0,4},{1,5},{2,6},{3,7},{4,0},{5,1},{6,2},{7,3},{8,12},{9,13},{10,... | collective-permute-start | bytes 718856 | tf_op jit(solution)/shard_map/ppermute | solution.py:642
  512.7 22.2 %collective-permute-start.39 = (f32[104,576]{0,1:T(8,128)S(1)}, f32[104,576]{0,1:T(8,128)S(1)}, u32[]{:S(2)}, u32[]{:S(2)}) collective-permute-start(f32[104,576]{0,1:T(8,128)S(1)} %add_add_fusion.1), channel_id=1, source_target_pairs={{0,2},{1,3},{2,4},{3,5},{4,6},{5,7},{6,0},{7,1},{8,10},{9,11},{10,... | collective-permute-start | bytes 718856 | tf_op jit(solution)/shard_map/ppermute | solution.py:642
  539.1 20.0 %collective-permute-start.42 = (f32[576,256]{1,0:T(8,128)S(1)}, f32[576,256]{1,0:T(8,128)}, u32[]{:S(2)}, u32[]{:S(2)}) collective-permute-start(f32[576,256]{1,0:T(8,128)S(1)} %get-tuple-element.400), channel_id=1, source_target_pairs={{0,2},{1,3},{2,4},{3,5},{4,6},{5,7},{6,0},{7,1},{8,10},{9,11},{10,... | collective-permute-start | bytes 1769480 | tf_op jit(solution)/shard_map/ppermute | solution.py:642
  544.7 64.1 %collective-permute-start.47 = (f32[3,104,768]{2,1,0:T(8,128)S(1)}, f32[3,104,768]{2,1,0:T(8,128)S(1)}, u32[]{:S(2)}, u32[]{:S(2)}) collective-permute-start(f32[3,104,768]{2,1,0:T(8,128)S(1)} %pad_maximum_fusion.21), channel_id=1, source_target_pairs={{0,24},{1,25},{2,26},{3,27},{4,28},{5,29},{6,30},{7,31},{8,0},{9,1... | collective-permute-start | bytes 2875400 | tf_op jit(solution)/shard_map/ppermute | solution.py:642
  545.3 63.5 %collective-permute-start.46 = (f32[3,104,768]{2,1,0:T(8,128)S(1)}, f32[3,104,768]{2,1,0:T(8,128)S(1)}, u32[]{:S(2)}, u32[]{:S(2)}) collective-permute-start(f32[3,104,768]{2,1,0:T(8,128)S(1)} %pad_maximum_fusion.21), channel_id=1, source_target_pairs={{0,16},{1,17},{2,18},{3,19},{4,20},{5,21},{6,22},{7,23},{8,24},{9,... | collective-permute-start | bytes 2875400 | tf_op jit(solution)/shard_map/ppermute | solution.py:642
  546.8 62.0 %collective-permute-start.45 = (f32[3,104,768]{2,1,0:T(8,128)S(1)}, f32[3,104,768]{2,1,0:T(8,128)}, u32[]{:S(2)}, u32[]{:S(2)}) collective-permute-start(f32[3,104,768]{2,1,0:T(8,128)S(1)} %pad_maximum_fusion.21), channel_id=1, source_target_pairs={{0,8},{1,9},{2,10},{3,11},{4,12},{5,13},{6,14},{7,15},{8,16},{9,17... | collective-permute-start | bytes 2875400 | tf_op jit(solution)/shard_map/ppermute | solution.py:642
  546.8 62.0 %collective-permute-start.43 = (f32[576,256]{1,0:T(8,128)}, f32[576,256]{1,0:T(8,128)}, u32[]{:S(2)}, u32[]{:S(2)}) collective-permute-start(f32[576,256]{1,0:T(8,128)} %get-tuple-element.401), channel_id=1, source_target_pairs={{0,4},{1,5},{2,6},{3,7},{4,0},{5,1},{6,2},{7,3},{8,12},{9,13},{10,... | collective-permute-start | bytes 1769480 | tf_op jit(solution)/shard_map/ppermute | solution.py:642
  559.1 49.6 %collective-permute-start.44 = (f32[576,256]{1,0:T(8,128)}, f32[576,256]{1,0:T(8,128)}, u32[]{:S(2)}, u32[]{:S(2)}) collective-permute-start(f32[576,256]{1,0:T(8,128)} %get-tuple-element.402), channel_id=1, source_target_pairs={{0,6},{1,7},{2,0},{3,1},{4,2},{5,3},{6,4},{7,5},{8,14},{9,15},{10,... | collective-permute-start | bytes 1769480 | tf_op jit(solution)/shard_map/ppermute | solution.py:642
  612.8 15.4 %collective-permute-start.48 = (f32[3,416,768]{2,1,0:T(8,128)}, f32[3,416,768]{2,1,0:T(8,128)}, u32[]{:S(2)}, u32[]{:S(2)}) collective-permute-start(f32[3,416,768]{2,1,0:T(8,128)} %pad_maximum_fusion.2.refs_0_), channel_id=1, source_target_pairs={{0,1},{1,0},{2,3},{3,2},{4,5},{5,4},{6,7},{7,6},{8,9},{9,8},{10,11... | collective-permute-start | bytes 11501576 | tf_op jit(solution)/shard_map/ppermute | solution.py:642
  (77 other events, 314.7 us)
Sparse Core Ops, SparseCore 0:
  256.6 57.5 reduce-scatter.6
  317.8 70.1 reduce-scatter.8
  392.4 59.2 all-gather.2
  464.3 96.9 all-gather.4

commit v4 on v3

--- a/solution.py
+++ b/solution.py
@@ -242,7 +242,7 @@
     sq[...] = signs_of(q_ref[0], proj_ref[...])
     copies[1].wait()
     sk[...] = signs_of(k_ref[0], proj_ref[...])
-    for copy in copies[2:]:
+    for copy in copies[2:5]:
         copy.wait()
     da = da_ref[0]
     v = v_ref[0]
@@ -253,6 +253,7 @@
     xq[...] = stacked(dn, dd)
     xk[...] = stacked(v, valid_ref[...])
     dv[...] = jnp.zeros(dv.shape, F32)
+    copies[5].wait()
 
     @pl.loop(0, hashes)
     def _(g):
@@ -283,6 +284,8 @@
             gk[pl.ds(base, 8), c : c + CHUNK] = sign_grad(r, rows, low, phi, d) * (2.0 - 2.0 * s8 * s8)
 
     back = proj_ref[...].T
+    if part:
+        copies[6].wait()
     copies = [
         pltpu.make_async_copy(source.at[0], out_hbm.at[64 * i : 64 * i + 64], sems.at[i])
         for i, source in enumerate((q_ref, k_ref, v_ref))
@@ -923,21 +926,19 @@
     qkv, valid = chunks[: 3 * feats].reshape(3 * heads, HEAD_SIZE, width), chunks[3 * feats : 3 * feats + 1]
 
     num_part, conv, subsets = read(qkv, tab, proj, taps, groups, inner)
-    num, step = num_part, 1
-    while step < inner:
-        num = num + grid.send(num, C, lambda i: i ^ step)
-        step *= 2
-    lines, num = lax.optimization_barrier((lines, num))
+    half = groups * tokens
+    own_num = grid.add(grid.deal(num_part, C, dim=2), C, dim=2)
+    lines, own_num = lax.optimization_barrier((lines, own_num))
     x_line = jnp.stack(grid.by_index(lines, places))
-    half = groups * tokens
-    own_num, own_conv = (lax.dynamic_slice_in_dim(t, c * half, half, 2) for t in (num, conv))
+    num = grid.collect(grid.offer(own_num, C), C, 2)
+    own_conv = lax.dynamic_slice_in_dim(conv, c * half, half, 2)
     attn = own_num[:, :HEAD_SIZE] / (own_num[:, HEAD_SIZE : HEAD_SIZE + 1] + HASH_COUNT) + own_conv
     attn = grid.deal(attn.reshape(feats, half), Z, dim=1)
 
     rows = MODEL_WIDTH // inner
     x_line = x_line[:, :tokens].reshape(half, MODEL_WIDTH)
     x_half = parts_of(jnp.concatenate(grid.take(grid.deal(x_line, C, dim=1), C, dim=1)))
-    attn, x_half = lax.optimization_barrier((attn, x_half))
+    attn, x_half, num = lax.optimization_barrier((attn, x_half, num))
     attn_t = jnp.concatenate(grid.take(attn, Z, dim=1))
 
     subsets = subsets.reshape(heads * hashes, BUCKETS)

time: 653 us -> 651 us (level)
    ppermute x49 -> x50, waiting for transfers between devices: 93.3 us -> 88.3 us  [send(): return lax.ppermute(x, AXES, pairs)]
    ppermute x49 -> x50, starting transfers between devices: 84.8 us -> 84.9 us  [send(): return lax.ppermute(x, AXES, pairs)]
  transfers between devices with their start and end apart: 53 -> 54, of which waited for: 16 -> 15; matrix products, arithmetic and copies ran while one was open for 10% -> 11% of each run, Pallas kernels for 34% -> 34%
where the time goes in v4:
time: 651 us; the launch traced here: 642 us
  Pallas kernels  276 us (42%)
  waiting for transfers between devices  92.9 us (14%)
  starting transfers between devices  85.3 us (13%)
  local copies, waits for them, and re-layouts  73.9 us (11%)
  other arithmetic  63.2 us (10%)
  matrix products  26.4 us (4%)
  between operations  24.8 us (4%)
    pallas_call x6, Pallas kernels, attend_back(): pl.pallas_call(functools.partial(bwd_kernel, hashes, groups, inner, head,...  159 us
    ppermute x50, waiting for transfers between devices, send(): return lax.ppermute(x, AXES, pairs)  88.3 us
    ppermute x50, starting transfers between devices, send(): return lax.ppermute(x, AXES, pairs)  84.9 us
    unnamed x196, local copies, waits for them, and re-layouts  39.6 us
    pallas_call x4, Pallas kernels, fill(): pl.pallas_call(fill_kernel, grid=(heads, parts), in_specs=specs[:len(ins)...  39.3 us
    pallas_call x1, Pallas kernels, read(): pl.pallas_call(functools.partial(read_kernel, hashes, groups, inner), gri...  36.5 us
    dot_general x29, matrix products, contract(): lax.dot_general(a, b, (((i,), (j,)), ((), ())), preferred_element_type=F32)  26.4 us
    add x2, other arithmetic, reduce(): x = sum((yield from self.moving(C, blocks)))  13.3 us
  transfers between devices with their start and end apart: 54, of which 15 were waited for; matrix products, arithmetic and copies ran while one was open for 11% of the time, Pallas kernels for 34%

profile of v4, /device:TPU:25, one launch (start us, length us, event | category | flops | bytes accessed | tf_op | source)
XLA Modules:
  0.0 642.1 jit_solution(572085251856387792)
XLA Ops:
  16.4 3.2 collective-permute-start.1
  23.8 9.8 %fill.4.refs_0_ = f32[3,16,256,128]{3,2,1,0:T(8,128)S(1)} custom-call(f32[9,64,512]{2,1,0:T(8,128)S(1)} %bitcast.369, f32[9,64,512]{2,1,0:T(8,128)S(1)} %bitcast.370, f32[1,512]{1,0:T(1,128)S(1)} %fusion.85.valid_ref, f32[128,64]{1,0:T(8,128)S(1)} %bitcast.377), custom_call_target="tpu_custom_call" | custom-call | tf_op jit(solution)/shard_map/fill/pallas_call | solution.py:343
  36.1 4.8 collective-permute-done
  47.4 9.9 %fill.5.refs_0_ = f32[3,16,256,128]{3,2,1,0:T(8,128)S(1)} custom-call(f32[9,64,512]{2,1,0:T(8,128)S(1)} %bitcast.373, f32[9,64,512]{2,1,0:T(8,128)S(1)} %bitcast.374, f32[1,512]{1,0:T(1,128)S(1)} %fusion.84.valid_ref, f32[128,64]{1,0:T(8,128)S(1)} %bitcast.378, f32[3,16,256,128]{3,2,1,0:T(8,128)S(1)} %fill.4.refs_0_), custom_call_target="tpu_custom_call" | custom-call | tf_op jit(solution)/shard_map/fill/pallas_call | solution.py:343
  58.4 8.4 %collective-permute-done.3 = f32[264,768]{1,0:T(8,128)S(1)} collective-permute-done((f32[264,768]{1,0:T(8,128)}, f32[264,768]{1,0:T(8,128)S(1)}, u32[]{:S(2)}, u32[]{:S(2)}) %collective-permute-start.3) | collective-permute-done | bytes 811040 | tf_op jit(solution)/shard_map/ppermute | solution.py:645
  73.0 9.9 %fill.6.refs_0_ = f32[3,16,256,128]{3,2,1,0:T(8,128)S(1)} custom-call(f32[9,64,512]{2,1,0:T(8,128)S(1)} %bitcast.375, f32[9,64,512]{2,1,0:T(8,128)S(1)} %bitcast.376, f32[1,512]{1,0:T(1,128)S(1)} %fusion.83.valid_ref, f32[128,64]{1,0:T(8,128)S(1)} %bitcast.379, f32[3,16,256,128]{3,2,1,0:T(8,128)S(1)} %fill.5.refs_0_), custom_call_target="tpu_custom_call" | custom-call | tf_op jit(solution)/shard_map/fill/pallas_call | solution.py:343
  84.2 7.9 %collective-permute-done.6 = f32[264,768]{1,0:T(8,128)S(1)} collective-permute-done((f32[264,768]{1,0:T(8,128)S(1)}, f32[264,768]{1,0:T(8,128)S(1)}, u32[]{:S(2)}, u32[]{:S(2)}) %collective-permute-start.6) | collective-permute-done | bytes 811040 | tf_op jit(solution)/shard_map/ppermute | solution.py:645
  103.0 2.8 copy-done.9
  105.8 9.8 %fill.7.tab_ref.tab_hbm = f32[3,16,256,128]{3,2,1,0:T(8,128)S(1)} custom-call(f32[9,64,512]{2,1,0:T(8,128)S(1)} %bitcast.371, f32[9,64,512]{2,1,0:T(8,128)S(1)} %bitcast.372, f32[1,512]{1,0:T(1,128)S(1)} %fusion.82.valid_ref, f32[128,64]{1,0:T(8,128)S(1)} %bitcast.380, f32[3,16,256,128]{3,2,1,0:T(8,128)S(1)} %copy-done.9), custom_call_target="tpu_custom_call" | custom-call | tf_op jit(solution)/shard_map/fill/pallas_call | solution.py:343
  117.8 2.0 copy-done.50
  119.8 36.5 %read.1 = (f32[3,80,2048]{2,1,0:T(8,128)S(1)}, f32[3,64,2048]{2,1,0:T(8,128)S(1)}, f32[3,16,256]{2,1,0:T(8,128)S(1)}) custom-call(f32[9,64,2048]{2,1,0:T(8,128)S(1)} %bitcast.361, f32[9,64,2048]{2,1,0:T(8,128)S(1)} %bitcast.362, f32[3,16,256,128]{3,2,1,0:T(8,128)S(1)} %fill.7.tab_ref.tab_hbm, f32[128,64]{1,0:T(8,128)S(1)} %bitcast.381, ...), custom_call_target="tpu_custom_call" | custom-call | tf_op jit(solution)/shard_map/read/pallas_call | solution.py:359
  158.7 2.7 collective-permute-done.10
  161.4 2.3 dynamic-slice_add_fusion
  164.7 1.7 copy-done.44
  171.4 3.1 collective-permute-start.12
  174.9 1.6 broadcast_select_fusion.1
  180.7 2.1 fusion.2
  182.9 5.3 collective-permute-done.12
  192.5 1.9 fusion.98
  201.0 1.9 fusion.hidden_ref
  203.0 1.8 fusion.9
  208.7 2.4 copy.72
  212.5 1.9 copy-done.7
  214.4 7.0 %outer_blocks.1 = (f32[4,384,768]{2,1,0:T(8,128)S(1)}, f32[4,384,768]{2,1,0:T(8,128)}) custom-call(s32[1]{0:T(128)} %bitcast.52.c_ref, f32[256,3072]{1,0:T(8,128)S(1)} %copy-done.7, f32[256,768]{1,0:T(8,128)S(1)} %get-tuple-element.278.second_ref.b_ref), custom_call_target="tpu_custom_call" | custom-call | tf_op jit(solution)/shard_map/outer_blocks/pallas_call | solution.py:522
  222.2 4.1 collective-permute-start.16
  228.9 9.8 %outer_rows.1 = (f32[2048,768]{1,0:T(8,128)S(1)}, f32[2048,768]{1,0:T(8,128)S(1)}) custom-call(s32[1]{0:T(128)} %bitcast.52.c_ref, f32[256,768]{1,0:T(8,128)S(1)} %get-tuple-element.274.first_ref, f32[256,3072]{1,0:T(8,128)S(1)} %copy-done.5, f32[768,256]{1,0:T(8,128)S(1)} %copy-done.26, f32[256,768]{1,0:T(8,128)S(1)} %subtract_multiply_fusion.pre_ref, ...), custom_call_target="tpu_custom_call" | custom-call | tf_op jit(solution)/shard_map/outer_rows/pallas_call | solution.py:609
  238.7 2.7 copy-done.25
  241.4 2.6 copy-done.43
  244.0 2.8 collective-permute-done.17
  248.8 5.0 add.599
  257.6 27.1 %attend_back.6 = (f32[192,2048]{1,0:T(8,128)}, f32[16,2048]{1,0:T(8,128)}) custom-call(f32[9,64,2048]{2,1,0:T(8,128)} %bitcast.363, f32[1,2048]{1,0:T(1,128)} %slice.630.valid_ref, f32[128,64]{1,0:T(8,128)} %bitcast.382, f32[3,80,2048]{2,1,0:T(8,128)} %pad_maximum_fusion.10.num_hbm, f32[3,64,2048]{2,1,0:T(8,128)} %bitcast.394, ...), custom_call_target="tpu_custom_call" | custom-call | tf_op jit(solution)/shard_map/attend_back/pallas_call | solution.py:385
  284.7 8.2 %add.600 = f32[4,512,768]{2,1,0:T(8,128)} add(f32[4,512,768]{2,1,0:T(8,128)} %bitcast.389, f32[4,512,768]{2,1,0:T(8,128)} %collective-permute-done.21) | non-fusion elementwise | flops 1572864 | bytes 18874368 | tf_op jit(solution)/shard_map/add | solution.py:759
  293.0 25.7 %attend_back.7 = (f32[192,2048]{1,0:T(8,128)}, f32[16,2048]{1,0:T(8,128)}) custom-call(f32[9,64,2048]{2,1,0:T(8,128)} %bitcast.364, f32[1,2048]{1,0:T(1,128)} %slice.630.valid_ref, f32[128,64]{1,0:T(8,128)} %bitcast.383, f32[3,80,2048]{2,1,0:T(8,128)} %pad_maximum_fusion.10.num_hbm, f32[3,64,2048]{2,1,0:T(8,128)} %bitcast.395, ...), custom_call_target="tpu_custom_call" | custom-call | tf_op jit(solution)/shard_map/attend_back/pallas_call | solution.py:385
  318.8 2.2 dynamic-slice_bitcast_fusion.20
  323.7 27.2 %attend_back.8 = (f32[192,2048]{1,0:T(8,128)}, f32[16,2048]{1,0:T(8,128)}) custom-call(f32[9,64,2048]{2,1,0:T(8,128)} %bitcast.365, f32[1,2048]{1,0:T(1,128)} %slice.630.valid_ref, f32[128,64]{1,0:T(8,128)} %bitcast.384, f32[3,80,2048]{2,1,0:T(8,128)} %pad_maximum_fusion.10.num_hbm, f32[3,64,2048]{2,1,0:T(8,128)} %bitcast.396, ...), custom_call_target="tpu_custom_call" | custom-call | tf_op jit(solution)/shard_map/attend_back/pallas_call | solution.py:385
  354.2 2.2 collective-permute-start.25
  356.4 25.8 %attend_back.9 = (f32[192,2048]{1,0:T(8,128)}, f32[16,2048]{1,0:T(8,128)}) custom-call(f32[9,64,2048]{2,1,0:T(8,128)} %bitcast.366, f32[1,2048]{1,0:T(1,128)} %slice.630.valid_ref, f32[128,64]{1,0:T(8,128)} %bitcast.385, f32[3,80,2048]{2,1,0:T(8,128)} %pad_maximum_fusion.10.num_hbm, f32[3,64,2048]{2,1,0:T(8,128)} %bitcast.397, ...), custom_call_target="tpu_custom_call" | custom-call | tf_op jit(solution)/shard_map/attend_back/pallas_call | solution.py:385
  382.3 4.5 reduce-scatter.9.cloned.1.call-done
  394.0 27.3 %attend_back.10 = (f32[192,2048]{1,0:T(8,128)}, f32[16,2048]{1,0:T(8,128)}) custom-call(f32[9,64,2048]{2,1,0:T(8,128)} %bitcast.367, f32[1,2048]{1,0:T(1,128)} %slice.630.valid_ref, f32[128,64]{1,0:T(8,128)} %bitcast.386, f32[3,80,2048]{2,1,0:T(8,128)} %pad_maximum_fusion.10.num_hbm, f32[3,64,2048]{2,1,0:T(8,128)} %bitcast.398, ...), custom_call_target="tpu_custom_call" | custom-call | tf_op jit(solution)/shard_map/attend_back/pallas_call | solution.py:385
  421.3 1.9 copy-done.29
  430.1 2.3 collective-permute-start.34
  433.7 25.7 %attend_back.11 = (f32[192,2048]{1,0:T(8,128)}, f32[16,2048]{1,0:T(8,128)}) custom-call(f32[9,64,2048]{2,1,0:T(8,128)} %bitcast.368, f32[1,2048]{1,0:T(1,128)} %slice.630.valid_ref, f32[128,64]{1,0:T(8,128)} %bitcast.387, f32[3,80,2048]{2,1,0:T(8,128)} %pad_maximum_fusion.10.num_hbm, f32[3,64,2048]{2,1,0:T(8,128)} %bitcast.399, ...), custom_call_target="tpu_custom_call" | custom-call | tf_op jit(solution)/shard_map/attend_back/pallas_call | solution.py:385
  467.1 3.6 weights_of.4
  472.9 3.0 weights_of.5
  482.5 1.9 collective-permute-start.39
  484.4 12.7 %collective-permute-done.37 = f32[104,576]{0,1:T(8,128)S(1)} collective-permute-done((f32[104,576]{0,1:T(8,128)S(1)}, f32[104,576]{0,1:T(8,128)S(1)}, u32[]{:S(2)}, u32[]{:S(2)}) %collective-permute-start.37) | collective-permute-done | bytes 239648 | tf_op jit(solution)/shard_map/ppermute | solution.py:645
  497.2 6.4 collective-permute-done.38
  503.6 6.1 collective-permute-done.39
  511.4 1.9 collective-permute-start.40
  514.9 4.5 collective-permute-done.42
  519.4 13.8 %collective-permute-done.41 = f32[104,576]{0,1:T(8,128)S(1)} collective-permute-done((f32[104,576]{0,1:T(8,128)S(1)}, f32[104,576]{0,1:T(8,128)S(1)}, u32[]{:S(2)}, u32[]{:S(2)}) %collective-permute-start.41) | collective-permute-done | bytes 239648 | tf_op jit(solution)/shard_map/ppermute | solution.py:645
  537.4 5.8 collective-permute-start.43
  545.5 1.8 collective-permute-start.44
  547.3 10.3 %collective-permute-done.43 = f32[576,256]{1,0:T(8,128)} collective-permute-done((f32[576,256]{1,0:T(8,128)S(1)}, f32[576,256]{1,0:T(8,128)}, u32[]{:S(2)}, u32[]{:S(2)}) %collective-permute-start.43) | collective-permute-done | bytes 589856 | tf_op jit(solution)/shard_map/ppermute | solution.py:645
  557.6 26.6 %collective-permute-start.45 = (f32[576,256]{1,0:T(8,128)}, f32[576,256]{1,0:T(8,128)}, u32[]{:S(2)}, u32[]{:S(2)}) collective-permute-start(f32[576,256]{1,0:T(8,128)} %get-tuple-element.404), channel_id=1, source_target_pairs={{0,6},{1,7},{2,0},{3,1},{4,2},{5,3},{6,4},{7,5},{8,14},{9,15},{10,... | collective-permute-start | bytes 1769480 | tf_op jit(solution)/shard_map/ppermute | solution.py:645
  584.2 3.7 copy-done.18
  587.9 4.7 copied.1
  592.6 2.1 slice.644
  594.7 3.2 slice.643
  597.9 4.6 copy-done.14
  602.5 4.7 widened.1
  609.0 2.2 pad_maximum_fusion.2.refs_0_
  611.2 2.3 collective-permute-start.49
  627.5 6.5 %rejoined.1 = (f32[768,768]{1,0:T(8,128)}, f32[768,768]{1,0:T(8,128)}, f32[768,768]{1,0:T(8,128)}) custom-call(s32[1]{0:T(128)} %bitcast.52.c_ref, f32[3,416,768]{2,1,0:T(8,128)} %pad_maximum_fusion.2.refs_0_, f32[3,416,768]{2,1,0:T(8,128)} %collective-permute-done.49.refs_1_), custom_call_target="tpu_custom_call" | custom-call | tf_op jit(solution)/shard_map/rejoined/pallas_call | solution.py:469
  (454 shorter events, 136.8 us)
Async XLA Ops:
  7.2 182.1 %copy-start = (bf16[768,768]{1,0:T(8,128)(2,1)S(1)}, bf16[768,768]{1,0:T(8,128)(2,1)}, u32[]{:S(2)}) copy-start(bf16[768,768]{1,0:T(8,128)(2,1)} %param.33) | copy-start | bytes 3538948
  7.2 311.6 %reduce-scatter.7.cloned.1.call-start = ((), (), s32[]{:S(2)}) async-start(), calls=%async_computation.4 | async-start | bytes 5898240
  15.6 6.7 %collective-permute-start.2 = (f32[584,256]{1,0:T(8,128)}, f32[584,256]{1,0:T(8,128)}, u32[]{:S(2)}, u32[]{:S(2)}) collective-permute-start(f32[584,256]{1,0:T(8,128)} %pad_maximum_fusion.28), channel_id=1, source_target_pairs={{0,1},{1,0},{2,3},{3,2},{4,5},{5,4},{6,7},{7,6},{8,9},{9,8},{10,11... | collective-permute-start | bytes 1794056 | tf_op jit(solution)/shard_map/ppermute | solution.py:645
  16.4 19.7 %collective-permute-start.1 = (f32[264,768]{1,0:T(8,128)S(1)}, f32[264,768]{1,0:T(8,128)}, u32[]{:S(2)}, u32[]{:S(2)}) collective-permute-start(f32[264,768]{1,0:T(8,128)S(1)} %select_maximum_fusion.1), channel_id=1, source_target_pairs={{2,0},{3,1},{4,2},{5,3},{6,4},{7,5},{10,8},{11,9},{12,10},{13,11},... | collective-permute-start | bytes 2433032 | tf_op jit(solution)/shard_map/ppermute | solution.py:645
  19.5 21.3 %collective-permute-start = (f32[264,768]{1,0:T(8,128)S(1)}, f32[264,768]{1,0:T(8,128)}, u32[]{:S(2)}, u32[]{:S(2)}) collective-permute-start(f32[264,768]{1,0:T(8,128)S(1)} %select_maximum_fusion.1), channel_id=1, source_target_pairs={{0,2},{1,3},{2,4},{3,5},{4,6},{5,7},{8,10},{9,11},{10,12},{11,13},... | collective-permute-start | bytes 2433032 | tf_op jit(solution)/shard_map/ppermute | solution.py:645
  22.2 97.5 %copy-start.17 = (f32[64,4,1,32]{0,3,2,1:T(8,128)}, f32[64,4,1,32]{0,3,2,1:T(8,128)S(1)}, u32[]{:S(2)}) copy-start(f32[64,4,1,32]{0,3,2,1:T(8,128)S(1)} %constant_dynamic-slice_fusion.26) | copy-start | bytes 98308
  43.9 3.2 collective-permute-start.5
  45.1 21.8 %collective-permute-start.3 = (f32[264,768]{1,0:T(8,128)}, f32[264,768]{1,0:T(8,128)S(1)}, u32[]{:S(2)}, u32[]{:S(2)}) collective-permute-start(f32[264,768]{1,0:T(8,128)} %collective-permute-done), channel_id=1, source_target_pairs={{2,4},{3,5},{4,6},{5,7},{10,12},{11,13},{12,14},{13,15},{18,20},{1... | collective-permute-start | bytes 2433032 | tf_op jit(solution)/shard_map/ppermute | solution.py:645
  46.4 20.5 %collective-permute-start.4 = (f32[264,768]{1,0:T(8,128)}, f32[264,768]{1,0:T(8,128)S(1)}, u32[]{:S(2)}, u32[]{:S(2)}) collective-permute-start(f32[264,768]{1,0:T(8,128)} %collective-permute-done.1), channel_id=1, source_target_pairs={{2,0},{3,1},{4,2},{5,3},{10,8},{11,9},{12,10},{13,11},{18,16},{19,... | collective-permute-start | bytes 2433032 | tf_op jit(solution)/shard_map/ppermute | solution.py:645
  69.7 3.1 collective-permute-start.8
  70.6 21.6 %collective-permute-start.6 = (f32[264,768]{1,0:T(8,128)S(1)}, f32[264,768]{1,0:T(8,128)S(1)}, u32[]{:S(2)}, u32[]{:S(2)}) collective-permute-start(f32[264,768]{1,0:T(8,128)S(1)} %collective-permute-done.3), channel_id=1, source_target_pairs={{4,6},{5,7},{12,14},{13,15},{20,22},{21,23},{28,30},{29,31}} | collective-permute-start | bytes 2433032 | tf_op jit(solution)/shard_map/ppermute | solution.py:645
  71.9 20.3 %collective-permute-start.7 = (f32[264,768]{1,0:T(8,128)S(1)}, f32[264,768]{1,0:T(8,128)S(1)}, u32[]{:S(2)}, u32[]{:S(2)}) collective-permute-start(f32[264,768]{1,0:T(8,128)S(1)} %collective-permute-done.4), channel_id=1, source_target_pairs={{2,0},{3,1},{10,8},{11,9},{18,16},{19,17},{26,24},{27,25}} | collective-permute-start | bytes 2433032 | tf_op jit(solution)/shard_map/ppermute | solution.py:645
  93.9 8.6 %collective-permute-start.9 = (f32[584,256]{1,0:T(8,128)S(1)}, f32[584,256]{1,0:T(8,128)S(1)}, u32[]{:S(2)}, u32[]{:S(2)}) collective-permute-start(f32[584,256]{1,0:T(8,128)S(1)} %pad_maximum_fusion.31), channel_id=1, source_target_pairs={{0,1},{1,0},{2,3},{3,2},{4,5},{5,4},{6,7},{7,6},{8,9},{9,8},{10,11... | collective-permute-start | bytes 1794056 | tf_op jit(solution)/shard_map/ppermute | solution.py:645
  119.8 36.5 %copy-start.3 = (f32[576,2048]{1,0:T(8,128)}, f32[576,2048]{1,0:T(8,128)S(1)}, u32[]{:S(2)}) copy-start(f32[576,2048]{1,0:T(8,128)S(1)} %slice.629) | copy-start | bytes 14155780
  158.5 2.9 collective-permute-start.10
  164.2 10.6 %collective-permute-start.15 = (f32[3,80,1024]{2,1,0:T(8,128)}, f32[3,80,1024]{2,1,0:T(8,128)}, u32[]{:S(2)}, u32[]{:S(2)}) collective-permute-start(f32[3,80,1024]{2,1,0:T(8,128)} %dynamic-slice_add_fusion), channel_id=1, source_target_pairs={{0,1},{1,0},{2,3},{3,2},{4,5},{5,4},{6,7},{7,6},{8,9},{9,8},{10,11... | collective-permute-start | bytes 2949128 | tf_op jit(solution)/shard_map/ppermute | solution.py:645
  167.6 10.3 %collective-permute-start.14 = (f32[1024,384]{1,0:T(8,128)}, f32[1024,384]{1,0:T(8,128)}, u32[]{:S(2)}, u32[]{:S(2)}) collective-permute-start(f32[1024,384]{1,0:T(8,128)} %constant_dynamic-slice_fusion.16), channel_id=1, source_target_pairs={{0,1},{1,0},{2,3},{3,2},{4,5},{5,4},{6,7},{7,6},{8,9},{9,8},{10,11... | collective-permute-start | bytes 4718600 | tf_op jit(solution)/shard_map/ppermute | solution.py:645
  171.3 11.6 %collective-permute-start.13 = (f32[192,256]{1,0:T(8,128)S(1)}, f32[192,256]{1,0:T(8,128)S(1)}, u32[]{:S(2)}, u32[]{:S(2)}) collective-permute-start(f32[192,256]{1,0:T(8,128)S(1)} %get-tuple-element.553), channel_id=1, source_target_pairs={{0,6},{1,7},{2,0},{3,1},{4,2},{5,3},{6,4},{7,5},{8,14},{9,15},{10,... | collective-permute-start | bytes 589832 | tf_op jit(solution)/shard_map/ppermute | solution.py:645
  171.4 16.8 %collective-permute-start.12 = (f32[192,256]{1,0:T(8,128)S(1)}, f32[192,256]{1,0:T(8,128)S(1)}, u32[]{:S(2)}, u32[]{:S(2)}) collective-permute-start(f32[192,256]{1,0:T(8,128)S(1)} %get-tuple-element.554), channel_id=1, source_target_pairs={{0,4},{1,5},{2,6},{3,7},{4,0},{5,1},{6,2},{7,3},{8,12},{9,13},{10,... | collective-permute-start | bytes 589832 | tf_op jit(solution)/shard_map/ppermute | solution.py:645
  174.5 13.7 %collective-permute-start.11 = (f32[192,256]{1,0:T(8,128)S(1)}, f32[192,256]{1,0:T(8,128)S(1)}, u32[]{:S(2)}, u32[]{:S(2)}) collective-permute-start(f32[192,256]{1,0:T(8,128)S(1)} %get-tuple-element.555), channel_id=1, source_target_pairs={{0,2},{1,3},{2,4},{3,5},{4,6},{5,7},{6,0},{7,1},{8,10},{9,11},{10,... | collective-permute-start | bytes 589832 | tf_op jit(solution)/shard_map/ppermute | solution.py:645
  206.7 21.0 %copy-start.12 = (f32[256,768]{1,0:T(8,128)}, f32[256,768]{1,0:T(8,128)S(1)}, u32[]{:S(2)}) copy-start(f32[256,768]{1,0:T(8,128)S(1)} %subtract_multiply_fusion.pre_ref) | copy-start | bytes 2359300
  208.7 19.0 %copy-start.26 = (f32[768,256]{1,0:T(8,128)S(1)}, f32[768,256]{1,0:T(8,128)}, u32[]{:S(2)}) copy-start(f32[768,256]{1,0:T(8,128)} %pad_maximum_fusion.26.attn_ref) | copy-start | bytes 2359300
  221.4 25.4 %collective-permute-start.19 = (f32[4,384,768]{2,1,0:T(8,128)}, f32[4,384,768]{2,1,0:T(8,128)}, u32[]{:S(2)}, u32[]{:S(2)}) collective-permute-start(f32[4,384,768]{2,1,0:T(8,128)} %get-tuple-element.287), channel_id=1, source_target_pairs={{0,1},{1,0},{2,3},{3,2},{4,5},{5,4},{6,7},{7,6},{8,9},{9,8},{10,11... | collective-permute-start | bytes 14155784 | tf_op jit(solution)/shard_map/ppermute | solution.py:645
  222.2 21.8 %collective-permute-start.16 = (f32[204,256]{1,0:T(8,128)S(1)}, f32[204,256]{1,0:T(8,128)S(1)}, u32[]{:S(2)}, u32[]{:S(2)}) collective-permute-start(f32[204,256]{1,0:T(8,128)S(1)} %get-tuple-element.271), channel_id=1, source_target_pairs={{0,2},{1,3},{2,4},{3,5},{4,6},{5,7},{6,0},{7,1},{8,10},{9,11},{10,... | collective-permute-start | bytes 626696 | tf_op jit(solution)/shard_map/ppermute | solution.py:645
  226.3 20.4 %collective-permute-start.17 = (f32[204,256]{1,0:T(8,128)S(1)}, f32[204,256]{1,0:T(8,128)S(1)}, u32[]{:S(2)}, u32[]{:S(2)}) collective-permute-start(f32[204,256]{1,0:T(8,128)S(1)} %get-tuple-element.272), channel_id=1, source_target_pairs={{0,4},{1,5},{2,6},{3,7},{4,0},{5,1},{6,2},{7,3},{8,12},{9,13},{10,... | collective-permute-start | bytes 626696 | tf_op jit(solution)/shard_map/ppermute | solution.py:645
  227.7 19.1 %collective-permute-start.18 = (f32[204,256]{1,0:T(8,128)S(1)}, f32[204,256]{1,0:T(8,128)S(1)}, u32[]{:S(2)}, u32[]{:S(2)}) collective-permute-start(f32[204,256]{1,0:T(8,128)S(1)} %get-tuple-element.273), channel_id=1, source_target_pairs={{0,6},{1,7},{2,0},{3,1},{4,2},{5,3},{6,4},{7,5},{8,14},{9,15},{10,... | collective-permute-start | bytes 626696 | tf_op jit(solution)/shard_map/ppermute | solution.py:645
  247.9 5.9 collective-permute-start.20
  255.3 131.5 %reduce-scatter.9.cloned.1.call-start = ((), (), s32[]{:S(2)}) async-start(), calls=%async_computation.5 | async-start | bytes 7864320
  255.5 29.2 %collective-permute-start.21 = (f32[4,512,768]{2,1,0:T(8,128)}, f32[4,512,768]{2,1,0:T(8,128)}, u32[]{:S(2)}, u32[]{:S(2)}) collective-permute-start(f32[4,512,768]{2,1,0:T(8,128)} %bitcast.393), channel_id=1, source_target_pairs={{0,1},{1,0},{2,3},{3,2},{4,5},{5,4},{6,7},{7,6},{8,9},{9,8},{10,11... | collective-permute-start | bytes 18874376 | tf_op jit(solution)/shard_map/ppermute | solution.py:645
  292.9 240.3 %all-gather.3.cloned.1.call-start = ((), (), s32[]{:S(2)}) async-start(), calls=%async_computation.2 | async-start | bytes 10616832 | tf_op jit(solution)/shard_map/all_gather | solution.py:813
  321.0 61.2 %collective-permute-start.28 = (f32[192,2048]{1,0:T(8,128)S(1)}, f32[192,2048]{1,0:T(8,128)S(1)}, u32[]{:S(2)}, u32[]{:S(2)}) collective-permute-start(f32[192,2048]{1,0:T(8,128)S(1)} %copy-done.28), channel_id=1, source_target_pairs={{0,1},{1,0},{2,3},{3,2},{4,5},{5,4},{6,7},{7,6},{8,9},{9,8},{10,11... | collective-permute-start | bytes 4718600 | tf_op jit(solution)/shard_map/ppermute | solution.py:645
  321.6 29.3 %collective-permute-start.22 = (f32[96,768]{1,0:T(8,128)}, f32[96,768]{1,0:T(8,128)}, u32[]{:S(2)}, u32[]{:S(2)}) collective-permute-start(f32[96,768]{1,0:T(8,128)} %get-tuple-element.311), channel_id=1, source_target_pairs={{0,2},{1,3},{2,4},{3,5},{4,6},{5,7},{6,0},{7,1},{8,10},{9,11},{10,... | collective-permute-start | bytes 884744 | tf_op jit(solution)/shard_map/ppermute | solution.py:645
  322.1 28.8 %collective-permute-start.23 = (f32[96,768]{1,0:T(8,128)}, f32[96,768]{1,0:T(8,128)}, u32[]{:S(2)}, u32[]{:S(2)}) collective-permute-start(f32[96,768]{1,0:T(8,128)} %get-tuple-element.312), channel_id=1, source_target_pairs={{0,4},{1,5},{2,6},{3,7},{4,0},{5,1},{6,2},{7,3},{8,12},{9,13},{10,... | collective-permute-start | bytes 884744 | tf_op jit(solution)/shard_map/ppermute | solution.py:645
  322.1 28.8 %collective-permute-start.24 = (f32[96,768]{1,0:T(8,128)S(1)}, f32[96,768]{1,0:T(8,128)}, u32[]{:S(2)}, u32[]{:S(2)}) collective-permute-start(f32[96,768]{1,0:T(8,128)S(1)} %get-tuple-element.313), channel_id=1, source_target_pairs={{0,6},{1,7},{2,0},{3,1},{4,2},{5,3},{6,4},{7,5},{8,14},{9,15},{10,... | collective-permute-start | bytes 884744 | tf_op jit(solution)/shard_map/ppermute | solution.py:645
  352.1 30.1 %collective-permute-start.27 = (f32[96,768]{1,0:T(8,128)S(1)}, f32[96,768]{1,0:T(8,128)}, u32[]{:S(2)}, u32[]{:S(2)}) collective-permute-start(f32[96,768]{1,0:T(8,128)S(1)} %add_add_fusion.2), channel_id=1, source_target_pairs={{0,6},{1,7},{2,0},{3,1},{4,2},{5,3},{6,4},{7,5},{8,14},{9,15},{10,... | collective-permute-start | bytes 884744 | tf_op jit(solution)/shard_map/ppermute | solution.py:645
  353.4 28.9 %collective-permute-start.26 = (f32[96,768]{1,0:T(8,128)S(1)}, f32[96,768]{1,0:T(8,128)}, u32[]{:S(2)}, u32[]{:S(2)}) collective-permute-start(f32[96,768]{1,0:T(8,128)S(1)} %add_add_fusion.2), channel_id=1, source_target_pairs={{0,4},{1,5},{2,6},{3,7},{4,0},{5,1},{6,2},{7,3},{8,12},{9,13},{10,... | collective-permute-start | bytes 884744 | tf_op jit(solution)/shard_map/ppermute | solution.py:645
  354.2 28.0 %collective-permute-start.25 = (f32[96,768]{1,0:T(8,128)S(1)}, f32[96,768]{1,0:T(8,128)}, u32[]{:S(2)}, u32[]{:S(2)}) collective-permute-start(f32[96,768]{1,0:T(8,128)S(1)} %add_add_fusion.2), channel_id=1, source_target_pairs={{0,2},{1,3},{2,4},{3,5},{4,6},{5,7},{6,0},{7,1},{8,10},{9,11},{10,... | collective-permute-start | bytes 884744 | tf_op jit(solution)/shard_map/ppermute | solution.py:645
  391.1 201.6 %all-gather.5.cloned.1.call-start = ((), (), s32[]{:S(2)}) async-start(), calls=%async_computation.3 | async-start | bytes 14155776 | tf_op jit(solution)/shard_map/all_gather | solution.py:813
  391.1 68.3 %collective-permute-start.29 = (f32[192,2048]{1,0:T(8,128)}, f32[192,2048]{1,0:T(8,128)}, u32[]{:S(2)}, u32[]{:S(2)}) collective-permute-start(f32[192,2048]{1,0:T(8,128)} %get-tuple-element.369.refs_0_), channel_id=1, source_target_pairs={{0,1},{1,0},{2,3},{3,2},{4,5},{5,4},{6,7},{7,6},{8,9},{9,8},{10,11... | collective-permute-start | bytes 4718600 | tf_op jit(solution)/shard_map/ppermute | solution.py:645
  391.9 35.1 %collective-permute-start.30 = (f32[128,768]{1,0:T(8,128)}, f32[128,768]{1,0:T(8,128)S(1)}, u32[]{:S(2)}, u32[]{:S(2)}) collective-permute-start(f32[128,768]{1,0:T(8,128)} %get-tuple-element.336), channel_id=1, source_target_pairs={{0,2},{1,3},{2,4},{3,5},{4,6},{5,7},{6,0},{7,1},{8,10},{9,11},{10,... | collective-permute-start | bytes 1179656 | tf_op jit(solution)/shard_map/ppermute | solution.py:645
  392.1 36.0 %collective-permute-start.31 = (f32[128,768]{1,0:T(8,128)}, f32[128,768]{1,0:T(8,128)}, u32[]{:S(2)}, u32[]{:S(2)}) collective-permute-start(f32[128,768]{1,0:T(8,128)} %get-tuple-element.337), channel_id=1, source_target_pairs={{0,4},{1,5},{2,6},{3,7},{4,0},{5,1},{6,2},{7,3},{8,12},{9,13},{10,... | collective-permute-start | bytes 1179656 | tf_op jit(solution)/shard_map/ppermute | solution.py:645
  393.3 34.8 %collective-permute-start.32 = (f32[128,768]{1,0:T(8,128)}, f32[128,768]{1,0:T(8,128)}, u32[]{:S(2)}, u32[]{:S(2)}) collective-permute-start(f32[128,768]{1,0:T(8,128)} %get-tuple-element.338), channel_id=1, source_target_pairs={{0,6},{1,7},{2,0},{3,1},{4,2},{5,3},{6,4},{7,5},{8,14},{9,15},{10,... | collective-permute-start | bytes 1179656 | tf_op jit(solution)/shard_map/ppermute | solution.py:645
  394.0 27.3 %copy-start.10 = (bf16[2048,384]{1,0:T(8,128)(2,1)S(1)}, bf16[2048,384]{1,0:T(8,128)(2,1)}, u32[]{:S(2)}) copy-start(bf16[2048,384]{1,0:T(8,128)(2,1)} %get-tuple-element.345.refs_3_) | copy-start | bytes 4718596
  394.0 27.3 %copy-start.11 = (bf16[2048,384]{1,0:T(8,128)(2,1)S(1)}, bf16[2048,384]{1,0:T(8,128)(2,1)}, u32[]{:S(2)}) copy-start(bf16[2048,384]{1,0:T(8,128)(2,1)} %get-tuple-element.344.refs_2_) | copy-start | bytes 4718596
  429.5 30.0 %collective-permute-start.35 = (f32[128,768]{1,0:T(8,128)S(1)}, f32[128,768]{1,0:T(8,128)}, u32[]{:S(2)}, u32[]{:S(2)}) collective-permute-start(f32[128,768]{1,0:T(8,128)S(1)} %add_add_fusion), channel_id=1, source_target_pairs={{0,6},{1,7},{2,0},{3,1},{4,2},{5,3},{6,4},{7,5},{8,14},{9,15},{10,... | collective-permute-start | bytes 1179656 | tf_op jit(solution)/shard_map/ppermute | solution.py:645
  430.1 29.4 %collective-permute-start.34 = (f32[128,768]{1,0:T(8,128)S(1)}, f32[128,768]{1,0:T(8,128)}, u32[]{:S(2)}, u32[]{:S(2)}) collective-permute-start(f32[128,768]{1,0:T(8,128)S(1)} %add_add_fusion), channel_id=1, source_target_pairs={{0,4},{1,5},{2,6},{3,7},{4,0},{5,1},{6,2},{7,3},{8,12},{9,13},{10,... | collective-permute-start | bytes 1179656 | tf_op jit(solution)/shard_map/ppermute | solution.py:645
  432.3 27.1 %collective-permute-start.33 = (f32[128,768]{1,0:T(8,128)S(1)}, f32[128,768]{1,0:T(8,128)}, u32[]{:S(2)}, u32[]{:S(2)}) collective-permute-start(f32[128,768]{1,0:T(8,128)S(1)} %add_add_fusion), channel_id=1, source_target_pairs={{0,2},{1,3},{2,4},{3,5},{4,6},{5,7},{6,0},{7,1},{8,10},{9,11},{10,... | collective-permute-start | bytes 1179656 | tf_op jit(solution)/shard_map/ppermute | solution.py:645
  462.2 10.0 %collective-permute-start.36 = (f32[192,2048]{1,0:T(8,128)}, f32[192,2048]{1,0:T(8,128)}, u32[]{:S(2)}, u32[]{:S(2)}) collective-permute-start(f32[192,2048]{1,0:T(8,128)} %get-tuple-element.376.refs_0_), channel_id=1, source_target_pairs={{0,1},{1,0},{2,3},{3,2},{4,5},{5,4},{6,7},{7,6},{8,9},{9,8},{10,11... | collective-permute-start | bytes 4718600 | tf_op jit(solution)/shard_map/ppermute | solution.py:645
  480.6 32.7 %copy-start.33 = (f32[192,1024]{1,0:T(8,128)S(1)}, f32[192,1024]{1,0:T(8,128)}, u32[]{:S(2)}) copy-start(f32[192,1024]{1,0:T(8,128)} %copy-done.32) | copy-start | bytes 2359300
  480.6 32.7 %copy-start.35 = (f32[192,1024]{1,0:T(8,128)S(1)}, f32[192,1024]{1,0:T(8,128)}, u32[]{:S(2)}) copy-start(f32[192,1024]{1,0:T(8,128)} %copy-done.34) | copy-start | bytes 2359300
  480.7 32.6 %copy-start.37 = (f32[192,1024]{1,0:T(8,128)S(1)}, f32[192,1024]{1,0:T(8,128)}, u32[]{:S(2)}) copy-start(f32[192,1024]{1,0:T(8,128)} %copy-done.36) | copy-start | bytes 2359300
  481.1 16.1 %collective-permute-start.37 = (f32[104,576]{0,1:T(8,128)S(1)}, f32[104,576]{0,1:T(8,128)S(1)}, u32[]{:S(2)}, u32[]{:S(2)}) collective-permute-start(f32[104,576]{0,1:T(8,128)S(1)} %get-tuple-element.389), channel_id=1, source_target_pairs={{0,8},{1,9},{2,10},{3,11},{4,12},{5,13},{6,14},{7,15},{8,16},{9,17... | collective-permute-start | bytes 718856 | tf_op jit(solution)/shard_map/ppermute | solution.py:645
  482.0 21.6 %collective-permute-start.38 = (f32[104,576]{0,1:T(8,128)S(1)}, f32[104,576]{0,1:T(8,128)S(1)}, u32[]{:S(2)}, u32[]{:S(2)}) collective-permute-start(f32[104,576]{0,1:T(8,128)S(1)} %get-tuple-element.390), channel_id=1, source_target_pairs={{0,16},{1,17},{2,18},{3,19},{4,20},{5,21},{6,22},{7,23},{8,24},{9,... | collective-permute-start | bytes 718856 | tf_op jit(solution)/shard_map/ppermute | solution.py:645
  482.5 27.2 %collective-permute-start.39 = (f32[104,576]{0,1:T(8,128)S(1)}, f32[104,576]{0,1:T(8,128)S(1)}, u32[]{:S(2)}, u32[]{:S(2)}) collective-permute-start(f32[104,576]{0,1:T(8,128)S(1)} %get-tuple-element.391), channel_id=1, source_target_pairs={{0,24},{1,25},{2,26},{3,27},{4,28},{5,29},{6,30},{7,31},{8,0},{9,1... | collective-permute-start | bytes 718856 | tf_op jit(solution)/shard_map/ppermute | solution.py:645
  509.8 9.6 %collective-permute-start.42 = (f32[104,576]{0,1:T(8,128)S(1)}, f32[104,576]{0,1:T(8,128)S(1)}, u32[]{:S(2)}, u32[]{:S(2)}) collective-permute-start(f32[104,576]{0,1:T(8,128)S(1)} %add_add_fusion.1), channel_id=1, source_target_pairs={{0,6},{1,7},{2,0},{3,1},{4,2},{5,3},{6,4},{7,5},{8,14},{9,15},{10,... | collective-permute-start | bytes 718856 | tf_op jit(solution)/shard_map/ppermute | solution.py:645
  511.1 22.1 %collective-permute-start.41 = (f32[104,576]{0,1:T(8,128)S(1)}, f32[104,576]{0,1:T(8,128)S(1)}, u32[]{:S(2)}, u32[]{:S(2)}) collective-permute-start(f32[104,576]{0,1:T(8,128)S(1)} %add_add_fusion.1), channel_id=1, source_target_pairs={{0,4},{1,5},{2,6},{3,7},{4,0},{5,1},{6,2},{7,3},{8,12},{9,13},{10,... | collective-permute-start | bytes 718856 | tf_op jit(solution)/shard_map/ppermute | solution.py:645
  511.4 21.9 %collective-permute-start.40 = (f32[104,576]{0,1:T(8,128)S(1)}, f32[104,576]{0,1:T(8,128)S(1)}, u32[]{:S(2)}, u32[]{:S(2)}) collective-permute-start(f32[104,576]{0,1:T(8,128)S(1)} %add_add_fusion.1), channel_id=1, source_target_pairs={{0,2},{1,3},{2,4},{3,5},{4,6},{5,7},{6,0},{7,1},{8,10},{9,11},{10,... | collective-permute-start | bytes 718856 | tf_op jit(solution)/shard_map/ppermute | solution.py:645
  537.4 20.2 %collective-permute-start.43 = (f32[576,256]{1,0:T(8,128)S(1)}, f32[576,256]{1,0:T(8,128)}, u32[]{:S(2)}, u32[]{:S(2)}) collective-permute-start(f32[576,256]{1,0:T(8,128)S(1)} %get-tuple-element.402), channel_id=1, source_target_pairs={{0,2},{1,3},{2,4},{3,5},{4,6},{5,7},{6,0},{7,1},{8,10},{9,11},{10,... | collective-permute-start | bytes 1769480 | tf_op jit(solution)/shard_map/ppermute | solution.py:645
  543.2 64.0 %collective-permute-start.48 = (f32[3,104,768]{2,1,0:T(8,128)S(1)}, f32[3,104,768]{2,1,0:T(8,128)S(1)}, u32[]{:S(2)}, u32[]{:S(2)}) collective-permute-start(f32[3,104,768]{2,1,0:T(8,128)S(1)} %pad_maximum_fusion.22), channel_id=1, source_target_pairs={{0,24},{1,25},{2,26},{3,27},{4,28},{5,29},{6,30},{7,31},{8,0},{9,1... | collective-permute-start | bytes 2875400 | tf_op jit(solution)/shard_map/ppermute | solution.py:645
  544.3 63.0 %collective-permute-start.47 = (f32[3,104,768]{2,1,0:T(8,128)S(1)}, f32[3,104,768]{2,1,0:T(8,128)S(1)}, u32[]{:S(2)}, u32[]{:S(2)}) collective-permute-start(f32[3,104,768]{2,1,0:T(8,128)S(1)} %pad_maximum_fusion.22), channel_id=1, source_target_pairs={{0,16},{1,17},{2,18},{3,19},{4,20},{5,21},{6,22},{7,23},{8,24},{9,... | collective-permute-start | bytes 2875400 | tf_op jit(solution)/shard_map/ppermute | solution.py:645
  545.5 61.8 %collective-permute-start.46 = (f32[3,104,768]{2,1,0:T(8,128)S(1)}, f32[3,104,768]{2,1,0:T(8,128)}, u32[]{:S(2)}, u32[]{:S(2)}) collective-permute-start(f32[3,104,768]{2,1,0:T(8,128)S(1)} %pad_maximum_fusion.22), channel_id=1, source_target_pairs={{0,8},{1,9},{2,10},{3,11},{4,12},{5,13},{6,14},{7,15},{8,16},{9,17... | collective-permute-start | bytes 2875400 | tf_op jit(solution)/shard_map/ppermute | solution.py:645
  545.5 61.8 %collective-permute-start.44 = (f32[576,256]{1,0:T(8,128)}, f32[576,256]{1,0:T(8,128)}, u32[]{:S(2)}, u32[]{:S(2)}) collective-permute-start(f32[576,256]{1,0:T(8,128)} %get-tuple-element.403), channel_id=1, source_target_pairs={{0,4},{1,5},{2,6},{3,7},{4,0},{5,1},{6,2},{7,3},{8,12},{9,13},{10,... | collective-permute-start | bytes 1769480 | tf_op jit(solution)/shard_map/ppermute | solution.py:645
  557.6 49.6 %collective-permute-start.45 = (f32[576,256]{1,0:T(8,128)}, f32[576,256]{1,0:T(8,128)}, u32[]{:S(2)}, u32[]{:S(2)}) collective-permute-start(f32[576,256]{1,0:T(8,128)} %get-tuple-element.404), channel_id=1, source_target_pairs={{0,6},{1,7},{2,0},{3,1},{4,2},{5,3},{6,4},{7,5},{8,14},{9,15},{10,... | collective-permute-start | bytes 1769480 | tf_op jit(solution)/shard_map/ppermute | solution.py:645
  611.2 15.1 %collective-permute-start.49 = (f32[3,416,768]{2,1,0:T(8,128)}, f32[3,416,768]{2,1,0:T(8,128)}, u32[]{:S(2)}, u32[]{:S(2)}) collective-permute-start(f32[3,416,768]{2,1,0:T(8,128)} %pad_maximum_fusion.2.refs_0_), channel_id=1, source_target_pairs={{0,1},{1,0},{2,3},{3,2},{4,5},{5,4},{6,7},{7,6},{8,9},{9,8},{10,11... | collective-permute-start | bytes 11501576 | tf_op jit(solution)/shard_map/ppermute | solution.py:645
  (78 other events, 316.4 us)
Sparse Core Ops, SparseCore 0:
  255.4 57.5 reduce-scatter.6
  316.5 70.2 reduce-scatter.8
  391.2 59.2 all-gather.2
  462.4 97.6 all-gather.4
